TPU v7x, 32 devices: a whole 2x2x4 slice. The times are simulated.
32 devices in a mesh: gx: 8 (over y, x, core), gy: 4 (over z).
Axes of the slice: x: 2, y: 2, z: 4, core: 2. Of those that a mesh axis runs over, the one named last changes fastest.
Arguments:
- incident: float32 [18, 10, 256, 512], P(None, None, 'gx', 'gy'), may hold values from -6 to 6
- cotangent: float32 [18, 10, 256, 512], P(None, None, 'gx', 'gy'), may hold values from -6 to 6
- scatter_table: float32 [4, 18, 18], replicated, may hold values from -1.5 to 1.5
- deriv_table: float32 [4, 18, 18], replicated, may hold values from -1.5 to 1.5
- material_code: int32 [10, 256, 64], P(None, 'gx', 'gy'), may hold values from 0 to 3
- boundary_code: int32 [2, 256, 64], P(None, 'gx', 'gy'), may hold values from 0 to 2
- param_ids: int32 [256, 512], P('gx', 'gy'), may hold values from 0 to 131071, as said below
Outputs:
- adjoint_field: float32 [18, 10, 256, 512], P(None, None, 'gx', 'gy')
- sensitivity: float32 [131072], P(('gx', 'gy'))
Inputs may be any that keep to these rules, and one draw needn't show every extreme that they name: `param_ids`: parameter i belongs to device i // 4096 of gx+gy, gy fastest. The columns of one device name parameters of any one owner at most 256 times, and on every device some owner is named exactly 256 times.
All inputs are finite; a program needn't handle non-finite values.
Results may differ from a plain program's by a relative error of at most 0.0001.
Values sent between devices are 32-bit elements; how exact they have to be, the bound alone decides.
No kernel may reach another device: no remote copies, remote signals or barrier semaphores. Data moves between devices by JAX's collectives and lax.ppermute only.
A program may use at most 128 MiB of HBM per device.

v0:
```python
import jax
import jax.numpy as jnp
from jax import lax
from jax.sharding import PartitionSpec as P

BW = 8
ITERS = 4


sens_scale = 1.0 / 32.0


def from_behind(value, axis, steps):
    count = lax.axis_size(axis)
    pairs = [(source, (source + steps) % count) for source in range(count)]
    return lax.ppermute(value, axis, pairs)


def passed_along(block, axis, distance):
    devices = range(lax.axis_size(axis))
    route = [(i - distance, i) for i in devices if i - distance in devices]
    return lax.ppermute(block, axis, route)


def end_coefficient(codes):
    return jnp.where(codes == 0, -1.0, jnp.where(codes == 1, 1.0, 0.0)).astype(jnp.float32)


def connect(reflected, lower_coef, upper_coef):
    east = reflected[:, 0:2]
    west = reflected[:, 2:4]
    north = reflected[:, 4:6]
    south = reflected[:, 6:8]
    upper = reflected[:, 8:10]
    lower = reflected[:, 10:12]
    from_west = from_behind(east[:, :, :, -1:, :], "gx", 1)
    from_east = from_behind(west[:, :, :, :1, :], "gx", -1)
    from_south = passed_along(north[..., -1:], "gy", 1)
    from_north = passed_along(south[..., :1], "gy", -1)
    position = lax.axis_index("gy")
    extent = lax.axis_size("gy")
    first_south = jnp.where(position == 0, -south[..., :1], from_south)
    last_north = jnp.where(position == extent - 1, -north[..., -1:], from_north)
    new_west = jnp.concatenate([from_west, east[:, :, :, :-1]], axis=3)
    new_east = jnp.concatenate([west[:, :, :, 1:], from_east], axis=3)
    new_south = jnp.concatenate([first_south, north[..., :-1]], axis=4)
    new_north = jnp.concatenate([south[..., 1:], last_north], axis=4)
    new_lower = jnp.concatenate([lower_coef * lower[:, :, :1], upper[:, :, :-1]], axis=2)
    new_upper = jnp.concatenate([lower[:, :, 1:], upper_coef * upper[:, :, -1:]], axis=2)
    return jnp.concatenate(
        [new_east, new_west, new_north, new_south, new_upper, new_lower, reflected[:, 12:]], axis=1
    )


def apply_table(table, selector, field, transpose):
    form = "mqp,qzxy->mpzxy" if transpose else "mpq,qzxy->mpzxy"
    product = jnp.einsum(form, table, field, precision=lax.Precision.HIGHEST)
    return jnp.sum(jnp.where(selector, product, 0.0), axis=0)


def shards(
    incident, cotangent, scatter_table, deriv_table, material_code, boundary_code, param_ids
):
    width_rows, width_cols = param_ids.shape
    cells = jnp.repeat(material_code, BW, axis=2)
    materials = jnp.arange(scatter_table.shape[0], dtype=jnp.int32)
    selector = cells[None, None] == materials[:, None, None, None, None]
    lower_coef = end_coefficient(jnp.repeat(boundary_code[0], BW, axis=1))[None, None, None]
    upper_coef = end_coefficient(jnp.repeat(boundary_code[1], BW, axis=1))[None, None, None]
    column = jnp.zeros((width_rows, width_cols), jnp.float32)
    field = incident
    saved = []
    for step in range(ITERS):
        saved.append(field)
        field = connect(
            apply_table(scatter_table, selector, field, False)[None], lower_coef, upper_coef
        )[0]
    adjoint = cotangent
    for step in reversed(range(ITERS)):
        reflected = connect(adjoint[None], lower_coef, upper_coef)[0]
        change = apply_table(deriv_table, selector, saved[step], False)
        column = column + jnp.sum(reflected * change, axis=(0, 1))
        adjoint = apply_table(scatter_table, selector, reflected, True)
    values = (column * sens_scale).reshape(-1)
    identities = param_ids.reshape(-1)
    owned = width_rows * width_cols
    owners_count = lax.axis_size("gx") * lax.axis_size("gy")
    everything = jnp.zeros((owned * owners_count,), jnp.float32).at[identities].add(values)
    sensitivity = lax.psum_scatter(everything, ("gx", "gy"), scatter_dimension=0, tiled=True)
    return (adjoint, sensitivity)


def solution(mesh):
    in_specs = (
        P(None, None, "gx", "gy"),
        P(None, None, "gx", "gy"),
        P(),
        P(),
        P(None, "gx", "gy"),
        P(None, "gx", "gy"),
        P("gx", "gy"),
    )
    out_specs = (P(None, None, "gx", "gy"), P(("gx", "gy")))
    return jax.shard_map(shards, mesh=mesh, in_specs=in_specs, out_specs=out_specs, check_vma=False)
```

profile of v0, /device:TPU:0, one launch (start us, length us, event | category | flops | bytes accessed | tf_op | source)
XLA Modules:
  0.0 625.3 jit_solution(15333547207029511107)
XLA Ops:
  7.2 1.9 broadcast_bitcast_fusion
  9.2 1.3 copy.49
  10.7 20.3 %select_reduce_fusion.1 = f32[18,10,32,128]{3,0,2,1:T(8,128)S(1)} fusion(pred[4,10,32,128]{3,0,2,1:T(4,128)(4,1)S(1)} %iota_compare_fusion, f32[18,10,32,128,1]{3,2,1,0,4:T(8,128)S(1)} %bitcast.134, f32[4,18,18,1,1]{2,0,1,4,3:T(4,128)} %bitcast.198), kind=kOutput, calls=%fused_computation.20 | convolution fusion | flops 642170880 | bytes 6067264 | tf_op jit(solution)/shard_map/mpq,qzxy->mpzxy/dot_general | solution.py:57
  31.0 1.7 fusion.48
  32.7 1.3 collective-permute-start.18
  34.0 6.3 %collective-permute-start.19 = (f32[1,2,10,32,1]{4,1,3,2,0:T(2,128)}, f32[1,2,10,32,1]{4,1,3,2,0:T(2,128)}, u32[]{:S(2)}, u32[]{:S(2)}) collective-permute-start(f32[1,2,10,32,1]{4,1,3,2,0:T(2,128)} %get-tuple-element.38), channel_id=1, source_target_pairs={{0,1},{1,2},{2,3},{4,5},{5,6},{6,7},{8,9},{9,10},{10,11},{12,13},{... | collective-permute-start | bytes 7688 | tf_op jit(solution)/shard_map/ppermute | solution.py:22
  40.3 1.8 collective-permute-start.16
  42.1 1.9 copy.144
  44.0 1.7 fusion.68
  45.7 1.7 collective-permute-start.2
  47.4 1.4 fusion.49
  51.9 1.3 fusion.69
  54.5 22.1 %select_reduce_fusion = f32[18,10,32,128]{3,0,2,1:T(8,128)} fusion(pred[4,10,32,128]{3,0,2,1:T(4,128)(4,1)} %copy-done.42, f32[18,10,32,128,1]{3,2,1,0,4:T(8,128)S(1)} %bitcast.135, f32[4,18,18,1,1]{2,0,1,4,3:T(4,128)} %bitcast.194), kind=kOutput, calls=%fused_computation.19 | convolution fusion | flops 642170880 | bytes 6067264 | tf_op jit(solution)/shard_map/mpq,qzxy->mpzxy/dot_general | solution.py:57
  78.6 1.9 slice.576
  80.5 1.9 slice.524
  82.4 4.7 collective-permute-start.3
  87.2 2.6 negate_select_fusion.4
  89.8 2.7 pad_maximum_fusion.26
  92.6 2.8 collective-permute-start
  95.3 2.5 negate_select_fusion.12
  97.9 1.6 pad_maximum_fusion.2
  101.2 18.7 %concatenate.181 = f32[1,18,10,32,128]{4,1,3,2,0:T(8,128)} concatenate(f32[1,2,10,32,128]{4,1,3,2,0:T(2,128)} %pad_maximum_fusion.24, f32[1,2,10,32,128]{4,1,3,2,0:T(2,128)} %pad_maximum_fusion.25, f32[1,2,10,32,128]{4,1,3,2,0:T(2,128)} %get-tuple-element.112, f32[1,2,10,32,128]{4,1,3,2,0:T(2,128)} %get-tuple-element.113, f32[1,2,10,32,128]{4,1,3,2,0:T(2,128)S(1)} %pad_maximum_fusion.28, ...), dimensions={1} | concatenate | bytes 5898240 | tf_op jit(solution)/shard_map/concatenate | solution.py:50
  119.9 15.5 %fusion.4 = f32[18,10,32,128]{3,0,2,1:T(8,128)S(1)} fusion(pred[4,10,32,128]{3,0,2,1:T(4,128)(4,1)S(1)} %copy-done.43, f32[1,18,10,32,128]{4,1,3,2,0:T(8,128)} %concatenate.181, f32[4,18,18,1,1]{2,0,1,4,3:T(4,128)} %bitcast.199), kind=kOutput, calls=%fused_computation.10 | convolution fusion | flops 642170880 | bytes 6067264 | tf_op jit(solution)/shard_map/mpq,qzxy->mpzxy/dot_general | solution.py:57
  137.5 17.9 %fusion = f32[18,10,32,128]{3,0,2,1:T(8,128)} fusion(pred[4,10,32,128]{3,0,2,1:T(4,128)(4,1)S(1)} %copy-done.43, f32[1,18,10,32,128]{4,1,3,2,0:T(8,128)S(1)} %copy-done.11, f32[4,18,18,1,1]{2,0,1,4,3:T(4,128)S(1)} %bitcast.196), kind=kOutput, calls=%fused_computation.2 | convolution fusion | flops 642170880 | bytes 6067264 | tf_op jit(solution)/shard_map/mpq,qzxy->mpzxy/dot_general | solution.py:57
  155.4 1.3 collective-permute-start.22
  156.6 4.6 collective-permute-start.23
  163.1 2.6 collective-permute-start.20
  171.9 20.3 %concatenate.188 = f32[1,18,10,32,128]{4,1,3,2,0:T(8,128)} concatenate(f32[1,2,10,32,128]{4,1,3,2,0:T(2,128)} %pad_maximum_fusion.30, f32[1,2,10,32,128]{4,1,3,2,0:T(2,128)} %pad_maximum_fusion.31, f32[1,2,10,32,128]{4,1,3,2,0:T(2,128)} %pad_maximum_fusion.32, f32[1,2,10,32,128]{4,1,3,2,0:T(2,128)} %pad_maximum_fusion.33, f32[1,2,10,32,128]{4,1,3,2,0:T(2,128)} %pad_maximum_fusion.34, ...), dimensions={1} | concatenate | bytes 5898240 | tf_op jit(solution)/shard_map/concatenate | solution.py:50
  192.2 15.4 %fusion.3 = f32[18,10,32,128]{3,0,2,1:T(8,128)S(1)} fusion(pred[4,10,32,128]{3,0,2,1:T(4,128)(4,1)S(1)} %copy-done.43, f32[1,18,10,32,128]{4,1,3,2,0:T(8,128)} %concatenate.188, f32[4,18,18,1,1]{2,0,1,4,3:T(4,128)S(1)} %bitcast.201), kind=kOutput, calls=%fused_computation.8 | convolution fusion | flops 642170880 | bytes 6067264 | tf_op jit(solution)/shard_map/mpq,qzxy->mpzxy/dot_general | solution.py:57
  207.7 1.7 fusion.38
  209.4 1.3 fusion.39
  216.5 19.8 %concatenate.153 = f32[1,18,10,32,128]{4,1,3,2,0:T(8,128)} concatenate(f32[1,2,10,32,128]{4,1,3,2,0:T(2,128)S(1)} %pad_maximum_fusion, f32[1,2,10,32,128]{4,1,3,2,0:T(2,128)S(1)} %pad_maximum_fusion.1, f32[1,2,10,32,128]{4,1,3,2,0:T(2,128)} %get-tuple-element.108, f32[1,2,10,32,128]{4,1,3,2,0:T(2,128)} %get-tuple-element.109, f32[1,2,10,32,128]{4,1,3,2,0:T(2,128)} %pad_maximum_fusion.4, ...), dimensions={1} | concatenate | bytes 5898240 | tf_op jit(solution)/shard_map/concatenate | solution.py:50
  236.3 15.7 %fusion.8 = f32[18,10,32,128]{3,0,2,1:T(8,128)S(1)} fusion(pred[4,10,32,128]{3,0,2,1:T(4,128)(4,1)S(1)} %copy-done.43, f32[1,18,10,32,128]{4,1,3,2,0:T(8,128)} %concatenate.153, f32[4,18,18,1,1]{2,0,1,4,3:T(4,128)} %bitcast.200), kind=kOutput, calls=%fused_computation.18 | convolution fusion | flops 642170880 | bytes 6067264 | tf_op jit(solution)/shard_map/mqp,qzxy->mpzxy/dot_general | solution.py:57
  254.1 17.8 %fusion.1 = f32[18,10,32,128]{3,0,2,1:T(8,128)} fusion(pred[4,10,32,128]{3,0,2,1:T(4,128)(4,1)S(1)} %copy-done.43, f32[1,18,10,32,128]{4,1,3,2,0:T(8,128)S(1)} %copy-done.10, f32[4,18,18,1,1]{2,0,1,4,3:T(4,128)S(1)} %bitcast.197), kind=kOutput, calls=%fused_computation.4 | convolution fusion | flops 642170880 | bytes 6067264 | tf_op jit(solution)/shard_map/mpq,qzxy->mpzxy/dot_general | solution.py:57
  271.9 1.4 collective-permute-start.26
  273.4 5.0 collective-permute-start.27
  278.4 1.9 collective-permute-start.24
  280.3 1.3 collective-permute-start.6
  283.9 4.6 collective-permute-start.7
  288.8 2.5 negate_select_fusion
  293.7 2.3 collective-permute-start.4
  300.8 20.3 %concatenate.160 = f32[1,18,10,32,128]{4,1,3,2,0:T(8,128)} concatenate(f32[1,2,10,32,128]{4,1,3,2,0:T(2,128)} %pad_maximum_fusion.6, f32[1,2,10,32,128]{4,1,3,2,0:T(2,128)} %pad_maximum_fusion.7, f32[1,2,10,32,128]{4,1,3,2,0:T(2,128)} %pad_maximum_fusion.8, f32[1,2,10,32,128]{4,1,3,2,0:T(2,128)} %pad_maximum_fusion.9, f32[1,2,10,32,128]{4,1,3,2,0:T(2,128)} %pad_maximum_fusion.10, ...), dimensions={1} | concatenate | bytes 5898240 | tf_op jit(solution)/shard_map/concatenate | solution.py:50
  321.1 15.5 %fusion.7 = f32[18,10,32,128]{3,0,2,1:T(8,128)S(1)} fusion(pred[4,10,32,128]{3,0,2,1:T(4,128)(4,1)S(1)} %copy-done.43, f32[1,18,10,32,128]{4,1,3,2,0:T(8,128)} %concatenate.160, f32[4,18,18,1,1]{2,0,1,4,3:T(4,128)S(1)} %bitcast.202), kind=kOutput, calls=%fused_computation.16 | convolution fusion | flops 642170880 | bytes 6067264 | tf_op jit(solution)/shard_map/mqp,qzxy->mpzxy/dot_general | solution.py:57
  337.8 1.4 fusion.58
  339.1 1.3 fusion.59
  343.9 17.2 %concatenate.195 = f32[1,18,10,32,128]{4,1,3,2,0:T(8,128)} concatenate(f32[1,2,10,32,128]{4,1,3,2,0:T(2,128)S(1)} %pad_maximum_fusion.36, f32[1,2,10,32,128]{4,1,3,2,0:T(2,128)S(1)} %pad_maximum_fusion.37, f32[1,2,10,32,128]{4,1,3,2,0:T(2,128)S(1)} %copy-done.16, f32[1,2,10,32,128]{4,1,3,2,0:T(2,128)S(1)} %copy-done.15, f32[1,2,10,32,128]{4,1,3,2,0:T(2,128)S(1)} %pad_maximum_fusion.40, ...), dimensions={1} | concatenate | bytes 5898240 | tf_op jit(solution)/shard_map/concatenate | solution.py:50
  361.2 15.8 %fusion.2 = f32[18,10,32,128]{3,0,2,1:T(8,128)S(1)} fusion(pred[4,10,32,128]{3,0,2,1:T(4,128)(4,1)S(1)} %copy-done.43, f32[1,18,10,32,128]{4,1,3,2,0:T(8,128)} %concatenate.195, f32[4,18,18,1,1]{2,0,1,4,3:T(4,128)} %bitcast.195), kind=kOutput, calls=%fused_computation.6 | convolution fusion | flops 642170880 | bytes 6067264 | tf_op jit(solution)/shard_map/mpq,qzxy->mpzxy/dot_general | solution.py:57
  377.5 1.6 collective-permute-start.10
  379.0 5.2 collective-permute-start.11
  384.3 2.7 collective-permute-start.8
  388.6 1.4 collective-permute-done.10
  393.0 17.3 %concatenate.167 = f32[1,18,10,32,128]{4,1,3,2,0:T(8,128)} concatenate(f32[1,2,10,32,128]{4,1,3,2,0:T(2,128)S(1)} %pad_maximum_fusion.12, f32[1,2,10,32,128]{4,1,3,2,0:T(2,128)S(1)} %pad_maximum_fusion.13, f32[1,2,10,32,128]{4,1,3,2,0:T(2,128)S(1)} %pad_maximum_fusion.14, f32[1,2,10,32,128]{4,1,3,2,0:T(2,128)S(1)} %pad_maximum_fusion.15, ...), dimensions={1} | concatenate | bytes 5898240 | tf_op jit(solution)/shard_map/concatenate | solution.py:50
  410.3 15.6 %fusion.6 = f32[18,10,32,128]{3,0,2,1:T(8,128)S(1)} fusion(pred[4,10,32,128]{3,0,2,1:T(4,128)(4,1)S(1)} %copy-done.43, f32[1,18,10,32,128]{4,1,3,2,0:T(8,128)} %concatenate.167, f32[4,18,18,1,1]{2,0,1,4,3:T(4,128)S(1)} %bitcast.203), kind=kOutput, calls=%fused_computation.14 | convolution fusion | flops 642170880 | bytes 6067264 | tf_op jit(solution)/shard_map/mqp,qzxy->mpzxy/dot_general | solution.py:57
  428.5 1.3 collective-permute-start.14
  429.8 5.0 collective-permute-start.15
  434.9 2.6 collective-permute-start.12
  438.0 1.7 collective-permute-done.14
  442.7 17.4 %concatenate.174 = f32[1,18,10,32,128]{4,1,3,2,0:T(8,128)} concatenate(f32[1,2,10,32,128]{4,1,3,2,0:T(2,128)S(1)} %pad_maximum_fusion.18, f32[1,2,10,32,128]{4,1,3,2,0:T(2,128)S(1)} %pad_maximum_fusion.19, f32[1,2,10,32,128]{4,1,3,2,0:T(2,128)S(1)} %pad_maximum_fusion.20, f32[1,2,10,32,128]{4,1,3,2,0:T(2,128)S(1)} %pad_maximum_fusion.21, ...), dimensions={1} | concatenate | bytes 5898240 | tf_op jit(solution)/shard_map/concatenate | solution.py:50
  460.1 3.8 fusion.20
  463.8 22.8 %scatter_custom_fusion = f32[131072]{0:T(1024)} fusion(s32[4096]{0:T(1024)} %bitcast.193, f32[4096]{0:T(1024)S(1)} %multiply_bitcast_fusion, f32[]{:T(128)} %constant.3.clone.1), kind=kCustom, calls=%fused_computation.99 | custom fusion | flops 4096 | bytes 524800 | tf_op jit(solution)/shard_map/scatter-add | solution.py:88
  486.7 15.6 %fusion.5 = f32[18,10,32,128]{3,0,2,1:T(8,128)S(1)} fusion(pred[4,10,32,128]{3,0,2,1:T(4,128)(4,1)S(1)} %copy-done.43, f32[1,18,10,32,128]{4,1,3,2,0:T(8,128)} %concatenate.174, f32[4,18,18,1,1]{2,0,1,4,3:T(4,128)S(1)} %bitcast.204), kind=kOutput, calls=%fused_computation.12 | convolution fusion | flops 642170880 | bytes 6067264 | tf_op jit(solution)/shard_map/mqp,qzxy->mpzxy/dot_general | solution.py:57
  502.4 2.1 copy.68
  504.5 112.2 %all-reduce.3.cloned.1.call-done = f32[131072]{0:T(1024)} async-done(((f32[131072]{0:T(1024)}), f32[131072]{0:T(1024)}) %all-reduce.3.cloned.1.call-update) | async-done | bytes 524304
  616.7 1.3 dynamic-slice
  (236 shorter events, 51.5 us)
Async XLA Ops:
  7.2 609.5 %all-reduce.3.cloned.1.call-start = ((), (), s32[]{:S(2)}) async-start(), calls=%async_computation | async-start | bytes 1048576
  10.7 20.3 %copy-start.42 = (pred[4,10,32,128]{3,0,2,1:T(4,128)(4,1)}, pred[4,10,32,128]{3,0,2,1:T(4,128)(4,1)S(1)}, u32[]{:S(2)}) copy-start(pred[4,10,32,128]{3,0,2,1:T(4,128)(4,1)S(1)} %iota_compare_fusion) | copy-start | bytes 491524
  10.7 31.4 %copy-start.14 = (f32[18,10,32,128]{3,2,1,0:T(8,128)S(1)}, f32[18,10,32,128]{3,2,1,0:T(8,128)}, u32[]{:S(2)}) copy-start(f32[18,10,32,128]{3,2,1,0:T(8,128)} %param.8) | copy-start | bytes 8847364
  31.0 18.8 %copy-start.6 = (f32[18,10,32,128]{3,0,2,1:T(8,128)}, f32[18,10,32,128]{3,0,2,1:T(8,128)S(1)}, u32[]{:S(2)}) copy-start(f32[18,10,32,128]{3,0,2,1:T(8,128)S(1)} %select_reduce_fusion.1) | copy-start | bytes 8847364
  32.7 49.7 %collective-permute-start.18 = (f32[1,2,10,32,1]{4,1,3,2,0:T(2,128)}, f32[1,2,10,32,1]{4,1,3,2,0:T(2,128)}, u32[]{:S(2)}, u32[]{:S(2)}) collective-permute-start(f32[1,2,10,32,1]{4,1,3,2,0:T(2,128)} %get-tuple-element.39), channel_id=1, source_target_pairs={{1,0},{2,1},{3,2},{5,4},{6,5},{7,6},{9,8},{10,9},{11,10},{13,12},{... | collective-permute-start | bytes 7688 | tf_op jit(solution)/shard_map/ppermute | solution.py:22
  34.0 53.2 %collective-permute-start.19 = (f32[1,2,10,32,1]{4,1,3,2,0:T(2,128)}, f32[1,2,10,32,1]{4,1,3,2,0:T(2,128)}, u32[]{:S(2)}, u32[]{:S(2)}) collective-permute-start(f32[1,2,10,32,1]{4,1,3,2,0:T(2,128)} %get-tuple-element.38), channel_id=1, source_target_pairs={{0,1},{1,2},{2,3},{4,5},{5,6},{6,7},{8,9},{9,10},{10,11},{12,13},{... | collective-permute-start | bytes 7688 | tf_op jit(solution)/shard_map/ppermute | solution.py:22
  40.3 59.2 %collective-permute-start.16 = (f32[1,2,10,1,128]{4,1,3,2,0:T(2,128)S(1)}, f32[1,2,10,1,128]{4,1,3,2,0:T(2,128)S(1)}, u32[]{:S(2)}, u32[]{:S(2)}) collective-permute-start(f32[1,2,10,1,128]{4,1,3,2,0:T(2,128)S(1)} %get-tuple-element.43), channel_id=1, source_target_pairs={{0,28},{4,0},{8,4},{12,8},{16,12},{20,16},{24,20},{28,24},{1,29},{... | collective-permute-start | bytes 30728 | tf_op jit(solution)/shard_map/ppermute | solution.py:16
  42.1 58.3 %collective-permute-start.17 = (f32[1,2,10,1,128]{4,1,3,2,0:T(2,128)S(1)}, f32[1,2,10,1,128]{4,1,3,2,0:T(2,128)S(1)}, u32[]{:S(2)}, u32[]{:S(2)}) collective-permute-start(f32[1,2,10,1,128]{4,1,3,2,0:T(2,128)S(1)} %get-tuple-element.42), channel_id=1, source_target_pairs={{0,4},{4,8},{8,12},{12,16},{16,20},{20,24},{24,28},{28,0},{1,5},{5... | collective-permute-start | bytes 30728 | tf_op jit(solution)/shard_map/ppermute | solution.py:16
  44.0 10.3 %copy-start.2 = (f32[18,10,32,128]{3,0,2,1:T(8,128)}, f32[18,10,32,128]{3,0,2,1:T(8,128)S(1)}, u32[]{:S(2)}) copy-start(f32[18,10,32,128]{3,0,2,1:T(8,128)S(1)} %copy.144) | copy-start | bytes 8847364
  45.7 46.9 %collective-permute-start.2 = (f32[1,2,10,32,1]{4,1,3,2,0:T(2,128)}, f32[1,2,10,32,1]{4,1,3,2,0:T(2,128)}, u32[]{:S(2)}, u32[]{:S(2)}) collective-permute-start(f32[1,2,10,32,1]{4,1,3,2,0:T(2,128)} %get-tuple-element.95), channel_id=1, source_target_pairs={{1,0},{2,1},{3,2},{5,4},{6,5},{7,6},{9,8},{10,9},{11,10},{13,12},{... | collective-permute-start | bytes 7688 | tf_op jit(solution)/shard_map/ppermute | solution.py:22
  54.5 22.1 %copy-start.46 = (s32[32,128]{1,0:T(8,128)S(1)}, s32[32,128]{1,0:T(8,128)}, u32[]{:S(2)}) copy-start(s32[32,128]{1,0:T(8,128)} %param.13) | copy-start | bytes 49156
  54.5 23.9 %copy-start.37 = (f32[1,2,9,32,128]{4,1,3,2,0:T(2,128)S(1)}, f32[1,2,9,32,128]{4,1,3,2,0:T(2,128)}, u32[]{:S(2)}) copy-start(f32[1,2,9,32,128]{4,1,3,2,0:T(2,128)} %get-tuple-element.34) | copy-start | bytes 884740
  82.4 15.5 %copy-start.21 = (f32[1,2,10,32,127]{4,1,3,2,0:T(2,128)S(1)}, f32[1,2,10,32,127]{4,1,3,2,0:T(2,128)}, u32[]{:S(2)}) copy-start(f32[1,2,10,32,127]{4,1,3,2,0:T(2,128)} %get-tuple-element.96) | copy-start | bytes 975364
  82.4 15.5 %copy-start.22 = (f32[1,2,10,32,127]{4,1,3,2,0:T(2,128)S(1)}, f32[1,2,10,32,127]{4,1,3,2,0:T(2,128)}, u32[]{:S(2)}) copy-start(f32[1,2,10,32,127]{4,1,3,2,0:T(2,128)} %get-tuple-element.97) | copy-start | bytes 975364
  82.4 12.9 %collective-permute-start.3 = (f32[1,2,10,32,1]{4,1,3,2,0:T(2,128)}, f32[1,2,10,32,1]{4,1,3,2,0:T(2,128)S(1)}, u32[]{:S(2)}, u32[]{:S(2)}) collective-permute-start(f32[1,2,10,32,1]{4,1,3,2,0:T(2,128)} %get-tuple-element.94), channel_id=1, source_target_pairs={{0,1},{1,2},{2,3},{4,5},{5,6},{6,7},{8,9},{9,10},{10,11},{12,13},{... | collective-permute-start | bytes 7688 | tf_op jit(solution)/shard_map/ppermute | solution.py:22
  87.1 12.3 %copy-start.28 = (f32[1,2,10,31,128]{4,1,3,2,0:T(2,128)S(1)}, f32[1,2,10,31,128]{4,1,3,2,0:T(2,128)}, u32[]{:S(2)}) copy-start(f32[1,2,10,31,128]{4,1,3,2,0:T(2,128)} %get-tuple-element.45) | copy-start | bytes 952324
  87.2 13.2 %copy-start.27 = (f32[1,2,10,31,128]{4,1,3,2,0:T(2,128)S(1)}, f32[1,2,10,31,128]{4,1,3,2,0:T(2,128)}, u32[]{:S(2)}) copy-start(f32[1,2,10,31,128]{4,1,3,2,0:T(2,128)} %get-tuple-element.44) | copy-start | bytes 952324
  87.2 75.9 %collective-permute-start.1 = (f32[1,2,10,1,128]{4,1,3,2,0:T(2,128)S(1)}, f32[1,2,10,1,128]{4,1,3,2,0:T(2,128)S(1)}, u32[]{:S(2)}, u32[]{:S(2)}) collective-permute-start(f32[1,2,10,1,128]{4,1,3,2,0:T(2,128)S(1)} %get-tuple-element.98), channel_id=1, source_target_pairs={{0,4},{4,8},{8,12},{12,16},{16,20},{20,24},{24,28},{28,0},{1,5},{5... | collective-permute-start | bytes 30728 | tf_op jit(solution)/shard_map/ppermute | solution.py:16
  92.6 73.3 %collective-permute-start = (f32[1,2,10,1,128]{4,1,3,2,0:T(2,128)S(1)}, f32[1,2,10,1,128]{4,1,3,2,0:T(2,128)S(1)}, u32[]{:S(2)}, u32[]{:S(2)}) collective-permute-start(f32[1,2,10,1,128]{4,1,3,2,0:T(2,128)S(1)} %get-tuple-element.99), channel_id=1, source_target_pairs={{0,28},{4,0},{8,4},{12,8},{16,12},{20,16},{24,20},{28,24},{1,29},{... | collective-permute-start | bytes 30728 | tf_op jit(solution)/shard_map/ppermute | solution.py:16
  100.4 19.5 %copy-start.43 = (pred[4,10,32,128]{3,0,2,1:T(4,128)(4,1)S(1)}, pred[4,10,32,128]{3,0,2,1:T(4,128)(4,1)}, u32[]{:S(2)}) copy-start(pred[4,10,32,128]{3,0,2,1:T(4,128)(4,1)} %copy-done.42) | copy-start | bytes 491524
  137.5 28.2 %copy-start.25 = (f32[1,2,10,31,128]{4,1,3,2,0:T(2,128)S(1)}, f32[1,2,10,31,128]{4,1,3,2,0:T(2,128)}, u32[]{:S(2)}) copy-start(f32[1,2,10,31,128]{4,1,3,2,0:T(2,128)} %get-tuple-element.100) | copy-start | bytes 952324
  137.5 28.4 %copy-start.23 = (f32[1,2,10,31,128]{4,1,3,2,0:T(2,128)S(1)}, f32[1,2,10,31,128]{4,1,3,2,0:T(2,128)}, u32[]{:S(2)}) copy-start(f32[1,2,10,31,128]{4,1,3,2,0:T(2,128)} %get-tuple-element.101) | copy-start | bytes 952324
  155.4 10.8 %collective-permute-start.22 = (f32[1,2,10,32,1]{4,1,3,2,0:T(2,128)S(1)}, f32[1,2,10,32,1]{4,1,3,2,0:T(2,128)S(1)}, u32[]{:S(2)}, u32[]{:S(2)}) collective-permute-start(f32[1,2,10,32,1]{4,1,3,2,0:T(2,128)S(1)} %get-tuple-element.25), channel_id=1, source_target_pairs={{1,0},{2,1},{3,2},{5,4},{6,5},{7,6},{9,8},{10,9},{11,10},{13,12},{... | collective-permute-start | bytes 7688 | tf_op jit(solution)/shard_map/ppermute | solution.py:22
  156.6 10.6 %collective-permute-start.23 = (f32[1,2,10,32,1]{4,1,3,2,0:T(2,128)S(1)}, f32[1,2,10,32,1]{4,1,3,2,0:T(2,128)S(1)}, u32[]{:S(2)}, u32[]{:S(2)}) collective-permute-start(f32[1,2,10,32,1]{4,1,3,2,0:T(2,128)S(1)} %get-tuple-element.24), channel_id=1, source_target_pairs={{0,1},{1,2},{2,3},{4,5},{5,6},{6,7},{8,9},{9,10},{10,11},{12,13},{... | collective-permute-start | bytes 7688 | tf_op jit(solution)/shard_map/ppermute | solution.py:22
  161.2 8.9 %collective-permute-start.21 = (f32[1,2,10,1,128]{4,1,3,2,0:T(2,128)S(1)}, f32[1,2,10,1,128]{4,1,3,2,0:T(2,128)S(1)}, u32[]{:S(2)}, u32[]{:S(2)}) collective-permute-start(f32[1,2,10,1,128]{4,1,3,2,0:T(2,128)S(1)} %get-tuple-element.28), channel_id=1, source_target_pairs={{0,4},{4,8},{8,12},{12,16},{16,20},{20,24},{24,28},{28,0},{1,5},{5... | collective-permute-start | bytes 30728 | tf_op jit(solution)/shard_map/ppermute | solution.py:16
  163.1 8.0 %collective-permute-start.20 = (f32[1,2,10,1,128]{4,1,3,2,0:T(2,128)S(1)}, f32[1,2,10,1,128]{4,1,3,2,0:T(2,128)S(1)}, u32[]{:S(2)}, u32[]{:S(2)}) collective-permute-start(f32[1,2,10,1,128]{4,1,3,2,0:T(2,128)S(1)} %get-tuple-element.29), channel_id=1, source_target_pairs={{0,28},{4,0},{8,4},{12,8},{16,12},{20,16},{24,20},{28,24},{1,29},{... | collective-permute-start | bytes 30728 | tf_op jit(solution)/shard_map/ppermute | solution.py:16
  171.0 21.2 %copy-start.51 = (f32[4,18,18]{2,0,1:T(4,128)S(1)}, f32[4,18,18]{2,0,1:T(4,128)}, u32[]{:S(2)}) copy-start(f32[4,18,18]{2,0,1:T(4,128)} %param.9) | copy-start | bytes 15556
  207.6 7.1 %copy-start.7 = (f32[18,10,32,128]{3,0,2,1:T(8,128)}, f32[18,10,32,128]{3,0,2,1:T(8,128)S(1)}, u32[]{:S(2)}) copy-start(f32[18,10,32,128]{3,0,2,1:T(8,128)S(1)} %fusion.3) | copy-start | bytes 8847364
  254.1 17.8 %copy-start.39 = (f32[1,2,10,32,1]{4,1,3,2,0:T(2,128)S(1)}, f32[1,2,10,32,1]{4,1,3,2,0:T(2,128)}, u32[]{:S(2)}) copy-start(f32[1,2,10,32,1]{4,1,3,2,0:T(2,128)} %get-tuple-element.11) | copy-start | bytes 7684
  254.1 19.3 %copy-start.38 = (f32[1,2,10,32,1]{4,1,3,2,0:T(2,128)S(1)}, f32[1,2,10,32,1]{4,1,3,2,0:T(2,128)}, u32[]{:S(2)}) copy-start(f32[1,2,10,32,1]{4,1,3,2,0:T(2,128)} %get-tuple-element.10) | copy-start | bytes 7684
  254.1 27.5 %copy-start.34 = (f32[1,2,9,32,128]{4,1,3,2,0:T(2,128)S(1)}, f32[1,2,9,32,128]{4,1,3,2,0:T(2,128)}, u32[]{:S(2)}) copy-start(f32[1,2,9,32,128]{4,1,3,2,0:T(2,128)} %get-tuple-element.7) | copy-start | bytes 884740
  254.1 27.7 %copy-start.33 = (f32[1,2,9,32,128]{4,1,3,2,0:T(2,128)S(1)}, f32[1,2,9,32,128]{4,1,3,2,0:T(2,128)}, u32[]{:S(2)}) copy-start(f32[1,2,9,32,128]{4,1,3,2,0:T(2,128)} %get-tuple-element.6) | copy-start | bytes 884740
  271.9 19.4 %copy-start.18 = (f32[1,2,10,32,127]{4,1,3,2,0:T(2,128)S(1)}, f32[1,2,10,32,127]{4,1,3,2,0:T(2,128)}, u32[]{:S(2)}) copy-start(f32[1,2,10,32,127]{4,1,3,2,0:T(2,128)} %get-tuple-element.12) | copy-start | bytes 975364
  271.9 11.9 %collective-permute-start.26 = (f32[1,2,10,32,1]{4,1,3,2,0:T(2,128)S(1)}, f32[1,2,10,32,1]{4,1,3,2,0:T(2,128)S(1)}, u32[]{:S(2)}, u32[]{:S(2)}) collective-permute-start(f32[1,2,10,32,1]{4,1,3,2,0:T(2,128)S(1)} %copy-done.39), channel_id=1, source_target_pairs={{1,0},{2,1},{3,2},{5,4},{6,5},{7,6},{9,8},{10,9},{11,10},{13,12},{... | collective-permute-start | bytes 7688 | tf_op jit(solution)/shard_map/ppermute | solution.py:22
  273.4 15.1 %collective-permute-start.27 = (f32[1,2,10,32,1]{4,1,3,2,0:T(2,128)S(1)}, f32[1,2,10,32,1]{4,1,3,2,0:T(2,128)S(1)}, u32[]{:S(2)}, u32[]{:S(2)}) collective-permute-start(f32[1,2,10,32,1]{4,1,3,2,0:T(2,128)S(1)} %copy-done.38), channel_id=1, source_target_pairs={{0,1},{1,2},{2,3},{4,5},{5,6},{6,7},{8,9},{9,10},{10,11},{12,13},{... | collective-permute-start | bytes 7688 | tf_op jit(solution)/shard_map/ppermute | solution.py:22
  278.4 63.8 %collective-permute-start.24 = (f32[1,2,10,1,128]{4,1,3,2,0:T(2,128)}, f32[1,2,10,1,128]{4,1,3,2,0:T(2,128)}, u32[]{:S(2)}, u32[]{:S(2)}) collective-permute-start(f32[1,2,10,1,128]{4,1,3,2,0:T(2,128)} %get-tuple-element.15), channel_id=1, source_target_pairs={{0,28},{4,0},{8,4},{12,8},{16,12},{20,16},{24,20},{28,24},{1,29},{... | collective-permute-start | bytes 30728 | tf_op jit(solution)/shard_map/ppermute | solution.py:16
  280.3 62.8 %collective-permute-start.25 = (f32[1,2,10,1,128]{4,1,3,2,0:T(2,128)S(1)}, f32[1,2,10,1,128]{4,1,3,2,0:T(2,128)}, u32[]{:S(2)}, u32[]{:S(2)}) collective-permute-start(f32[1,2,10,1,128]{4,1,3,2,0:T(2,128)S(1)} %get-tuple-element.14), channel_id=1, source_target_pairs={{0,4},{4,8},{8,12},{12,16},{16,20},{20,24},{24,28},{28,0},{1,5},{5... | collective-permute-start | bytes 30728 | tf_op jit(solution)/shard_map/ppermute | solution.py:16
  280.3 13.4 %collective-permute-start.6 = (f32[1,2,10,32,1]{4,1,3,2,0:T(2,128)S(1)}, f32[1,2,10,32,1]{4,1,3,2,0:T(2,128)S(1)}, u32[]{:S(2)}, u32[]{:S(2)}) collective-permute-start(f32[1,2,10,32,1]{4,1,3,2,0:T(2,128)S(1)} %get-tuple-element.81), channel_id=1, source_target_pairs={{1,0},{2,1},{3,2},{5,4},{6,5},{7,6},{9,8},{10,9},{11,10},{13,12},{... | collective-permute-start | bytes 7688 | tf_op jit(solution)/shard_map/ppermute | solution.py:22
  281.8 10.8 %copy-start.17 = (f32[1,2,10,32,127]{4,1,3,2,0:T(2,128)S(1)}, f32[1,2,10,32,127]{4,1,3,2,0:T(2,128)}, u32[]{:S(2)}) copy-start(f32[1,2,10,32,127]{4,1,3,2,0:T(2,128)} %get-tuple-element.13) | copy-start | bytes 975364
  283.9 12.3 %collective-permute-start.7 = (f32[1,2,10,32,1]{4,1,3,2,0:T(2,128)S(1)}, f32[1,2,10,32,1]{4,1,3,2,0:T(2,128)S(1)}, u32[]{:S(2)}, u32[]{:S(2)}) collective-permute-start(f32[1,2,10,32,1]{4,1,3,2,0:T(2,128)S(1)} %get-tuple-element.80), channel_id=1, source_target_pairs={{0,1},{1,2},{2,3},{4,5},{5,6},{6,7},{8,9},{9,10},{10,11},{12,13},{... | collective-permute-start | bytes 7688 | tf_op jit(solution)/shard_map/ppermute | solution.py:22
  288.4 10.6 %collective-permute-start.5 = (f32[1,2,10,1,128]{4,1,3,2,0:T(2,128)S(1)}, f32[1,2,10,1,128]{4,1,3,2,0:T(2,128)S(1)}, u32[]{:S(2)}, u32[]{:S(2)}) collective-permute-start(f32[1,2,10,1,128]{4,1,3,2,0:T(2,128)S(1)} %get-tuple-element.84), channel_id=1, source_target_pairs={{0,4},{4,8},{8,12},{12,16},{16,20},{20,24},{24,28},{28,0},{1,5},{5... | collective-permute-start | bytes 30728 | tf_op jit(solution)/shard_map/ppermute | solution.py:16
  293.7 6.2 collective-permute-start.4
  299.9 21.2 %copy-start.52 = (f32[4,18,18]{2,0,1:T(4,128)S(1)}, f32[4,18,18]{2,0,1:T(4,128)}, u32[]{:S(2)}) copy-start(f32[4,18,18]{2,0,1:T(4,128)} %param.9) | copy-start | bytes 15556
  336.7 7.3 %copy-start.15 = (f32[1,2,10,32,128]{4,1,3,2,0:T(2,128)S(1)}, f32[1,2,10,32,128]{4,1,3,2,0:T(2,128)}, u32[]{:S(2)}) copy-start(f32[1,2,10,32,128]{4,1,3,2,0:T(2,128)} %pad_maximum_fusion.39) | copy-start | bytes 983044
  336.7 7.3 %copy-start.16 = (f32[1,2,10,32,128]{4,1,3,2,0:T(2,128)S(1)}, f32[1,2,10,32,128]{4,1,3,2,0:T(2,128)}, u32[]{:S(2)}) copy-start(f32[1,2,10,32,128]{4,1,3,2,0:T(2,128)} %pad_maximum_fusion.38) | copy-start | bytes 983044
  361.1 15.8 %copy-start.3 = (f32[1,18,10,32,128]{4,1,3,2,0:T(8,128)S(1)}, f32[1,18,10,32,128]{4,1,3,2,0:T(8,128)}, u32[]{:S(2)}) copy-start(f32[1,18,10,32,128]{4,1,3,2,0:T(8,128)} %concatenate.153) | copy-start | bytes 8847364
  361.2 16.3 %copy-start.41 = (f32[1,2,10,32,1]{4,1,3,2,0:T(2,128)S(1)}, f32[1,2,10,32,1]{4,1,3,2,0:T(2,128)}, u32[]{:S(2)}) copy-start(f32[1,2,10,32,1]{4,1,3,2,0:T(2,128)} %get-tuple-element.67) | copy-start | bytes 7684
  361.2 17.9 %copy-start.40 = (f32[1,2,10,32,1]{4,1,3,2,0:T(2,128)S(1)}, f32[1,2,10,32,1]{4,1,3,2,0:T(2,128)}, u32[]{:S(2)}) copy-start(f32[1,2,10,32,1]{4,1,3,2,0:T(2,128)} %get-tuple-element.66) | copy-start | bytes 7684
  377.0 7.3 %copy-start.48 = (f32[1,2,10,1,128]{4,1,3,2,0:T(2,128)S(1)}, f32[1,2,10,1,128]{4,1,3,2,0:T(2,128)}, u32[]{:S(2)}) copy-start(f32[1,2,10,1,128]{4,1,3,2,0:T(2,128)} %get-tuple-element.70) | copy-start | bytes 30724
  377.0 7.3 %copy-start.47 = (f32[1,2,10,1,128]{4,1,3,2,0:T(2,128)S(1)}, f32[1,2,10,1,128]{4,1,3,2,0:T(2,128)}, u32[]{:S(2)}) copy-start(f32[1,2,10,1,128]{4,1,3,2,0:T(2,128)} %get-tuple-element.71) | copy-start | bytes 30724
  377.0 10.0 %copy-start.4 = (f32[1,18,10,32,128]{4,1,3,2,0:T(8,128)S(1)}, f32[1,18,10,32,128]{4,1,3,2,0:T(8,128)}, u32[]{:S(2)}) copy-start(f32[1,18,10,32,128]{4,1,3,2,0:T(8,128)} %concatenate.160) | copy-start | bytes 8847364
  377.0 10.0 %copy-start.13 = (f32[18,10,32,128]{3,0,2,1:T(8,128)S(1)}, f32[18,10,32,128]{3,0,2,1:T(8,128)}, u32[]{:S(2)}) copy-start(f32[18,10,32,128]{3,0,2,1:T(8,128)} %fusion.1) | copy-start | bytes 8847364
  377.5 12.5 %collective-permute-start.10 = (f32[1,2,10,32,1]{4,1,3,2,0:T(2,128)S(1)}, f32[1,2,10,32,1]{4,1,3,2,0:T(2,128)S(1)}, u32[]{:S(2)}, u32[]{:S(2)}) collective-permute-start(f32[1,2,10,32,1]{4,1,3,2,0:T(2,128)S(1)} %copy-done.41), channel_id=1, source_target_pairs={{1,0},{2,1},{3,2},{5,4},{6,5},{7,6},{9,8},{10,9},{11,10},{13,12},{... | collective-permute-start | bytes 7688 | tf_op jit(solution)/shard_map/ppermute | solution.py:22
  379.0 12.1 %collective-permute-start.11 = (f32[1,2,10,32,1]{4,1,3,2,0:T(2,128)S(1)}, f32[1,2,10,32,1]{4,1,3,2,0:T(2,128)S(1)}, u32[]{:S(2)}, u32[]{:S(2)}) collective-permute-start(f32[1,2,10,32,1]{4,1,3,2,0:T(2,128)S(1)} %copy-done.40), channel_id=1, source_target_pairs={{0,1},{1,2},{2,3},{4,5},{5,6},{6,7},{8,9},{9,10},{10,11},{12,13},{... | collective-permute-start | bytes 7688 | tf_op jit(solution)/shard_map/ppermute | solution.py:22
  384.2 8.4 %collective-permute-start.9 = (f32[1,2,10,1,128]{4,1,3,2,0:T(2,128)S(1)}, f32[1,2,10,1,128]{4,1,3,2,0:T(2,128)S(1)}, u32[]{:S(2)}, u32[]{:S(2)}) collective-permute-start(f32[1,2,10,1,128]{4,1,3,2,0:T(2,128)S(1)} %copy-done.48), channel_id=1, source_target_pairs={{0,4},{4,8},{8,12},{12,16},{16,20},{20,24},{24,28},{28,0},{1,5},{5... | collective-permute-start | bytes 30728 | tf_op jit(solution)/shard_map/ppermute | solution.py:16
  384.3 8.5 %collective-permute-start.8 = (f32[1,2,10,1,128]{4,1,3,2,0:T(2,128)S(1)}, f32[1,2,10,1,128]{4,1,3,2,0:T(2,128)S(1)}, u32[]{:S(2)}, u32[]{:S(2)}) collective-permute-start(f32[1,2,10,1,128]{4,1,3,2,0:T(2,128)S(1)} %copy-done.47), channel_id=1, source_target_pairs={{0,28},{4,0},{8,4},{12,8},{16,12},{20,16},{24,20},{28,24},{1,29},{... | collective-permute-start | bytes 30728 | tf_op jit(solution)/shard_map/ppermute | solution.py:16
  392.8 17.5 %copy-start.53 = (f32[4,18,18]{2,0,1:T(4,128)S(1)}, f32[4,18,18]{2,0,1:T(4,128)}, u32[]{:S(2)}) copy-start(f32[4,18,18]{2,0,1:T(4,128)} %param.9) | copy-start | bytes 15556
  410.3 17.1 %copy-start.12 = (f32[18,10,32,128]{3,0,2,1:T(8,128)S(1)}, f32[18,10,32,128]{3,0,2,1:T(8,128)}, u32[]{:S(2)}) copy-start(f32[18,10,32,128]{3,0,2,1:T(8,128)} %fusion) | copy-start | bytes 8847364
  428.5 11.2 %collective-permute-start.14 = (f32[1,2,10,32,1]{4,1,3,2,0:T(2,128)S(1)}, f32[1,2,10,32,1]{4,1,3,2,0:T(2,128)S(1)}, u32[]{:S(2)}, u32[]{:S(2)}) collective-permute-start(f32[1,2,10,32,1]{4,1,3,2,0:T(2,128)S(1)} %get-tuple-element.53), channel_id=1, source_target_pairs={{1,0},{2,1},{3,2},{5,4},{6,5},{7,6},{9,8},{10,9},{11,10},{13,12},{... | collective-permute-start | bytes 7688 | tf_op jit(solution)/shard_map/ppermute | solution.py:22
  429.8 11.1 %collective-permute-start.15 = (f32[1,2,10,32,1]{4,1,3,2,0:T(2,128)S(1)}, f32[1,2,10,32,1]{4,1,3,2,0:T(2,128)S(1)}, u32[]{:S(2)}, u32[]{:S(2)}) collective-permute-start(f32[1,2,10,32,1]{4,1,3,2,0:T(2,128)S(1)} %get-tuple-element.52), channel_id=1, source_target_pairs={{0,1},{1,2},{2,3},{4,5},{5,6},{6,7},{8,9},{9,10},{10,11},{12,13},{... | collective-permute-start | bytes 7688 | tf_op jit(solution)/shard_map/ppermute | solution.py:22
  434.8 7.5 %collective-permute-start.13 = (f32[1,2,10,1,128]{4,1,3,2,0:T(2,128)S(1)}, f32[1,2,10,1,128]{4,1,3,2,0:T(2,128)S(1)}, u32[]{:S(2)}, u32[]{:S(2)}) collective-permute-start(f32[1,2,10,1,128]{4,1,3,2,0:T(2,128)S(1)} %get-tuple-element.56), channel_id=1, source_target_pairs={{0,4},{4,8},{8,12},{12,16},{16,20},{20,24},{24,28},{28,0},{1,5},{5... | collective-permute-start | bytes 30728 | tf_op jit(solution)/shard_map/ppermute | solution.py:16
  434.9 7.6 %collective-permute-start.12 = (f32[1,2,10,1,128]{4,1,3,2,0:T(2,128)S(1)}, f32[1,2,10,1,128]{4,1,3,2,0:T(2,128)S(1)}, u32[]{:S(2)}, u32[]{:S(2)}) collective-permute-start(f32[1,2,10,1,128]{4,1,3,2,0:T(2,128)S(1)} %get-tuple-element.57), channel_id=1, source_target_pairs={{0,28},{4,0},{8,4},{12,8},{16,12},{20,16},{24,20},{28,24},{1,29},{... | collective-permute-start | bytes 30728 | tf_op jit(solution)/shard_map/ppermute | solution.py:16
  460.1 26.7 %copy-start.54 = (f32[4,18,18]{2,0,1:T(4,128)S(1)}, f32[4,18,18]{2,0,1:T(4,128)}, u32[]{:S(2)}) copy-start(f32[4,18,18]{2,0,1:T(4,128)} %param.9) | copy-start | bytes 15556
  486.7 131.3 %copy-start.1 = (f32[18,10,32,128]{3,2,1,0:T(8,128)S(1)}, f32[18,10,32,128]{3,2,1,0:T(8,128)}, u32[]{:S(2)}) copy-start(f32[18,10,32,128]{3,2,1,0:T(8,128)} %param.7) | copy-start | bytes 8847364
  (20 other events, 83.4 us)
Sparse Core Ops, SparseCore 0:
  486.8 129.7 all-reduce.2
where the time goes:
time: 637 us; the launch traced here: 625 us
  matrix products  187 us (29%)
  local copies, waits for them, and re-layouts  172 us (27%)
  waiting for transfers between devices  119 us (19%)
  other arithmetic  69 us (11%)
  starting transfers between devices  62.5 us (10%)
  between operations  15.8 us (2%)
    dot_general x11, matrix products, apply_table(): product = jnp.einsum(form, table, field, precision=lax.Precision.HIGHEST)  187 us
    concatenate x7, local copies, waits for them, and re-layouts, connect(): jnp.concatenate([new_east, new_west, new_north, new_south, new_upper, new...  131 us
    unnamed x2, waiting for transfers between devices  112 us
    ppermute x14, starting transfers between devices, passed_along(): return lax.ppermute(block, axis, route)  45.2 us
    scatter-add x1, other arithmetic, shards(): jnp.zeros((owned * owners_count,), jnp.float32).at[identities].add(values)  22.8 us
    ppermute x14, starting transfers between devices, from_behind(): return lax.ppermute(value, axis, pairs)  17.3 us
  transfers between devices with their start and end apart: 29, of which 7 were waited for; matrix products, arithmetic and copies ran while one was open for 30% of the time, Pallas kernels for 0%

commit v1 on v0

v1 whole, which is shorter than its diff:
```python
import functools

import jax
import jax.numpy as jnp
from jax import lax
from jax.experimental import pallas as pl
from jax.experimental.pallas import tpu as pltpu
from jax.sharding import PartitionSpec as P

BW = 8
ITERS = 4
HALO = 4
SUB = 8
LANES = 128
GROUP = LANES // (2 * HALO)
MSG = 40
ROWS = 24
KDIM = 144
F32 = jnp.float32
BF16 = jnp.bfloat16
sens_scale = 1.0 / 32.0
MIB = 2**20
VMEM = pl.BlockSpec(memory_space=pltpu.VMEM)
SMEM = pl.BlockSpec(memory_space=pltpu.SMEM)
ANY = pl.BlockSpec(memory_space=pl.ANY)


def iota(shape, dim):
    return lax.broadcasted_iota(jnp.int32, shape, dim)


def roll(value, amount, axis):
    return pltpu.roll(value, amount, axis)


def shifted(block):
    row = iota((SUB, LANES), 0)
    up = roll(block, LANES - 1, 1)
    down = roll(block, 1, 1)
    return jnp.where(row < 4, block, jnp.where(row < 6, up, down))


def swap_pairs(block):
    row = iota((SUB, LANES), 0)
    return jnp.where(row % 4 < 2, roll(block, SUB - 2, 0), roll(block, 2, 0))


def swap_first(block):
    row = iota((SUB, LANES), 0)
    return jnp.where(row < 4, swap_pairs(block), block)


def pack_kernel(inc, cot, mat, low, high, pk, es, xl, xr):
    z = pl.program_id(0)
    cz = pl.num_programs(0)
    nx = inc.shape[2]
    lane = iota((SUB, LANES), 1)
    row = iota((SUB, LANES), 0)
    spread = (iota((mat.shape[2], LANES), 1) // BW == iota((mat.shape[2], LANES), 0)).astype(BF16)

    def expand(codes):
        return jnp.dot(codes.astype(F32).astype(BF16), spread, preferred_element_type=F32)

    def coefficient(codes):
        return jnp.where(codes == 0, -1.0, jnp.where(codes == 1, 1.0, 0.0))

    code = expand(mat[0])
    lower = expand(coefficient(low[0]))
    upper = expand(coefficient(high[0]))
    ends = jnp.where(z == 0, lower, jnp.where(z == cz - 1, upper, 0.0))
    flat_inc = inc.reshape(inc.shape[0] * nx, LANES)
    flat_cot = cot.reshape(cot.shape[0] * nx, LANES)
    for half in range(nx // GROUP):
        edge = [jnp.zeros((SUB, LANES), F32) for _ in range(5)]
        for g in range(GROUP):
            x = half * GROUP + g
            f0 = flat_inc[pl.ds(x, 8, stride=nx), :]
            f1 = flat_inc[pl.ds(8 * nx + x, 8, stride=nx), :]
            a0 = swap_pairs(flat_cot[pl.ds(x, 8, stride=nx), :])
            a1 = swap_first(flat_cot[pl.ds(8 * nx + x, 8, stride=nx), :])
            last = [
                flat_inc[pl.ds(16 * nx + x, 1), :],
                flat_inc[pl.ds(17 * nx + x, 1), :],
                flat_cot[pl.ds(16 * nx + x, 1), :],
                flat_cot[pl.ds(17 * nx + x, 1), :],
                code[x : x + 1],
                ends[x : x + 1],
            ]
            tail = jnp.zeros((SUB, LANES), F32)
            for i, value in enumerate(last):
                tail = jnp.where(row == i, jnp.broadcast_to(value, (SUB, LANES)), tail)
            mine = lane // (2 * HALO) == g
            for i, value in enumerate((f0, f1, a0, a1, tail)):
                edge[i] = jnp.where(mine, roll(value, 2 * HALO * g + HALO, 1), edge[i])
            for i, value in enumerate((f0, f1, shifted(a0), a1, tail)):
                pk[0, x, pl.ds(8 * i, 8), :] = value
                if x < HALO:
                    xl[0, x, pl.ds(8 * i, 8), :] = value
                if x >= nx - HALO:
                    xr[0, x - nx + HALO, pl.ds(8 * i, 8), :] = value
        for i in range(5):
            es[0, half, pl.ds(8 * i, 8), :] = edge[i]


def pack(incident, cotangent, material, lower, upper):
    ports, cz, nx, ny = incident.shape
    halves = nx // GROUP
    field = pl.BlockSpec((ports, 1, nx, ny), lambda z: (0, z, 0, 0))
    codes = pl.BlockSpec((1, nx, material.shape[2]), lambda z: (z, 0, 0))
    ends = pl.BlockSpec((1, nx, material.shape[2]), lambda z: (0, 0, 0))

    def out(rows):
        return pl.BlockSpec((1, rows, MSG, LANES), lambda z: (z, 0, 0, 0))

    def shape(rows):
        return jax.ShapeDtypeStruct((cz, rows, MSG, LANES), F32)

    sizes = (nx, halves, HALO, HALO)
    return pl.pallas_call(
        pack_kernel,
        grid=(cz,),
        in_specs=[field, field, codes, ends, ends],
        out_specs=[out(n) for n in sizes],
        out_shape=[shape(n) for n in sizes],
        compiler_params=pltpu.CompilerParams(vmem_limit_bytes=24 * MIB),
        name="pack",
    )(incident, cotangent, material, lower, upper)


def build_tables(scatter, deriv, tables):
    nmat, ports, _ = scatter.shape
    r = iota((ROWS, ports), 0)
    c = iota((ROWS, ports), 1)
    tail = (r >= 16) & (c == 16 + r % 2)
    natural = (((r < 16) & (r == c)) | tail).astype(F32).astype(BF16)
    swapped_port = jnp.where(r < 12, r + jnp.where(r % 4 < 2, 2, -2), r)
    permuted = (((r < 16) & (swapped_port == c)) | tail).astype(F32).astype(BF16)
    plain = (r == c).astype(F32).astype(BF16)
    q = iota((ports, KDIM), 0)
    k = iota((ports, KDIM), 1)

    def place(m):
        main = (k < 128) & ((k // 16) % 4 == m) & (q == k % 16)
        end = (k >= 128) & ((k % 8) // 2 == m) & (q == 16 + k % 2)
        return (main | end).astype(F32).astype(BF16)

    places = [place(m) for m in range(nmat)]

    def split(value):
        high = value.astype(BF16)
        return high, (value - high.astype(F32)).astype(BF16)

    def form(table, rows, transpose):
        parts = []
        for part in range(2):
            total = jnp.zeros((ROWS, KDIM), F32)
            for m in range(nmat):
                piece = split(table[m])[part]
                axes = (((1,), (1 if transpose else 0,)), ((), ()))
                picked = lax.dot_general(rows, piece, axes, preferred_element_type=F32).astype(BF16)
                total = total + jnp.dot(picked, places[m], preferred_element_type=F32)
            parts.append(total.astype(BF16))
        return parts

    forms = (
        form(scatter, permuted, False)
        + form(deriv, plain, False)
        + form(scatter, permuted, True)
        + form(scatter, natural, True)
    )
    for i, value in enumerate(forms):
        tables[pl.ds(ROWS * i, ROWS), :] = value.astype(F32)


def main_kernel(
    flags, scatter, deriv, pk, fl, fr, hl, hr,
    adjoint, column,
    rf, ra, rtail, masks, saved_d, saved_r, xf, xa, tf, ta, acc, tables, ebuf, sems,
):
    cz, nx = pk.shape[0], pk.shape[1]
    ne = nx + 2 * HALO
    nb = rf.shape[2] - ne
    row = iota((SUB, LANES), 0)
    lane = iota((SUB, LANES), 1)
    is_first = flags[0] == 1
    is_last = flags[1] == 1

    copies = []
    for i, (source, first, count) in enumerate(((pk, HALO, nx), (hl, 0, HALO), (hr, HALO + nx, HALO))):
        src = source.at[:, pl.ds(0, count)]
        for j, (target, at, size) in enumerate(
            ((rf.at[0, :, pl.ds(first, count), pl.ds(0, 16)], 0, 16),
             (ra.at[0, :, pl.ds(first, count), pl.ds(0, 16)], 16, 16),
             (rtail.at[:, pl.ds(first, count)], 32, 8))
        ):
            copies.append(pltpu.make_async_copy(src.at[:, :, pl.ds(at, size)], target, sems.at[3 * i + j]))
    for copy in copies:
        copy.start()
    build_tables(scatter, deriv, tables)

    def halo_blocks(z, _):
        for i in range(5):
            part = pl.ds(8 * i, 8)
            blocks = [
                roll(jnp.where(lane % 8 < HALO, fl[z, h, part, :], fr[z, h, part, :]), 8 * HALO, 1)
                for h in range(nb - 1)
            ]
            for b in range(nb):
                before = hl[z, HALO, part, :] if b == 0 else blocks[b - 1]
                after = hr[z, HALO, part, :] if b == nb - 1 else blocks[b]
                value = jnp.where(lane < 8 * HALO, before, after)
                if i == 0 or i == 1:
                    rf[0, z, ne + b, part, :] = value
                elif i == 2:
                    ra[0, z, ne + b, pl.ds(0, 8), :] = shifted(value)
                elif i == 3:
                    ra[0, z, ne + b, pl.ds(8, 8), :] = value
                else:
                    rtail[z, ne + b] = value
        return 0

    lax.fori_loop(0, cz, halo_blocks, 0)
    for copy in copies:
        copy.wait()

    def repeated(value):
        value = jnp.where(row < 2, value, 0.0)
        value = value + roll(value, 2, 0)
        return value + roll(value, 4, 0)

    wide_row = iota((16, LANES), 0)

    def start_rows(r, _):
        for z in range(cz):
            t = rtail[z, r]
            rf[0, z, r, pl.ds(16, 8), :] = repeated(t)
            ra[0, z, r, pl.ds(16, 8), :] = repeated(roll(t, 6, 0))
            code = jnp.broadcast_to(rtail[z, r, pl.ds(4, 1), :], (16, LANES))
            for m in range(4):
                masks[z, r, pl.ds(16 * m, 16), :] = jnp.where(code == m, 1.0, 0.0).astype(BF16)
            own = ((wide_row % 8) // 2).astype(F32)
            masks[z, r, pl.ds(64, 16), :] = jnp.where(code == own, 1.0, 0.0).astype(BF16)
        return 0

    lax.fori_loop(0, ne + nb, start_rows, 0)

    def operand(values, z, r):
        v0, v1, v2 = values
        main = jnp.concatenate([v0, v1], axis=0)
        high = main.astype(BF16)
        low = (main - high.astype(F32)).astype(BF16)
        high2 = v2.astype(BF16).astype(F32)
        end = jnp.concatenate([high2, v2 - high2], axis=0).astype(BF16)
        mask = [masks[z, r, pl.ds(16 * m, 16), :] for m in range(5)]
        pieces = [high * mask[m] for m in range(4)] + [low * mask[m] for m in range(4)]
        return jnp.concatenate(pieces + [end * mask[4]], axis=0)

    def apply(table, values, r):
        outs = []
        for z in range(0, cz, 2):
            rhs = jnp.concatenate([operand(values[z], z, r), operand(values[z + 1], z + 1, r)], axis=1)
            y = jnp.dot(table, rhs, preferred_element_type=F32)
            for h in range(2):
                part = y[:, h * LANES : (h + 1) * LANES]
                outs.append([
                    [part[at + 8 * i : at + 8 * i + 8] + part[at + ROWS + 8 * i : at + ROWS + 8 * i + 8] for i in range(3)]
                    for at in range(0, table.shape[0], 2 * ROWS)
                ])
        return outs

    def read(ref, slot, r):
        return [[ref[slot, z, r, pl.ds(8 * i, 8), :] for i in range(3)] for z in range(cz)]

    def along_z(values, r):
        low = jnp.broadcast_to(rtail[0, r, pl.ds(5, 1), :], (SUB, LANES))
        high = jnp.broadcast_to(rtail[cz - 1, r, pl.ds(5, 1), :], (SUB, LANES))
        outs = []
        for z in range(cz):
            own = values[z][1]
            above = values[z + 1][1] if z + 1 < cz else high * roll(own, 6, 0)
            below = values[z - 1][1] if z > 0 else low * roll(own, 2, 0)
            outs.append(jnp.where(row < 2, above, jnp.where(row < 4, below, own)))
        return outs

    at_ends = ((row // 2 == 2) & (lane == LANES - 1)) | ((row // 2 == 3) & (lane == 0))
    at_edges = ((row // 2 == 2) & (lane % 8 == HALO - 1)) | ((row // 2 == 3) & (lane % 8 == HALO))

    def connect_row(ref, slot, tm, e):
        values = read(ref, slot, e)
        planes = along_z(values, e)
        amount = LANES - (8 * (e % GROUP) + HALO)
        outs = []
        for z in range(cz):
            after = ref[slot, z, e + 1, pl.ds(0, 8), :]
            before = ref[slot, z, e - 1, pl.ds(0, 8), :]
            outer = roll(tm[z, e // GROUP], amount, 1)
            own = jnp.where(at_ends, outer, values[z][0])
            outs.append([jnp.where(row < 2, after, jnp.where(row < 4, before, own)), planes[z], values[z][2]])
        return outs

    def connect_edge(ref, slot, x, tm, b):
        r = ne + b
        values = read(ref, slot, r)
        planes = along_z(values, r)
        outs = []
        for z in range(cz):
            own = values[z][0]
            nxt = ref[slot, z, ne + (b + 1) % nb, pl.ds(0, 8), :]
            prv = ref[slot, z, ne + (b + nb - 1) % nb, pl.ds(0, 8), :]
            after = roll(jnp.where(lane >= 8, own, nxt), LANES - 8, 1)
            before = roll(jnp.where(lane < LANES - 8, own, prv), 8, 1)
            inner = x[z, b]
            top = roll(roll(inner, LANES - 1, 1), 6, 0)
            bottom = roll(roll(inner, 1, 1), 2, 0)
            tm[z, b] = jnp.where(
                is_last & (row < 6), -top, jnp.where(is_first & (row >= 6), -bottom, own)
            )
            own = jnp.where(at_edges, inner, own)
            outs.append([jnp.where(row < 2, after, jnp.where(row < 4, before, own)), planes[z], values[z][2]])
        return outs

    def collect(x, e, blocks):
        g = e % GROUP
        for z in range(cz):
            moved = roll(blocks[z], 8 * g + HALO, 1)
            x[z, e // GROUP] = jnp.where(lane // 8 == g, moved, x[z, e // GROUP])

    def write(ref, slot, r, z, part):
        first = shifted(part[0])
        ref[slot, z, r, pl.ds(0, 8), :] = first
        ref[slot, z, r, pl.ds(8, 8), :] = part[1]
        ref[slot, z, r, pl.ds(16, 8), :] = part[2]
        return first

    for x in (xf, xa):
        x[...] = jnp.zeros_like(x)

    def gather_first(e, _):
        collect(xa, e, [ra[0, z, e, pl.ds(0, 8), :] for z in range(cz)])
        return 0

    lax.fori_loop(0, ne, gather_first, 0)
    flat = adjoint.reshape(adjoint.shape[0] * cz * nx, LANES)

    def product(e, left, right):
        total = acc[e]
        for z in range(cz):
            for i in range(3):
                total = total + left[z][i] * right(z, i)
        acc[e] = total

    for step in range(ITERS):
        slot, other = step % 2, (step + 1) % 2
        last = step == ITERS - 1
        s_table = tables[pl.ds(0, 2 * ROWS), :].astype(BF16)
        sd_table = tables[pl.ds(0, 4 * ROWS), :].astype(BF16)
        d_table = tables[pl.ds(2 * ROWS, 2 * ROWS), :].astype(BF16)
        a_table = tables[pl.ds((6 if last else 4) * ROWS, 2 * ROWS), :].astype(BF16)

        def edges(b, _, step=step, slot=slot, other=other, last=last, s_table=s_table, a_table=a_table):
            av = connect_edge(ra, slot, xa, ta, b)
            fv = connect_edge(rf, slot, xf, tf, b) if step > 0 else read(rf, slot, ne + b)
            if not last:
                for z, parts in enumerate(apply(a_table, av, ne + b)):
                    write(ra, other, ne + b, z, parts[0])
                for z, parts in enumerate(apply(s_table, fv, ne + b)):
                    write(rf, other, ne + b, z, parts[0])
            return 0

        lax.fori_loop(0, nb, edges, 0)

        def rows(e, _, step=step, slot=slot, other=other, last=last, sd_table=sd_table, d_table=d_table, a_table=a_table):
            av = connect_row(ra, slot, ta, e)
            fv = connect_row(rf, slot, tf, e) if step > 0 else read(rf, slot, e)
            a_out = apply(a_table, av, e)
            if last:
                for z in range(cz):
                    part = a_out[z][0]
                    at = z * nx + e - HALO
                    flat[pl.ds(at, 8, stride=cz * nx), :] = part[0]
                    flat[pl.ds(8 * cz * nx + at, 8, stride=cz * nx), :] = part[1]
                    flat[pl.ds(16 * cz * nx + at, 1), :] = part[2][0:1]
                    flat[pl.ds(17 * cz * nx + at, 1), :] = part[2][1:2]
                change = [parts[0] for parts in apply(d_table, fv, e)]
            else:
                collect(xa, e, [write(ra, other, e, z, a_out[z][0]) for z in range(cz)])
                f_out = apply(sd_table, fv, e)
                collect(xf, e, [write(rf, other, e, z, f_out[z][0]) for z in range(cz)])
                change = [parts[1] for parts in f_out]
            if step < 2:
                for z in range(cz):
                    for i in range(3):
                        saved_r[step, z, e, pl.ds(8 * i, 8), :] = av[z][i]
                        saved_d[step, z, e, pl.ds(8 * i, 8), :] = change[z][i]
            else:
                k = ITERS - 1 - step
                product(e, av, lambda z, i: saved_d[k, z, e, pl.ds(8 * i, 8), :])
                product(e, change, lambda z, i: saved_r[k, z, e, pl.ds(8 * i, 8), :])
            return 0

        if step == 0:
            acc[...] = jnp.zeros_like(acc)
        lax.fori_loop(1 + step, ne - 1 - step, rows, 0)

    for x in range(nx):
        column[pl.ds(x, 1), :] = jnp.sum(acc[HALO + x], axis=0, keepdims=True) * sens_scale


def main_call(flags, scatter, deriv, pk, fl, fr, hl, hr):
    cz, nx = pk.shape[0], pk.shape[1]
    ports = scatter.shape[1]
    ne = nx + 2 * HALO
    nb = ne // GROUP + 1
    total = ne + nb
    return pl.pallas_call(
        main_kernel,
        in_specs=[SMEM, VMEM, VMEM, ANY, VMEM, VMEM, VMEM, VMEM],
        out_specs=[VMEM, VMEM],
        out_shape=[
            jax.ShapeDtypeStruct((ports, cz, nx, LANES), F32),
            jax.ShapeDtypeStruct((nx, LANES), F32),
        ],
        scratch_shapes=[
            pltpu.VMEM((2, cz, total, ROWS, LANES), F32),
            pltpu.VMEM((2, cz, total, ROWS, LANES), F32),
            pltpu.VMEM((cz, total, SUB, LANES), F32),
            pltpu.VMEM((cz, total, 80, LANES), BF16),
            pltpu.VMEM((2, cz, ne, ROWS, LANES), F32),
            pltpu.VMEM((2, cz, ne, ROWS, LANES), F32),
            pltpu.VMEM((cz, nb, SUB, LANES), F32),
            pltpu.VMEM((cz, nb, SUB, LANES), F32),
            pltpu.VMEM((cz, nb, SUB, LANES), F32),
            pltpu.VMEM((cz, nb, SUB, LANES), F32),
            pltpu.VMEM((ne, SUB, LANES), F32),
            pltpu.VMEM((8 * ROWS, KDIM), F32),
            pltpu.VMEM((SUB, LANES), F32),
            pltpu.SemaphoreType.DMA((9,)),
        ],
        compiler_params=pltpu.CompilerParams(vmem_limit_bytes=63 * MIB),
        name="adjoint_steps",
    )(flags, scatter, deriv, pk, fl, fr, hl, hr)


def route_kernel(ids, owner_hot, rank_hot, id_slots):
    nx = ids.shape[0]
    ndev, cap = id_slots.shape
    owned = nx * LANES
    who = iota((ndev, LANES), 0)
    place = iota((cap, LANES), 0)
    before = (iota((LANES, LANES), 0) < iota((LANES, LANES), 1)).astype(BF16)
    offset = jnp.zeros((ndev, 1), F32)
    id_slots[...] = jnp.zeros_like(id_slots)
    for x in range(nx):
        wanted = ids[pl.ds(x, 1), :]
        hot = (wanted // owned == who).astype(F32)
        counts = jnp.dot(hot.astype(BF16), before, preferred_element_type=F32) + offset
        rank = jnp.sum(hot * counts, axis=0, keepdims=True).astype(jnp.int32)
        ranked = (rank == place).astype(F32).astype(BF16)
        offset = offset + jnp.sum(hot, axis=1, keepdims=True)
        local = wanted % owned
        owner_hot[:, pl.ds(x * LANES, LANES)] = hot.astype(BF16)
        rank_hot[:, pl.ds(x * LANES, LANES)] = ranked
        high = (hot * (local // 64).astype(F32)).astype(BF16)
        low = (hot * (local % 64).astype(F32)).astype(BF16)
        both = lax.dot_general(
            jnp.concatenate([high, low], axis=0), ranked, (((1,), (1,)), ((), ())), preferred_element_type=F32
        )
        id_slots[...] += 64.0 * both[:ndev] + both[ndev:]


def route(ids, ndev, cap):
    n = ids.shape[0] * ids.shape[1]
    return pl.pallas_call(
        route_kernel,
        in_specs=[VMEM],
        out_specs=[VMEM] * 3,
        out_shape=[
            jax.ShapeDtypeStruct((ndev, n), BF16),
            jax.ShapeDtypeStruct((cap, n), BF16),
            jax.ShapeDtypeStruct((ndev, cap), F32),
        ],
        compiler_params=pltpu.CompilerParams(vmem_limit_bytes=24 * MIB),
        name="route",
    )(ids)


def send_kernel(column, owner_hot, rank_hot, id_slots, message):
    nx = column.shape[0]
    ndev, cap = id_slots.shape
    total = jnp.zeros((2 * ndev, cap), F32)
    for x in range(nx):
        value = jnp.broadcast_to(column[pl.ds(x, 1), :], (ndev, LANES))
        high = value.astype(BF16)
        low = (value - high.astype(F32)).astype(BF16)
        part = pl.ds(x * LANES, LANES)
        hot = owner_hot[:, part]
        total = total + lax.dot_general(
            jnp.concatenate([high * hot, low * hot], axis=0), rank_hot[:, part],
            (((1,), (1,)), ((), ())), preferred_element_type=F32,
        )
    message[:, pl.ds(0, cap)] = total[:ndev] + total[ndev:]
    message[:, pl.ds(cap, cap)] = id_slots[...]


def send(column, owner_hot, rank_hot, id_slots):
    ndev, cap = id_slots.shape
    return pl.pallas_call(
        send_kernel,
        in_specs=[VMEM] * 4,
        out_specs=VMEM,
        out_shape=jax.ShapeDtypeStruct((ndev, 2 * cap), F32),
        compiler_params=pltpu.CompilerParams(vmem_limit_bytes=24 * MIB),
        name="send",
    )(column, owner_hot, rank_hot, id_slots)


def gather_kernel(message, out):
    ndev, cap = message.shape[0], message.shape[1] // 2
    nrow = out.shape[0]
    rows = iota((nrow, cap), 0)
    lanes = iota((LANES, cap), 0)
    total = jnp.zeros((2 * nrow, LANES), F32)
    for s in range(ndev):
        value = jnp.broadcast_to(message[pl.ds(s, 1), pl.ds(0, cap)], (nrow, cap))
        local = message[pl.ds(s, 1), pl.ds(cap, cap)].astype(jnp.int32)
        high = value.astype(BF16).astype(F32)
        mine = local // LANES == rows
        left = jnp.concatenate([jnp.where(mine, high, 0.0), jnp.where(mine, value - high, 0.0)], axis=0)
        right = (local % LANES == lanes).astype(F32).astype(BF16)
        total = total + lax.dot_general(
            left.astype(BF16), right, (((1,), (1,)), ((), ())), preferred_element_type=F32
        )
    out[...] = total[:nrow] + total[nrow:]


def gather(message, owned):
    return pl.pallas_call(
        gather_kernel,
        in_specs=[VMEM],
        out_specs=VMEM,
        out_shape=jax.ShapeDtypeStruct((owned // LANES, LANES), F32),
        compiler_params=pltpu.CompilerParams(vmem_limit_bytes=24 * MIB),
        name="gather",
    )(message)


def moved(block, axis, distance, wrap):
    count = lax.axis_size(axis)
    pairs = [(i, (i + distance) % count) for i in range(count) if wrap or 0 <= i + distance < count]
    return lax.ppermute(block, axis, pairs)


def shards(incident, cotangent, scatter_table, deriv_table, material_code, boundary_code, param_ids):
    position = lax.axis_index("gy")
    extent = lax.axis_size("gy")
    ndev = lax.axis_size("gx") * extent
    owned = param_ids.shape[0] * param_ids.shape[1]
    cap = 2 * owned // ndev
    pk, es, xl, xr = pack(incident, cotangent, material_code, boundary_code[0:1], boundary_code[1:2])
    fl = moved(es, "gy", 1, False)
    fr = moved(es, "gy", -1, False)
    owner_hot, rank_hot, id_slots = route(param_ids, ndev, cap)
    near = (jnp.arange(LANES) % (2 * HALO) < HALO)[None, None, None]
    low = jnp.where(near, fl[:, :1], fr[:, :1])
    high = jnp.where(near, fl[:, -1:], fr[:, -1:])
    place = 8 * HALO
    low = jnp.roll(low, place, axis=3)
    high = jnp.roll(high, place, axis=3)
    hr = moved(jnp.concatenate([xl, low], axis=1), "gx", -1, True)
    hl = moved(jnp.concatenate([xr, high], axis=1), "gx", 1, True)
    flags = jnp.stack([position == 0, position == extent - 1]).astype(jnp.int32)
    adjoint, column = main_call(flags, scatter_table, deriv_table, pk, fl, fr, hl, hr)
    message = send(column, owner_hot, rank_hot, id_slots)
    received = lax.all_to_all(message, ("gx", "gy"), 0, 0, tiled=True)
    sensitivity = gather(received, owned).reshape(-1)
    return adjoint, sensitivity


def solution(mesh):
    in_specs = (
        P(None, None, "gx", "gy"),
        P(None, None, "gx", "gy"),
        P(),
        P(),
        P(None, "gx", "gy"),
        P(None, "gx", "gy"),
        P("gx", "gy"),
    )
    out_specs = (P(None, None, "gx", "gy"), P(("gx", "gy")))
    return jax.shard_map(shards, mesh=mesh, in_specs=in_specs, out_specs=out_specs, check_vma=False)
```

time: 637 us -> 151 us (0.24); the launches traced: 625 us -> 151 us
  matrix products: 187 us -> 0 us
  local copies, waits for them, and re-layouts: 172 us -> 11.5 us
  Pallas kernels: 0 us -> 89.7 us
  waiting for transfers between devices: 119 us -> 30.2 us
  other arithmetic: 69 us -> 0.93 us
  starting transfers between devices: 62.5 us -> 7.05 us
  between operations: 15.8 us -> 0.82 us
  blocking collectives: 0 us -> 10.2 us
    dot_general x11 -> x0, matrix products: 187 us -> none  [apply_table(): product = jnp.einsum(form, table, field, precision=lax.Precision.HIGHEST)]
    concatenate x7 -> x0, local copies, waits for them, and re-layouts: 131 us -> none  [connect(): jnp.concatenate([new_east, new_west, new_north, new_south, new_upper, new...]
    unnamed x2 -> x0, waiting for transfers between devices: 112 us -> none
    pallas_call x0 -> x5, Pallas kernels: none -> 89.7 us  [the longest x1 79.2 us: main_call(): pl.pallas_call(main_kernel, in_specs=[SMEM, VMEM, VMEM, ANY, VMEM, VMEM,...]
    ppermute x28 -> x4, starting transfers between devices: 62.5 us -> 7.05 us  [moved(): return lax.ppermute(block, axis, pairs)]
    slice x42 -> x3, local copies, waits for them, and re-layouts: 30.3 us -> 0.93 us  [the longest x1 0.72 us: shards(): boundary_code[1:2]]
    concatenate x40 -> x2, other arithmetic: 27.3 us -> 0.26 us  [the longest x1 0.13 us: shards(): hr = moved(jnp.concatenate([xl, low], axis=1), 'gx', -1, True)]
    ppermute x28 -> x4, waiting for transfers between devices: 6.72 us -> 30.2 us  [moved(): return lax.ppermute(block, axis, pairs)]
  transfers between devices with their start and end apart: 29 -> 4, of which waited for: 7 -> 4; matrix products, arithmetic and copies ran while one was open for 30% -> 1% of each run, Pallas kernels for 0% -> 2%
where the time goes in v1:
time: 151 us
  Pallas kernels  89.7 us (59%)
  waiting for transfers between devices  30.2 us (20%)
  local copies, waits for them, and re-layouts  11.5 us (8%)
  blocking collectives  10.2 us (7%)
  starting transfers between devices  7.05 us (5%)
    pallas_call x1, Pallas kernels, main_call(): pl.pallas_call(main_kernel, in_specs=[SMEM, VMEM, VMEM, ANY, VMEM, VMEM,...  79.2 us
    ppermute x4, waiting for transfers between devices, moved(): return lax.ppermute(block, axis, pairs)  30.2 us
    unnamed x28, local copies, waits for them, and re-layouts  10.5 us
    all_to_all x1, blocking collectives, shards(): received = lax.all_to_all(message, ('gx', 'gy'), 0, 0, tiled=True)  10.2 us
    ppermute x4, starting transfers between devices, moved(): return lax.ppermute(block, axis, pairs)  7.05 us
    pallas_call x1, Pallas kernels, pack(): pl.pallas_call(pack_kernel, grid=(cz,), in_specs=[field, field, codes, en...  5.17 us
  transfers between devices with their start and end apart: 4, of which 4 were waited for; matrix products, arithmetic and copies ran while one was open for 1% of the time, Pallas kernels for 2%

profile of v1, /device:TPU:0, one launch (start us, length us, event | category | flops | bytes accessed | tf_op | source)
XLA Modules:
  0.0 150.5 jit_solution(16011683266189343976)
XLA Ops:
  0.6 0.7 fusion.1
  1.3 0.1 copy.21.low
  1.4 0.1 copy.22.high
  1.5 1.0 copy.16.mat
  2.5 0.0 copy-start.1
  2.5 1.8 %copy-done.1 = f32[18,10,32,128]{3,2,1,0:T(8,128)S(1)} copy-done((f32[18,10,32,128]{3,2,1,0:T(8,128)S(1)}, f32[18,10,32,128]{3,2,1,0:T(8,128)}, u32[]{:S(2)}) %copy-start.1) | copy-done | bytes 2949144
  4.3 0.0 copy-start.2
  4.3 1.8 %copy-done.2 = f32[18,10,32,128]{3,2,1,0:T(8,128)S(1)} copy-done((f32[18,10,32,128]{3,2,1,0:T(8,128)S(1)}, f32[18,10,32,128]{3,2,1,0:T(8,128)}, u32[]{:S(2)}) %copy-start.2) | copy-done | bytes 2949144
  6.2 5.2 %pack.1 = (f32[10,32,40,128]{3,2,1,0:T(8,128)S(1)}, f32[10,2,40,128]{3,2,1,0:T(8,128)S(1)}, f32[10,4,40,128]{3,2,1,0:T(8,128)S(1)}, f32[10,4,40,128]{3,2,1,0:T(8,128)S(1)}) custom-call(f32[18,10,32,128]{3,2,1,0:T(8,128)S(1)} %copy-done.1, f32[18,10,32,128]{3,2,1,0:T(8,128)S(1)} %copy-done.2, s32[10,32,16]{2,1,0:T(8,128)S(1)} %copy.16.mat, ...), custom_call_target="tpu_custom_call" | custom-call | tf_op jit(solution)/shard_map/pack/pallas_call | solution.py:119
  11.3 0.0 copy-start
  11.4 5.0 %collective-permute-start = (f32[10,2,40,128]{3,2,1,0:T(8,128)S(1)}, f32[10,2,40,128]{3,2,1,0:T(8,128)S(1)}, u32[]{:S(2)}, u32[]{:S(2)}) collective-permute-start(f32[10,2,40,128]{3,2,1,0:T(8,128)S(1)} %get-tuple-element.12), channel_id=1, source_target_pairs={{0,1},{1,2},{2,3},{4,5},{5,6},{6,7},{8,9},{9,10},{10,11},{12,13},{... | collective-permute-start | bytes 1228808 | tf_op jit(solution)/shard_map/ppermute | solution.py:550
  16.3 1.3 collective-permute-start.1
  17.6 7.4 %collective-permute-done.fl = f32[10,2,40,128]{3,2,1,0:T(8,128)S(1)} collective-permute-done((f32[10,2,40,128]{3,2,1,0:T(8,128)S(1)}, f32[10,2,40,128]{3,2,1,0:T(8,128)S(1)}, u32[]{:S(2)}, u32[]{:S(2)}) %collective-permute-start) | collective-permute-done | bytes 409632 | tf_op jit(solution)/shard_map/ppermute | solution.py:550
  25.0 0.0 copy-start.7
  25.0 4.1 %collective-permute-done.1.fr = f32[10,2,40,128]{3,2,1,0:T(8,128)S(1)} collective-permute-done((f32[10,2,40,128]{3,2,1,0:T(8,128)S(1)}, f32[10,2,40,128]{3,2,1,0:T(8,128)S(1)}, u32[]{:S(2)}, u32[]{:S(2)}) %collective-permute-start.1) | collective-permute-done | bytes 409632 | tf_op jit(solution)/shard_map/ppermute | solution.py:550
  29.1 0.0 copy-start.8
  29.1 0.7 copy-done.8
  29.9 0.1 slice_select_fusion
  29.9 0.0 copy-start.9
  29.9 0.0 copy-start.10
  30.0 0.0 copy-start.6
  30.0 0.1 slice.48
  30.1 0.1 maximum_maximum_fusion.1
  30.2 0.7 collective-permute-start.3
  31.0 0.1 slice.44
  31.1 0.1 maximum_maximum_fusion
  31.2 0.0 copy-done
  31.2 0.1 collective-permute-start.2
  31.3 0.0 copy-done.9
  31.3 0.6 copy.17.scatter
  31.9 0.0 copy-done.10
  31.9 0.6 copy.18.deriv
  32.6 0.0 copy-done.6
  32.6 3.0 %route.1 = (bf16[32,4096]{1,0:T(8,128)(2,1)S(1)}, bf16[256,4096]{1,0:T(8,128)(2,1)S(1)}, f32[32,256]{1,0:T(8,128)S(1)}) custom-call(s32[32,128]{1,0:T(8,128)S(1)} %copy-done.6), custom_call_target="tpu_custom_call" | custom-call | tf_op jit(solution)/shard_map/route/pallas_call | solution.py:473
  35.6 0.0 copy-start.3
  35.6 1.4 copy-done.3
  37.0 0.6 add_convert_fusion.flags
  37.6 15.9 %collective-permute-done.3.hr = f32[10,5,40,128]{3,2,1,0:T(8,128)} collective-permute-done((f32[10,5,40,128]{3,2,1,0:T(8,128)S(1)}, f32[10,5,40,128]{3,2,1,0:T(8,128)}, u32[]{:S(2)}, u32[]{:S(2)}) %collective-permute-start.3) | collective-permute-done | bytes 1024032 | tf_op jit(solution)/shard_map/ppermute | solution.py:550
  53.5 2.8 %collective-permute-done.2.hl = f32[10,5,40,128]{3,2,1,0:T(8,128)} collective-permute-done((f32[10,5,40,128]{3,2,1,0:T(8,128)S(1)}, f32[10,5,40,128]{3,2,1,0:T(8,128)}, u32[]{:S(2)}, u32[]{:S(2)}) %collective-permute-start.2) | collective-permute-done | bytes 1024032 | tf_op jit(solution)/shard_map/ppermute | solution.py:550
  56.3 0.0 copy-done.7
  56.3 79.2 %adjoint_steps.1 = (f32[18,10,32,128]{3,2,1,0:T(8,128)}, f32[32,128]{1,0:T(8,128)}) custom-call(s32[2]{0:T(128)} %add_convert_fusion.flags, f32[4,18,18]{2,1,0:T(8,128)} %copy.17.scatter, f32[4,18,18]{2,1,0:T(8,128)} %copy.18.deriv, f32[10,32,40,128]{3,2,1,0:T(8,128)} %copy-done, f32[10,2,40,128]{3,2,1,0:T(8,128)} %copy-done.7, ...), custom_call_target="tpu_custom_call" | custom-call | tf_op jit(solution)/shard_map/adjoint_steps/pallas_call | solution.py:415
  135.6 0.0 copy-start.4
  135.6 1.6 %copy-done.4 = bf16[256,4096]{1,0:T(8,128)(2,1)S(1)} copy-done((bf16[256,4096]{1,0:T(8,128)(2,1)S(1)}, bf16[256,4096]{1,0:T(8,128)(2,1)}, u32[]{:S(2)}) %copy-start.4) | copy-done | bytes 2097176
  137.1 0.0 copy-start.5
  137.1 0.7 copy-done.5
  137.9 0.8 send.1
  138.7 0.1 copy.19
  138.8 10.2 %all_to_all.11 = f32[32,1,512]{2,1,0:T(1,128)S(1)} all-to-all(f32[32,1,512]{2,1,0:T(1,128)S(1)} %copy.19), channel_id=1, replica_groups=mesh['gx'=8,'gy'=4] {'gx','gy'}, dimensions={0} | all-to-all | bytes 131072 | tf_op jit(solution)/shard_map/all_to_all | solution.py:574
  149.0 1.5 gather.1
  (2 shorter events, 0.0 us)
Async XLA Ops:
  2.5 1.8 %copy-start.1 = (f32[18,10,32,128]{3,2,1,0:T(8,128)S(1)}, f32[18,10,32,128]{3,2,1,0:T(8,128)}, u32[]{:S(2)}) copy-start(f32[18,10,32,128]{3,2,1,0:T(8,128)} %inc.1) | copy-start | bytes 8847364
  4.3 1.8 %copy-start.2 = (f32[18,10,32,128]{3,2,1,0:T(8,128)S(1)}, f32[18,10,32,128]{3,2,1,0:T(8,128)}, u32[]{:S(2)}) copy-start(f32[18,10,32,128]{3,2,1,0:T(8,128)} %cot.1) | copy-start | bytes 8847364
  11.3 19.9 %copy-start = (f32[10,32,40,128]{3,2,1,0:T(8,128)}, f32[10,32,40,128]{3,2,1,0:T(8,128)S(1)}, u32[]{:S(2)}) copy-start(f32[10,32,40,128]{3,2,1,0:T(8,128)S(1)} %get-tuple-element.11.pk) | copy-start | bytes 19660804
  11.4 13.6 %collective-permute-start = (f32[10,2,40,128]{3,2,1,0:T(8,128)S(1)}, f32[10,2,40,128]{3,2,1,0:T(8,128)S(1)}, u32[]{:S(2)}, u32[]{:S(2)}) collective-permute-start(f32[10,2,40,128]{3,2,1,0:T(8,128)S(1)} %get-tuple-element.12), channel_id=1, source_target_pairs={{0,1},{1,2},{2,3},{4,5},{5,6},{6,7},{8,9},{9,10},{10,11},{12,13},{... | collective-permute-start | bytes 1228808 | tf_op jit(solution)/shard_map/ppermute | solution.py:550
  16.3 12.8 %collective-permute-start.1 = (f32[10,2,40,128]{3,2,1,0:T(8,128)S(1)}, f32[10,2,40,128]{3,2,1,0:T(8,128)S(1)}, u32[]{:S(2)}, u32[]{:S(2)}) collective-permute-start(f32[10,2,40,128]{3,2,1,0:T(8,128)S(1)} %get-tuple-element.12), channel_id=1, source_target_pairs={{1,0},{2,1},{3,2},{5,4},{6,5},{7,6},{9,8},{10,9},{11,10},{13,12},{... | collective-permute-start | bytes 1228808 | tf_op jit(solution)/shard_map/ppermute | solution.py:550
  25.0 31.3 %copy-start.7 = (f32[10,2,40,128]{3,2,1,0:T(8,128)}, f32[10,2,40,128]{3,2,1,0:T(8,128)S(1)}, u32[]{:S(2)}) copy-start(f32[10,2,40,128]{3,2,1,0:T(8,128)S(1)} %collective-permute-done.fl) | copy-start | bytes 1228804
  29.1 0.7 copy-start.8
  29.9 1.4 copy-start.9
  29.9 2.0 %copy-start.10 = (f32[4,18,18]{2,0,1:T(4,128)S(1)}, f32[4,18,18]{2,0,1:T(4,128)}, u32[]{:S(2)}) copy-start(f32[4,18,18]{2,0,1:T(4,128)} %param.10) | copy-start | bytes 15556
  30.0 2.6 %copy-start.6 = (s32[32,128]{1,0:T(8,128)S(1)}, s32[32,128]{1,0:T(8,128)}, u32[]{:S(2)}) copy-start(s32[32,128]{1,0:T(8,128)} %ids.1) | copy-start | bytes 49156
  30.2 23.3 %collective-permute-start.3 = (f32[10,5,40,128]{3,2,1,0:T(8,128)S(1)}, f32[10,5,40,128]{3,2,1,0:T(8,128)}, u32[]{:S(2)}, u32[]{:S(2)}) collective-permute-start(f32[10,5,40,128]{3,2,1,0:T(8,128)S(1)} %maximum_maximum_fusion.1), channel_id=1, source_target_pairs={{0,28},{4,0},{8,4},{12,8},{16,12},{20,16},{24,20},{28,24},{1,29},{... | collective-permute-start | bytes 3072008 | tf_op jit(solution)/shard_map/ppermute | solution.py:550
  31.2 25.1 %collective-permute-start.2 = (f32[10,5,40,128]{3,2,1,0:T(8,128)S(1)}, f32[10,5,40,128]{3,2,1,0:T(8,128)}, u32[]{:S(2)}, u32[]{:S(2)}) collective-permute-start(f32[10,5,40,128]{3,2,1,0:T(8,128)S(1)} %maximum_maximum_fusion), channel_id=1, source_target_pairs={{0,4},{4,8},{8,12},{12,16},{16,20},{20,24},{24,28},{28,0},{1,5},{5... | collective-permute-start | bytes 3072008 | tf_op jit(solution)/shard_map/ppermute | solution.py:550
  35.6 1.4 copy-start.3
  135.6 1.6 %copy-start.4 = (bf16[256,4096]{1,0:T(8,128)(2,1)S(1)}, bf16[256,4096]{1,0:T(8,128)(2,1)}, u32[]{:S(2)}) copy-start(bf16[256,4096]{1,0:T(8,128)(2,1)} %copy-done.3) | copy-start | bytes 6291460
  137.1 0.7 copy-start.5

commit v2 on v1

--- a/solution.py
+++ b/solution.py
@@ -9,6 +9,7 @@
 
 BW = 8
 ITERS = 4
+CHUNK = 8
 HALO = 4
 SUB = 8
 LANES = 128
@@ -175,11 +176,12 @@
 def main_kernel(
     flags, scatter, deriv, pk, fl, fr, hl, hr,
     adjoint, column,
-    rf, ra, rtail, masks, saved_d, saved_r, xf, xa, tf, ta, acc, tables, ebuf, sems,
+    rf0, rf1, ra0, ra1, rtail, masks, saved_d, saved_r, xf, xa, tf, ta, acc, tables, ebuf, sems,
 ):
     cz, nx = pk.shape[0], pk.shape[1]
     ne = nx + 2 * HALO
-    nb = rf.shape[2] - ne
+    nb = rf0.shape[1] - ne
+    rf, ra = (rf0, rf1), (ra0, ra1)
     row = iota((SUB, LANES), 0)
     lane = iota((SUB, LANES), 1)
     is_first = flags[0] == 1
@@ -189,8 +191,8 @@
     for i, (source, first, count) in enumerate(((pk, HALO, nx), (hl, 0, HALO), (hr, HALO + nx, HALO))):
         src = source.at[:, pl.ds(0, count)]
         for j, (target, at, size) in enumerate(
-            ((rf.at[0, :, pl.ds(first, count), pl.ds(0, 16)], 0, 16),
-             (ra.at[0, :, pl.ds(first, count), pl.ds(0, 16)], 16, 16),
+            ((rf0.at[:, pl.ds(first, count), pl.ds(0, 16)], 0, 16),
+             (ra0.at[:, pl.ds(first, count), pl.ds(0, 16)], 16, 16),
              (rtail.at[:, pl.ds(first, count)], 32, 8))
         ):
             copies.append(pltpu.make_async_copy(src.at[:, :, pl.ds(at, size)], target, sems.at[3 * i + j]))
@@ -210,11 +212,11 @@
                 after = hr[z, HALO, part, :] if b == nb - 1 else blocks[b]
                 value = jnp.where(lane < 8 * HALO, before, after)
                 if i == 0 or i == 1:
-                    rf[0, z, ne + b, part, :] = value
+                    rf0[z, ne + b, part, :] = value
                 elif i == 2:
-                    ra[0, z, ne + b, pl.ds(0, 8), :] = shifted(value)
+                    ra0[z, ne + b, pl.ds(0, 8), :] = shifted(value)
                 elif i == 3:
-                    ra[0, z, ne + b, pl.ds(8, 8), :] = value
+                    ra0[z, ne + b, pl.ds(8, 8), :] = value
                 else:
                     rtail[z, ne + b] = value
         return 0
@@ -233,8 +235,8 @@
     def start_rows(r, _):
         for z in range(cz):
             t = rtail[z, r]
-            rf[0, z, r, pl.ds(16, 8), :] = repeated(t)
-            ra[0, z, r, pl.ds(16, 8), :] = repeated(roll(t, 6, 0))
+            rf0[z, r, pl.ds(16, 8), :] = repeated(t)
+            ra0[z, r, pl.ds(16, 8), :] = repeated(roll(t, 6, 0))
             code = jnp.broadcast_to(rtail[z, r, pl.ds(4, 1), :], (16, LANES))
             for m in range(4):
                 masks[z, r, pl.ds(16 * m, 16), :] = jnp.where(code == m, 1.0, 0.0).astype(BF16)
@@ -244,163 +246,200 @@
 
     lax.fori_loop(0, ne + nb, start_rows, 0)
 
-    def operand(values, z, r):
+    def operand(values, mask):
         v0, v1, v2 = values
         main = jnp.concatenate([v0, v1], axis=0)
         high = main.astype(BF16)
         low = (main - high.astype(F32)).astype(BF16)
         high2 = v2.astype(BF16).astype(F32)
         end = jnp.concatenate([high2, v2 - high2], axis=0).astype(BF16)
-        mask = [masks[z, r, pl.ds(16 * m, 16), :] for m in range(5)]
         pieces = [high * mask[m] for m in range(4)] + [low * mask[m] for m in range(4)]
         return jnp.concatenate(pieces + [end * mask[4]], axis=0)
 
-    def apply(table, values, r):
+    def mask_of(z, r):
+        return [masks[z, r, pl.ds(16 * m, 16), :] for m in range(5)]
+
+    def apply(table, values, mask):
+        rhs = jnp.concatenate([operand(values[h], mask[h]) for h in range(2)], axis=1)
+        y = jnp.dot(table, rhs, preferred_element_type=F32)
         outs = []
-        for z in range(0, cz, 2):
-            rhs = jnp.concatenate([operand(values[z], z, r), operand(values[z + 1], z + 1, r)], axis=1)
-            y = jnp.dot(table, rhs, preferred_element_type=F32)
-            for h in range(2):
-                part = y[:, h * LANES : (h + 1) * LANES]
-                outs.append([
-                    [part[at + 8 * i : at + 8 * i + 8] + part[at + ROWS + 8 * i : at + ROWS + 8 * i + 8] for i in range(3)]
-                    for at in range(0, table.shape[0], 2 * ROWS)
-                ])
+        for h in range(2):
+            part = y[:, h * LANES : (h + 1) * LANES]
+            outs.append([
+                [part[at + 8 * i : at + 8 * i + 8] + part[at + ROWS + 8 * i : at + ROWS + 8 * i + 8] for i in range(3)]
+                for at in range(0, table.shape[0], 2 * ROWS)
+            ])
         return outs
 
-    def read(ref, slot, r):
-        return [[ref[slot, z, r, pl.ds(8 * i, 8), :] for i in range(3)] for z in range(cz)]
-
-    def along_z(values, r):
-        low = jnp.broadcast_to(rtail[0, r, pl.ds(5, 1), :], (SUB, LANES))
-        high = jnp.broadcast_to(rtail[cz - 1, r, pl.ds(5, 1), :], (SUB, LANES))
-        outs = []
-        for z in range(cz):
-            own = values[z][1]
-            above = values[z + 1][1] if z + 1 < cz else high * roll(own, 6, 0)
-            below = values[z - 1][1] if z > 0 else low * roll(own, 2, 0)
-            outs.append(jnp.where(row < 2, above, jnp.where(row < 4, below, own)))
-        return outs
+    def load(ref, z, r, i):
+        return ref[z, r, pl.ds(8 * i, 8), :]
+
+    def read(ref, z, r):
+        return [load(ref, z, r, i) for i in range(3)]
+
+    def along_z(ref, z, r):
+        own = load(ref, z, r, 1)
+        if z + 1 < cz:
+            above = load(ref, z + 1, r, 1)
+        else:
+            above = jnp.broadcast_to(rtail[z, r, pl.ds(5, 1), :], (SUB, LANES)) * roll(own, 6, 0)
+        if z > 0:
+            below = load(ref, z - 1, r, 1)
+        else:
+            below = jnp.broadcast_to(rtail[z, r, pl.ds(5, 1), :], (SUB, LANES)) * roll(own, 2, 0)
+        return jnp.where(row < 2, above, jnp.where(row < 4, below, own))
 
     at_ends = ((row // 2 == 2) & (lane == LANES - 1)) | ((row // 2 == 3) & (lane == 0))
     at_edges = ((row // 2 == 2) & (lane % 8 == HALO - 1)) | ((row // 2 == 3) & (lane % 8 == HALO))
 
-    def connect_row(ref, slot, tm, e):
-        values = read(ref, slot, e)
-        planes = along_z(values, e)
+    def connect_row(ref, tm, z, e):
         amount = LANES - (8 * (e % GROUP) + HALO)
-        outs = []
-        for z in range(cz):
-            after = ref[slot, z, e + 1, pl.ds(0, 8), :]
-            before = ref[slot, z, e - 1, pl.ds(0, 8), :]
-            outer = roll(tm[z, e // GROUP], amount, 1)
-            own = jnp.where(at_ends, outer, values[z][0])
-            outs.append([jnp.where(row < 2, after, jnp.where(row < 4, before, own)), planes[z], values[z][2]])
-        return outs
-
-    def connect_edge(ref, slot, x, tm, b):
-        r = ne + b
-        values = read(ref, slot, r)
-        planes = along_z(values, r)
-        outs = []
-        for z in range(cz):
-            own = values[z][0]
-            nxt = ref[slot, z, ne + (b + 1) % nb, pl.ds(0, 8), :]
-            prv = ref[slot, z, ne + (b + nb - 1) % nb, pl.ds(0, 8), :]
-            after = roll(jnp.where(lane >= 8, own, nxt), LANES - 8, 1)
-            before = roll(jnp.where(lane < LANES - 8, own, prv), 8, 1)
-            inner = x[z, b]
-            top = roll(roll(inner, LANES - 1, 1), 6, 0)
-            bottom = roll(roll(inner, 1, 1), 2, 0)
-            tm[z, b] = jnp.where(
-                is_last & (row < 6), -top, jnp.where(is_first & (row >= 6), -bottom, own)
-            )
-            own = jnp.where(at_edges, inner, own)
-            outs.append([jnp.where(row < 2, after, jnp.where(row < 4, before, own)), planes[z], values[z][2]])
-        return outs
-
-    def collect(x, e, blocks):
+        outer = roll(tm[z, e // GROUP], amount, 1)
+        own = jnp.where(at_ends, outer, load(ref, z, e, 0))
+        first = jnp.where(row < 2, load(ref, z, e + 1, 0), jnp.where(row < 4, load(ref, z, e - 1, 0), own))
+        return [first, along_z(ref, z, e), load(ref, z, e, 2)]
+
+    def connect_edge(ref, x, tm, z, b):
+        own = load(ref, z, ne + b, 0)
+        nxt = load(ref, z, ne + (b + 1) % nb, 0)
+        prv = load(ref, z, ne + (b + nb - 1) % nb, 0)
+        after = roll(jnp.where(lane >= 8, own, nxt), LANES - 8, 1)
+        before = roll(jnp.where(lane < LANES - 8, own, prv), 8, 1)
+        inner = x[z, b]
+        top = roll(roll(inner, LANES - 1, 1), 6, 0)
+        bottom = roll(roll(inner, 1, 1), 2, 0)
+        tm[z, b] = jnp.where(is_last & (row < 6), -top, jnp.where(is_first & (row >= 6), -bottom, own))
+        own = jnp.where(at_edges, inner, own)
+        first = jnp.where(row < 2, after, jnp.where(row < 4, before, own))
+        return [first, along_z(ref, z, ne + b), load(ref, z, ne + b, 2)]
+
+    def collect(x, z, e, block):
         g = e % GROUP
-        for z in range(cz):
-            moved = roll(blocks[z], 8 * g + HALO, 1)
-            x[z, e // GROUP] = jnp.where(lane // 8 == g, moved, x[z, e // GROUP])
-
-    def write(ref, slot, r, z, part):
+        moved = roll(block, 8 * g + HALO, 1)
+        x[z, e // GROUP] = jnp.where(lane // 8 == g, moved, x[z, e // GROUP])
+
+    def write(ref, z, r, part):
         first = shifted(part[0])
-        ref[slot, z, r, pl.ds(0, 8), :] = first
-        ref[slot, z, r, pl.ds(8, 8), :] = part[1]
-        ref[slot, z, r, pl.ds(16, 8), :] = part[2]
+        ref[z, r, pl.ds(0, 8), :] = first
+        ref[z, r, pl.ds(8, 8), :] = part[1]
+        ref[z, r, pl.ds(16, 8), :] = part[2]
         return first
 
     for x in (xf, xa):
         x[...] = jnp.zeros_like(x)
 
     def gather_first(e, _):
-        collect(xa, e, [ra[0, z, e, pl.ds(0, 8), :] for z in range(cz)])
+        for z in range(cz):
+            collect(xa, z, e, ra0[z, e, pl.ds(0, 8), :])
         return 0
 
-    lax.fori_loop(0, ne, gather_first, 0)
+    lax.fori_loop(0, ne, gather_first, 0, unroll=2)
     flat = adjoint.reshape(adjoint.shape[0] * cz * nx, LANES)
 
-    def product(e, left, right):
-        total = acc[e]
-        for z in range(cz):
-            for i in range(3):
-                total = total + left[z][i] * right(z, i)
-        acc[e] = total
+    def in_pairs(before, after):
+        pending = None
+        for z in range(0, cz, 2):
+            made = before(z)
+            if pending is not None:
+                after(*pending)
+            pending = (z, made)
+        after(*pending)
 
     for step in range(ITERS):
-        slot, other = step % 2, (step + 1) % 2
+        fa, ta_, fb, tb = rf[step % 2], ra[step % 2], rf[(step + 1) % 2], ra[(step + 1) % 2]
         last = step == ITERS - 1
+        a_table = tables[pl.ds((6 if last else 4) * ROWS, 2 * ROWS), :].astype(BF16)
+        if last:
+            f_table = tables[pl.ds(2 * ROWS, 2 * ROWS), :].astype(BF16)
+        else:
+            f_table = tables[pl.ds(0, 4 * ROWS), :].astype(BF16)
         s_table = tables[pl.ds(0, 2 * ROWS), :].astype(BF16)
-        sd_table = tables[pl.ds(0, 4 * ROWS), :].astype(BF16)
-        d_table = tables[pl.ds(2 * ROWS, 2 * ROWS), :].astype(BF16)
-        a_table = tables[pl.ds((6 if last else 4) * ROWS, 2 * ROWS), :].astype(BF16)
-
-        def edges(b, _, step=step, slot=slot, other=other, last=last, s_table=s_table, a_table=a_table):
-            av = connect_edge(ra, slot, xa, ta, b)
-            fv = connect_edge(rf, slot, xf, tf, b) if step > 0 else read(rf, slot, ne + b)
-            if not last:
-                for z, parts in enumerate(apply(a_table, av, ne + b)):
-                    write(ra, other, ne + b, z, parts[0])
-                for z, parts in enumerate(apply(s_table, fv, ne + b)):
-                    write(rf, other, ne + b, z, parts[0])
+
+        for b in range(nb):
+            def before(z, b=b):
+                av = [connect_edge(ta_, xa, ta, z + h, b) for h in range(2)]
+                if step > 0:
+                    fv = [connect_edge(fa, xf, tf, z + h, b) for h in range(2)]
+                else:
+                    fv = [read(fa, z + h, ne + b) for h in range(2)]
+                if last:
+                    return None
+                mask = [mask_of(z + h, ne + b) for h in range(2)]
+                return apply(a_table, av, mask), apply(s_table, fv, mask)
+
+            def after(z, made, b=b):
+                if last:
+                    return
+                for h in range(2):
+                    write(tb, z + h, ne + b, made[0][h][0])
+                    write(fb, z + h, ne + b, made[1][h][0])
+
+            in_pairs(before, after)
+
+        def rows(e, _):
+            total = []
+
+            def before(z):
+                mask = [mask_of(z + h, e) for h in range(2)]
+                av = [connect_row(ta_, ta, z + h, e) for h in range(2)]
+                a_out = apply(a_table, av, mask)
+                if step < 2:
+                    for h in range(2):
+                        for i in range(3):
+                            saved_r[step, z + h, e, pl.ds(8 * i, 8), :] = av[h][i]
+                else:
+                    for h in range(2):
+                        for i in range(3):
+                            total.append(av[h][i] * load(saved_d.at[ITERS - 1 - step], z + h, e, i))
+                if step > 0:
+                    fv = [connect_row(fa, tf, z + h, e) for h in range(2)]
+                else:
+                    fv = [read(fa, z + h, e) for h in range(2)]
+                return a_out, apply(f_table, fv, mask)
+
+            def after(z, made):
+                a_out, f_out = made
+                for h in range(2):
+                    part = a_out[h][0]
+                    if last:
+                        at = (z + h) * nx + e - HALO
+                        flat[pl.ds(at, 8, stride=cz * nx), :] = part[0]
+                        flat[pl.ds(8 * cz * nx + at, 8, stride=cz * nx), :] = part[1]
+                        flat[pl.ds(16 * cz * nx + at, 1), :] = part[2][0:1]
+                        flat[pl.ds(17 * cz * nx + at, 1), :] = part[2][1:2]
+                        change = f_out[h][0]
+                    else:
+                        collect(xa, z + h, e, write(tb, z + h, e, part))
+                        collect(xf, z + h, e, write(fb, z + h, e, f_out[h][0]))
+                        change = f_out[h][1]
+                    for i in range(3):
+                        if step < 2:
+                            saved_d[step, z + h, e, pl.ds(8 * i, 8), :] = change[i]
+                        else:
+                            total.append(change[i] * load(saved_r.at[ITERS - 1 - step], z + h, e, i))
+                if total:
+                    value = functools.reduce(lambda p, q: p + q, total)
+                    del total[:]
+                    total.append(value)
+
+            in_pairs(before, after)
+            if step == 2:
+                acc[e] = total[0]
+            elif step > 2:
+                acc[e] = acc[e] + total[0]
             return 0
 
-        lax.fori_loop(0, nb, edges, 0)
-
-        def rows(e, _, step=step, slot=slot, other=other, last=last, sd_table=sd_table, d_table=d_table, a_table=a_table):
-            av = connect_row(ra, slot, ta, e)
-            fv = connect_row(rf, slot, tf, e) if step > 0 else read(rf, slot, e)
-            a_out = apply(a_table, av, e)
-            if last:
-                for z in range(cz):
-                    part = a_out[z][0]
-                    at = z * nx + e - HALO
-                    flat[pl.ds(at, 8, stride=cz * nx), :] = part[0]
-                    flat[pl.ds(8 * cz * nx + at, 8, stride=cz * nx), :] = part[1]
-                    flat[pl.ds(16 * cz * nx + at, 1), :] = part[2][0:1]
-                    flat[pl.ds(17 * cz * nx + at, 1), :] = part[2][1:2]
-                change = [parts[0] for parts in apply(d_table, fv, e)]
-            else:
-                collect(xa, e, [write(ra, other, e, z, a_out[z][0]) for z in range(cz)])
-                f_out = apply(sd_table, fv, e)
-                collect(xf, e, [write(rf, other, e, z, f_out[z][0]) for z in range(cz)])
-                change = [parts[1] for parts in f_out]
-            if step < 2:
-                for z in range(cz):
-                    for i in range(3):
-                        saved_r[step, z, e, pl.ds(8 * i, 8), :] = av[z][i]
-                        saved_d[step, z, e, pl.ds(8 * i, 8), :] = change[z][i]
-            else:
-                k = ITERS - 1 - step
-                product(e, av, lambda z, i: saved_d[k, z, e, pl.ds(8 * i, 8), :])
-                product(e, change, lambda z, i: saved_r[k, z, e, pl.ds(8 * i, 8), :])
+        first, end = 1 + step, ne - 1 - step
+        spare = (end - first) % CHUNK
+        for e in range(first, first + spare):
+            rows(e, 0)
+
+        def chunk(c, _):
+            for i in range(CHUNK):
+                rows(first + spare + c * CHUNK + i, 0)
             return 0
 
-        if step == 0:
-            acc[...] = jnp.zeros_like(acc)
-        lax.fori_loop(1 + step, ne - 1 - step, rows, 0)
+        lax.fori_loop(0, (end - first) // CHUNK, chunk, 0)
 
     for x in range(nx):
         column[pl.ds(x, 1), :] = jnp.sum(acc[HALO + x], axis=0, keepdims=True) * sens_scale
@@ -421,8 +460,10 @@
             jax.ShapeDtypeStruct((nx, LANES), F32),
         ],
         scratch_shapes=[
-            pltpu.VMEM((2, cz, total, ROWS, LANES), F32),
-            pltpu.VMEM((2, cz, total, ROWS, LANES), F32),
+            pltpu.VMEM((cz, total, ROWS, LANES), F32),
+            pltpu.VMEM((cz, total, ROWS, LANES), F32),
+            pltpu.VMEM((cz, total, ROWS, LANES), F32),
+            pltpu.VMEM((cz, total, ROWS, LANES), F32),
             pltpu.VMEM((cz, total, SUB, LANES), F32),
             pltpu.VMEM((cz, total, 80, LANES), BF16),
             pltpu.VMEM((2, cz, ne, ROWS, LANES), F32),

time: 151 us -> 111 us (0.74)
  Pallas kernels: 89.7 us -> 49.8 us
    pallas_call x1, Pallas kernels: 79.2 us -> 39.3 us  [main_call(): pl.pallas_call(main_kernel, in_specs=[SMEM, VMEM, VMEM, ANY, VMEM, VMEM,...]
  transfers between devices with their start and end apart: 4 -> 4, of which waited for: 4 -> 4; matrix products, arithmetic and copies ran while one was open for 1% -> 2% of each run, Pallas kernels for 2% -> 3%
where the time goes in v2:
time: 111 us
  Pallas kernels  49.8 us (45%)
  waiting for transfers between devices  30.2 us (27%)
  local copies, waits for them, and re-layouts  11.5 us (10%)
  blocking collectives  10.2 us (9%)
  starting transfers between devices  7.05 us (6%)
    pallas_call x1, Pallas kernels, main_call(): pl.pallas_call(main_kernel, in_specs=[SMEM, VMEM, VMEM, ANY, VMEM, VMEM,...  39.3 us
    ppermute x4, waiting for transfers between devices, moved(): return lax.ppermute(block, axis, pairs)  30.2 us
    unnamed x28, local copies, waits for them, and re-layouts  10.5 us
    all_to_all x1, blocking collectives, shards(): received = lax.all_to_all(message, ('gx', 'gy'), 0, 0, tiled=True)  10.2 us
    ppermute x4, starting transfers between devices, moved(): return lax.ppermute(block, axis, pairs)  7.05 us
    pallas_call x1, Pallas kernels, pack(): pl.pallas_call(pack_kernel, grid=(cz,), in_specs=[field, field, codes, en...  5.17 us
    pallas_call x1, Pallas kernels, route(): pl.pallas_call(route_kernel, in_specs=[VMEM], out_specs=[VMEM] * 3, out_s...  3.01 us
  transfers between devices with their start and end apart: 4, of which 4 were waited for; matrix products, arithmetic and copies ran while one was open for 2% of the time, Pallas kernels for 3%

profile of v2, /device:TPU:0, one launch (start us, length us, event | category | flops | bytes accessed | tf_op | source)
XLA Modules:
  0.0 110.6 jit_solution(13921212865866409638)
XLA Ops:
  0.6 0.7 fusion.1
  1.3 0.1 copy.21.low
  1.4 0.1 copy.22.high
  1.5 1.0 copy.16.mat
  2.5 0.0 copy-start.1
  2.5 1.8 %copy-done.1 = f32[18,10,32,128]{3,2,1,0:T(8,128)S(1)} copy-done((f32[18,10,32,128]{3,2,1,0:T(8,128)S(1)}, f32[18,10,32,128]{3,2,1,0:T(8,128)}, u32[]{:S(2)}) %copy-start.1) | copy-done | bytes 2949144
  4.3 0.0 copy-start.2
  4.3 1.8 %copy-done.2 = f32[18,10,32,128]{3,2,1,0:T(8,128)S(1)} copy-done((f32[18,10,32,128]{3,2,1,0:T(8,128)S(1)}, f32[18,10,32,128]{3,2,1,0:T(8,128)}, u32[]{:S(2)}) %copy-start.2) | copy-done | bytes 2949144
  6.2 5.2 %pack.1 = (f32[10,32,40,128]{3,2,1,0:T(8,128)S(1)}, f32[10,2,40,128]{3,2,1,0:T(8,128)S(1)}, f32[10,4,40,128]{3,2,1,0:T(8,128)S(1)}, f32[10,4,40,128]{3,2,1,0:T(8,128)S(1)}) custom-call(f32[18,10,32,128]{3,2,1,0:T(8,128)S(1)} %copy-done.1, f32[18,10,32,128]{3,2,1,0:T(8,128)S(1)} %copy-done.2, s32[10,32,16]{2,1,0:T(8,128)S(1)} %copy.16.mat, ...), custom_call_target="tpu_custom_call" | custom-call | tf_op jit(solution)/shard_map/pack/pallas_call | solution.py:120
  11.3 0.0 copy-start
  11.4 5.0 %collective-permute-start = (f32[10,2,40,128]{3,2,1,0:T(8,128)S(1)}, f32[10,2,40,128]{3,2,1,0:T(8,128)S(1)}, u32[]{:S(2)}, u32[]{:S(2)}) collective-permute-start(f32[10,2,40,128]{3,2,1,0:T(8,128)S(1)} %get-tuple-element.12), channel_id=1, source_target_pairs={{0,1},{1,2},{2,3},{4,5},{5,6},{6,7},{8,9},{9,10},{10,11},{12,13},{... | collective-permute-start | bytes 1228808 | tf_op jit(solution)/shard_map/ppermute | solution.py:591
  16.3 1.3 %collective-permute-start.1 = (f32[10,2,40,128]{3,2,1,0:T(8,128)S(1)}, f32[10,2,40,128]{3,2,1,0:T(8,128)S(1)}, u32[]{:S(2)}, u32[]{:S(2)}) collective-permute-start(f32[10,2,40,128]{3,2,1,0:T(8,128)S(1)} %get-tuple-element.12), channel_id=1, source_target_pairs={{1,0},{2,1},{3,2},{5,4},{6,5},{7,6},{9,8},{10,9},{11,10},{13,12},{... | collective-permute-start | bytes 1228808 | tf_op jit(solution)/shard_map/ppermute | solution.py:591
  17.6 7.4 %collective-permute-done.fl = f32[10,2,40,128]{3,2,1,0:T(8,128)S(1)} collective-permute-done((f32[10,2,40,128]{3,2,1,0:T(8,128)S(1)}, f32[10,2,40,128]{3,2,1,0:T(8,128)S(1)}, u32[]{:S(2)}, u32[]{:S(2)}) %collective-permute-start) | collective-permute-done | bytes 409632 | tf_op jit(solution)/shard_map/ppermute | solution.py:591
  25.0 0.0 copy-start.7
  25.0 4.1 %collective-permute-done.1.fr = f32[10,2,40,128]{3,2,1,0:T(8,128)S(1)} collective-permute-done((f32[10,2,40,128]{3,2,1,0:T(8,128)S(1)}, f32[10,2,40,128]{3,2,1,0:T(8,128)S(1)}, u32[]{:S(2)}, u32[]{:S(2)}) %collective-permute-start.1) | collective-permute-done | bytes 409632 | tf_op jit(solution)/shard_map/ppermute | solution.py:591
  29.1 0.0 copy-start.8
  29.1 0.7 copy-done.8
  29.9 0.1 slice_select_fusion
  29.9 0.0 copy-start.9
  29.9 0.0 copy-start.10
  30.0 0.0 copy-start.6
  30.0 0.1 slice.48
  30.1 0.1 maximum_maximum_fusion.1
  30.2 0.7 collective-permute-start.3
  31.0 0.1 slice.44
  31.1 0.1 maximum_maximum_fusion
  31.2 0.0 copy-done
  31.2 0.1 collective-permute-start.2
  31.3 0.0 copy-done.9
  31.3 0.6 copy.17.scatter
  31.9 0.0 copy-done.10
  31.9 0.6 copy.18.deriv
  32.6 0.0 copy-done.6
  32.6 3.0 %route.1 = (bf16[32,4096]{1,0:T(8,128)(2,1)S(1)}, bf16[256,4096]{1,0:T(8,128)(2,1)S(1)}, f32[32,256]{1,0:T(8,128)S(1)}) custom-call(s32[32,128]{1,0:T(8,128)S(1)} %copy-done.6), custom_call_target="tpu_custom_call" | custom-call | tf_op jit(solution)/shard_map/route/pallas_call | solution.py:514
  35.6 0.0 copy-start.3
  35.6 1.4 %copy-done.3 = bf16[256,4096]{1,0:T(8,128)(2,1)} copy-done((bf16[256,4096]{1,0:T(8,128)(2,1)}, bf16[256,4096]{1,0:T(8,128)(2,1)S(1)}, u32[]{:S(2)}) %copy-start.3) | copy-done | bytes 2097176
  37.0 0.6 add_convert_fusion.flags
  37.6 15.9 %collective-permute-done.3.hr = f32[10,5,40,128]{3,2,1,0:T(8,128)} collective-permute-done((f32[10,5,40,128]{3,2,1,0:T(8,128)S(1)}, f32[10,5,40,128]{3,2,1,0:T(8,128)}, u32[]{:S(2)}, u32[]{:S(2)}) %collective-permute-start.3) | collective-permute-done | bytes 1024032 | tf_op jit(solution)/shard_map/ppermute | solution.py:591
  53.5 2.8 %collective-permute-done.2.hl = f32[10,5,40,128]{3,2,1,0:T(8,128)} collective-permute-done((f32[10,5,40,128]{3,2,1,0:T(8,128)S(1)}, f32[10,5,40,128]{3,2,1,0:T(8,128)}, u32[]{:S(2)}, u32[]{:S(2)}) %collective-permute-start.2) | collective-permute-done | bytes 1024032 | tf_op jit(solution)/shard_map/ppermute | solution.py:591
  56.3 0.0 copy-done.7
  56.3 39.3 %adjoint_steps.1 = (f32[18,10,32,128]{3,2,1,0:T(8,128)}, f32[32,128]{1,0:T(8,128)}) custom-call(s32[2]{0:T(128)} %add_convert_fusion.flags, f32[4,18,18]{2,1,0:T(8,128)} %copy.17.scatter, f32[4,18,18]{2,1,0:T(8,128)} %copy.18.deriv, f32[10,32,40,128]{3,2,1,0:T(8,128)} %copy-done, f32[10,2,40,128]{3,2,1,0:T(8,128)} %copy-done.7, ...), custom_call_target="tpu_custom_call" | custom-call | tf_op jit(solution)/shard_map/adjoint_steps/pallas_call | solution.py:454
  95.6 0.0 copy-start.4
  95.6 1.6 %copy-done.4 = bf16[256,4096]{1,0:T(8,128)(2,1)S(1)} copy-done((bf16[256,4096]{1,0:T(8,128)(2,1)S(1)}, bf16[256,4096]{1,0:T(8,128)(2,1)}, u32[]{:S(2)}) %copy-start.4) | copy-done | bytes 2097176
  97.2 0.0 copy-start.5
  97.2 0.7 copy-done.5
  97.9 0.8 send.1
  98.7 0.1 copy.19
  98.9 10.2 %all_to_all.11 = f32[32,1,512]{2,1,0:T(1,128)S(1)} all-to-all(f32[32,1,512]{2,1,0:T(1,128)S(1)} %copy.19), channel_id=1, replica_groups=mesh['gx'=8,'gy'=4] {'gx','gy'}, dimensions={0} | all-to-all | bytes 131072 | tf_op jit(solution)/shard_map/all_to_all | solution.py:615
  109.1 1.5 %gather.1 = f32[32,128]{1,0:T(8,128)} custom-call(f32[32,512]{1,0:T(8,128)S(1)} %bitcast.10), custom_call_target="tpu_custom_call" | custom-call | tf_op jit(solution)/shard_map/gather/pallas_call | solution.py:578
  (2 shorter events, 0.0 us)
Async XLA Ops:
  2.5 1.8 %copy-start.1 = (f32[18,10,32,128]{3,2,1,0:T(8,128)S(1)}, f32[18,10,32,128]{3,2,1,0:T(8,128)}, u32[]{:S(2)}) copy-start(f32[18,10,32,128]{3,2,1,0:T(8,128)} %inc.1) | copy-start | bytes 8847364
  4.3 1.8 %copy-start.2 = (f32[18,10,32,128]{3,2,1,0:T(8,128)S(1)}, f32[18,10,32,128]{3,2,1,0:T(8,128)}, u32[]{:S(2)}) copy-start(f32[18,10,32,128]{3,2,1,0:T(8,128)} %cot.1) | copy-start | bytes 8847364
  11.3 19.9 %copy-start = (f32[10,32,40,128]{3,2,1,0:T(8,128)}, f32[10,32,40,128]{3,2,1,0:T(8,128)S(1)}, u32[]{:S(2)}) copy-start(f32[10,32,40,128]{3,2,1,0:T(8,128)S(1)} %get-tuple-element.11.pk) | copy-start | bytes 19660804
  11.4 13.6 %collective-permute-start = (f32[10,2,40,128]{3,2,1,0:T(8,128)S(1)}, f32[10,2,40,128]{3,2,1,0:T(8,128)S(1)}, u32[]{:S(2)}, u32[]{:S(2)}) collective-permute-start(f32[10,2,40,128]{3,2,1,0:T(8,128)S(1)} %get-tuple-element.12), channel_id=1, source_target_pairs={{0,1},{1,2},{2,3},{4,5},{5,6},{6,7},{8,9},{9,10},{10,11},{12,13},{... | collective-permute-start | bytes 1228808 | tf_op jit(solution)/shard_map/ppermute | solution.py:591
  16.3 12.8 %collective-permute-start.1 = (f32[10,2,40,128]{3,2,1,0:T(8,128)S(1)}, f32[10,2,40,128]{3,2,1,0:T(8,128)S(1)}, u32[]{:S(2)}, u32[]{:S(2)}) collective-permute-start(f32[10,2,40,128]{3,2,1,0:T(8,128)S(1)} %get-tuple-element.12), channel_id=1, source_target_pairs={{1,0},{2,1},{3,2},{5,4},{6,5},{7,6},{9,8},{10,9},{11,10},{13,12},{... | collective-permute-start | bytes 1228808 | tf_op jit(solution)/shard_map/ppermute | solution.py:591
  25.0 31.3 %copy-start.7 = (f32[10,2,40,128]{3,2,1,0:T(8,128)}, f32[10,2,40,128]{3,2,1,0:T(8,128)S(1)}, u32[]{:S(2)}) copy-start(f32[10,2,40,128]{3,2,1,0:T(8,128)S(1)} %collective-permute-done.fl) | copy-start | bytes 1228804
  29.1 0.7 copy-start.8
  29.9 1.4 %copy-start.9 = (f32[4,18,18]{2,0,1:T(4,128)S(1)}, f32[4,18,18]{2,0,1:T(4,128)}, u32[]{:S(2)}) copy-start(f32[4,18,18]{2,0,1:T(4,128)} %param.9) | copy-start | bytes 15556
  29.9 2.0 %copy-start.10 = (f32[4,18,18]{2,0,1:T(4,128)S(1)}, f32[4,18,18]{2,0,1:T(4,128)}, u32[]{:S(2)}) copy-start(f32[4,18,18]{2,0,1:T(4,128)} %param.10) | copy-start | bytes 15556
  30.0 2.6 %copy-start.6 = (s32[32,128]{1,0:T(8,128)S(1)}, s32[32,128]{1,0:T(8,128)}, u32[]{:S(2)}) copy-start(s32[32,128]{1,0:T(8,128)} %ids.1) | copy-start | bytes 49156
  30.2 23.3 %collective-permute-start.3 = (f32[10,5,40,128]{3,2,1,0:T(8,128)S(1)}, f32[10,5,40,128]{3,2,1,0:T(8,128)}, u32[]{:S(2)}, u32[]{:S(2)}) collective-permute-start(f32[10,5,40,128]{3,2,1,0:T(8,128)S(1)} %maximum_maximum_fusion.1), channel_id=1, source_target_pairs={{0,28},{4,0},{8,4},{12,8},{16,12},{20,16},{24,20},{28,24},{1,29},{... | collective-permute-start | bytes 3072008 | tf_op jit(solution)/shard_map/ppermute | solution.py:591
  31.2 25.1 %collective-permute-start.2 = (f32[10,5,40,128]{3,2,1,0:T(8,128)S(1)}, f32[10,5,40,128]{3,2,1,0:T(8,128)}, u32[]{:S(2)}, u32[]{:S(2)}) collective-permute-start(f32[10,5,40,128]{3,2,1,0:T(8,128)S(1)} %maximum_maximum_fusion), channel_id=1, source_target_pairs={{0,4},{4,8},{8,12},{12,16},{16,20},{20,24},{24,28},{28,0},{1,5},{5... | collective-permute-start | bytes 3072008 | tf_op jit(solution)/shard_map/ppermute | solution.py:591
  35.6 1.4 %copy-start.3 = (bf16[256,4096]{1,0:T(8,128)(2,1)}, bf16[256,4096]{1,0:T(8,128)(2,1)S(1)}, u32[]{:S(2)}) copy-start(bf16[256,4096]{1,0:T(8,128)(2,1)S(1)} %get-tuple-element.18.rank_hot) | copy-start | bytes 6291460
  95.6 1.6 %copy-start.4 = (bf16[256,4096]{1,0:T(8,128)(2,1)S(1)}, bf16[256,4096]{1,0:T(8,128)(2,1)}, u32[]{:S(2)}) copy-start(bf16[256,4096]{1,0:T(8,128)(2,1)} %copy-done.3) | copy-start | bytes 6291460
  97.2 0.7 copy-start.5

commit v3 on v2

--- a/solution.py
+++ b/solution.py
@@ -10,11 +10,13 @@
 BW = 8
 ITERS = 4
 CHUNK = 8
+PACK_VMEM = 60
 HALO = 4
 SUB = 8
 LANES = 128
 GROUP = LANES // (2 * HALO)
 MSG = 40
+DEEP = 3
 ROWS = 24
 KDIM = 144
 F32 = jnp.float32
@@ -51,81 +53,151 @@
     return jnp.where(row < 4, swap_pairs(block), block)
 
 
-def pack_kernel(inc, cot, mat, low, high, pk, es, xl, xr):
+def near_lanes(first):
+    lane = iota((SUB, LANES), 1)
+    x = jnp.clip(first + lane // (2 * HALO), 0, LANES // HALO - 1)
+    c = lane % HALO
+    return HALO * x + c, HALO * ((x + 1) % (LANES // HALO)) + c
+
+
+def pick(below, above, lanes):
+    lane = iota((SUB, LANES), 1)
+    below = jnp.take_along_axis(below, lanes[0], axis=1)
+    above = jnp.take_along_axis(above, lanes[1], axis=1)
+    return jnp.where(lane % (2 * HALO) < HALO, below, above)
+
+
+def pack_kernel(inc, cot, mat, ends, pk, up, down, xl, xr):
     z = pl.program_id(0)
     cz = pl.num_programs(0)
     nx = inc.shape[2]
     lane = iota((SUB, LANES), 1)
     row = iota((SUB, LANES), 0)
-    spread = (iota((mat.shape[2], LANES), 1) // BW == iota((mat.shape[2], LANES), 0)).astype(BF16)
+    width = mat.shape[1]
+    spread = (iota((width, LANES), 1) // BW == iota((width, LANES), 0)).astype(F32).astype(BF16)
 
     def expand(codes):
-        return jnp.dot(codes.astype(F32).astype(BF16), spread, preferred_element_type=F32)
+        dims = (((0,), (0,)), ((), ()))
+        return lax.dot_general(codes.astype(F32).astype(BF16), spread, dims, preferred_element_type=F32)
 
     def coefficient(codes):
         return jnp.where(codes == 0, -1.0, jnp.where(codes == 1, 1.0, 0.0))
 
     code = expand(mat[0])
-    lower = expand(coefficient(low[0]))
-    upper = expand(coefficient(high[0]))
-    ends = jnp.where(z == 0, lower, jnp.where(z == cz - 1, upper, 0.0))
+    lower = expand(coefficient(ends[0]))
+    upper = expand(coefficient(ends[1]))
+    end = jnp.where(z == 0, lower, jnp.where(z == cz - 1, upper, 0.0))
     flat_inc = inc.reshape(inc.shape[0] * nx, LANES)
     flat_cot = cot.reshape(cot.shape[0] * nx, LANES)
-    for half in range(nx // GROUP):
-        edge = [jnp.zeros((SUB, LANES), F32) for _ in range(5)]
-        for g in range(GROUP):
-            x = half * GROUP + g
-            f0 = flat_inc[pl.ds(x, 8, stride=nx), :]
-            f1 = flat_inc[pl.ds(8 * nx + x, 8, stride=nx), :]
-            a0 = swap_pairs(flat_cot[pl.ds(x, 8, stride=nx), :])
-            a1 = swap_first(flat_cot[pl.ds(8 * nx + x, 8, stride=nx), :])
-            last = [
-                flat_inc[pl.ds(16 * nx + x, 1), :],
-                flat_inc[pl.ds(17 * nx + x, 1), :],
-                flat_cot[pl.ds(16 * nx + x, 1), :],
-                flat_cot[pl.ds(17 * nx + x, 1), :],
-                code[x : x + 1],
-                ends[x : x + 1],
-            ]
-            tail = jnp.zeros((SUB, LANES), F32)
-            for i, value in enumerate(last):
-                tail = jnp.where(row == i, jnp.broadcast_to(value, (SUB, LANES)), tail)
-            mine = lane // (2 * HALO) == g
-            for i, value in enumerate((f0, f1, a0, a1, tail)):
-                edge[i] = jnp.where(mine, roll(value, 2 * HALO * g + HALO, 1), edge[i])
-            for i, value in enumerate((f0, f1, shifted(a0), a1, tail)):
-                pk[0, x, pl.ds(8 * i, 8), :] = value
-                if x < HALO:
-                    xl[0, x, pl.ds(8 * i, 8), :] = value
-                if x >= nx - HALO:
-                    xr[0, x - nx + HALO, pl.ds(8 * i, 8), :] = value
-        for i in range(5):
-            es[0, half, pl.ds(8 * i, 8), :] = edge[i]
-
-
-def pack(incident, cotangent, material, lower, upper):
+    to_up = [jnp.zeros((SUB, LANES), F32) for _ in range(5)]
+    to_down = [jnp.zeros((SUB, LANES), F32) for _ in range(5)]
+    firsts = {}
+    for x in range(nx):
+        f0 = flat_inc[pl.ds(x, 8, stride=nx), :]
+        f1 = flat_inc[pl.ds(8 * nx + x, 8, stride=nx), :]
+        a0 = swap_pairs(flat_cot[pl.ds(x, 8, stride=nx), :])
+        a1 = swap_first(flat_cot[pl.ds(8 * nx + x, 8, stride=nx), :])
+        last = [
+            flat_inc[pl.ds(16 * nx + x, 1), :],
+            flat_inc[pl.ds(17 * nx + x, 1), :],
+            flat_cot[pl.ds(16 * nx + x, 1), :],
+            flat_cot[pl.ds(17 * nx + x, 1), :],
+            code[x : x + 1],
+            end[x : x + 1],
+        ]
+        tail = jnp.zeros((SUB, LANES), F32)
+        for i, value in enumerate(last):
+            tail = jnp.where(row == i, jnp.broadcast_to(value, (SUB, LANES)), tail)
+        group = lane // HALO
+        for i, value in enumerate((f0, f1, a0, a1, tail)):
+            turned = roll(value, (HALO * x + HALO) % LANES, 1) if x + 1 < nx else value
+            to_up[i] = jnp.where(group == x, turned, to_up[i])
+            to_down[i] = jnp.where(group == (x + 1) % nx, turned, to_down[i])
+        firsts[x] = a0
+        for i, value in enumerate((f0, f1, shifted(a0), a1, tail)):
+            pk[0, x, pl.ds(8 * i, 8), :] = value
+            if x < DEEP:
+                xl[0, pl.ds(MSG * x + 8 * i, 8), :] = value
+            if x >= nx - DEEP:
+                xr[0, pl.ds(MSG * (x - nx + DEEP) + 8 * i, 8), :] = value
+    xl[0, pl.ds(DEEP * MSG - 2, 2), :] = firsts[DEEP][0:2]
+    xr[0, pl.ds(MSG - 2, 2), :] = firsts[nx - DEEP - 1][2:4]
+    for i in range(5):
+        up[0, pl.ds(8 * i, 8), :] = to_up[i]
+        down[0, pl.ds(8 * i, 8), :] = to_down[i]
+
+
+def pack(incident, cotangent, material, ends):
     ports, cz, nx, ny = incident.shape
-    halves = nx // GROUP
     field = pl.BlockSpec((ports, 1, nx, ny), lambda z: (0, z, 0, 0))
-    codes = pl.BlockSpec((1, nx, material.shape[2]), lambda z: (z, 0, 0))
-    ends = pl.BlockSpec((1, nx, material.shape[2]), lambda z: (0, 0, 0))
-
-    def out(rows):
-        return pl.BlockSpec((1, rows, MSG, LANES), lambda z: (z, 0, 0, 0))
-
-    def shape(rows):
-        return jax.ShapeDtypeStruct((cz, rows, MSG, LANES), F32)
-
-    sizes = (nx, halves, HALO, HALO)
+    codes = pl.BlockSpec((1,) + material.shape[1:], lambda z: (z, 0, 0))
+    both = pl.BlockSpec(ends.shape, lambda z: (0, 0, 0))
+    edge = pl.BlockSpec((1, MSG, LANES), lambda z: (z, 0, 0))
+    deep = pl.BlockSpec((1, DEEP * MSG, LANES), lambda z: (z, 0, 0))
     return pl.pallas_call(
         pack_kernel,
         grid=(cz,),
-        in_specs=[field, field, codes, ends, ends],
-        out_specs=[out(n) for n in sizes],
-        out_shape=[shape(n) for n in sizes],
-        compiler_params=pltpu.CompilerParams(vmem_limit_bytes=24 * MIB),
+        in_specs=[field, field, codes, both],
+        out_specs=[pl.BlockSpec((1, nx, MSG, LANES), lambda z: (z, 0, 0, 0)), edge, edge, deep, deep],
+        out_shape=[
+            jax.ShapeDtypeStruct((cz, nx, MSG, LANES), F32),
+            jax.ShapeDtypeStruct((cz, MSG, LANES), F32),
+            jax.ShapeDtypeStruct((cz, MSG, LANES), F32),
+            jax.ShapeDtypeStruct((cz + 1, DEEP * MSG, LANES), F32),
+            jax.ShapeDtypeStruct((cz + 1, DEEP * MSG, LANES), F32),
+        ],
+        compiler_params=pltpu.CompilerParams(vmem_limit_bytes=PACK_VMEM * MIB),
         name="pack",
-    )(incident, cotangent, material, lower, upper)
+    )(incident, cotangent, material, ends)
+
+
+def corner_kernel(below, above, xl_in, xr_in, xl, xr, left, right, sems):
+    cz = below.shape[0]
+    nx = LANES // HALO
+    lane = iota((SUB, LANES), 1)
+    x = (lane % 32) // (2 * HALO)
+    c = lane % HALO
+
+    def lanes(first):
+        return HALO * (first + x) + c, HALO * ((first + x + 1) % nx) + c
+
+    low, high = lanes(0), lanes(nx - HALO)
+    for out, place in ((left, low), (right, high)):
+        for q in range(DEEP):
+            for i in range(5):
+                part = pl.ds(8 * i, 8)
+                value = jnp.zeros((SUB, LANES), F32)
+                for h in range(4):
+                    z = 4 * q + h
+                    if z < cz:
+                        value = jnp.where(lane // 32 == h, pick(below[z, part, :], above[z, part, :], place), value)
+                out[pl.ds(MSG * q + 8 * i, 8), :] = value
+    copies = [
+        pltpu.make_async_copy(left, xl.at[cz], sems.at[0]),
+        pltpu.make_async_copy(right, xr.at[cz], sems.at[1]),
+    ]
+    for copy in copies:
+        copy.start()
+    for copy in copies:
+        copy.wait()
+
+
+def corners(below, above, xl, xr):
+    shape = jax.ShapeDtypeStruct(xl.shape, F32)
+    return pl.pallas_call(
+        corner_kernel,
+        in_specs=[VMEM, VMEM, ANY, ANY],
+        out_specs=[ANY, ANY],
+        out_shape=[shape, shape],
+        input_output_aliases={2: 0, 3: 1},
+        scratch_shapes=[
+            pltpu.VMEM((DEEP * MSG, LANES), F32),
+            pltpu.VMEM((DEEP * MSG, LANES), F32),
+            pltpu.SemaphoreType.DMA((2,)),
+        ],
+        compiler_params=pltpu.CompilerParams(vmem_limit_bytes=16 * MIB),
+        name="corners",
+    )(below, above, xl, xr)
 
 
 def build_tables(scatter, deriv, tables):
@@ -176,7 +248,7 @@
 def main_kernel(
     flags, scatter, deriv, pk, fl, fr, hl, hr,
     adjoint, column,
-    rf0, rf1, ra0, ra1, rtail, masks, saved_d, saved_r, xf, xa, tf, ta, acc, tables, ebuf, sems,
+    rf0, rf1, ra0, ra1, rtail, masks, saved_d, saved_r, xf, xa, tf, ta, acc, tables, cbuf, sems,
 ):
     cz, nx = pk.shape[0], pk.shape[1]
     ne = nx + 2 * HALO
@@ -188,29 +260,41 @@
     is_last = flags[1] == 1
 
     copies = []
-    for i, (source, first, count) in enumerate(((pk, HALO, nx), (hl, 0, HALO), (hr, HALO + nx, HALO))):
-        src = source.at[:, pl.ds(0, count)]
-        for j, (target, at, size) in enumerate(
-            ((rf0.at[:, pl.ds(first, count), pl.ds(0, 16)], 0, 16),
-             (ra0.at[:, pl.ds(first, count), pl.ds(0, 16)], 16, 16),
-             (rtail.at[:, pl.ds(first, count)], 32, 8))
-        ):
-            copies.append(pltpu.make_async_copy(src.at[:, :, pl.ds(at, size)], target, sems.at[3 * i + j]))
+
+    def bring(source, target):
+        copies.append(pltpu.make_async_copy(source, target, sems.at[len(copies)]))
+
+    for buffer, at in ((rf0, 0), (ra0, 16)):
+        bring(pk.at[:, :, pl.ds(at, 16)], buffer.at[:, pl.ds(HALO, nx), pl.ds(0, 16)])
+    bring(pk.at[:, :, pl.ds(32, 8)], rtail.at[:, pl.ds(HALO, nx)])
+    for source, first in ((hl, HALO - DEEP), (hr, HALO + nx)):
+        for i in range(DEEP):
+            for buffer, at in ((rf0, 0), (ra0, 16)):
+                bring(source.at[pl.ds(0, cz), pl.ds(MSG * i + at, 16)], buffer.at[:, first + i, pl.ds(0, 16)])
+            bring(source.at[pl.ds(0, cz), pl.ds(MSG * i + 32, 8)], rtail.at[:, first + i])
+    for q in range(DEEP):
+        for i, source in enumerate((hl, hr)):
+            bring(source.at[cz, pl.ds(MSG * q, MSG)], cbuf.at[i, q])
     for copy in copies:
         copy.start()
     build_tables(scatter, deriv, tables)
+    for copy in copies:
+        copy.wait()
+
+    places = [near_lanes(GROUP * b - HALO) for b in range(nb)]
 
     def halo_blocks(z, _):
+        turn = LANES - 32 * (z % 4)
         for i in range(5):
             part = pl.ds(8 * i, 8)
-            blocks = [
-                roll(jnp.where(lane % 8 < HALO, fl[z, h, part, :], fr[z, h, part, :]), 8 * HALO, 1)
-                for h in range(nb - 1)
-            ]
             for b in range(nb):
-                before = hl[z, HALO, part, :] if b == 0 else blocks[b - 1]
-                after = hr[z, HALO, part, :] if b == nb - 1 else blocks[b]
-                value = jnp.where(lane < 8 * HALO, before, after)
+                value = pick(fl[z, part, :], fr[z, part, :], places[b])
+                if b == 0:
+                    outer = roll(cbuf[0, z // 4, part, :], turn % LANES, 1)
+                    value = jnp.where(lane < 8 * HALO, outer, value)
+                if b == nb - 1:
+                    outer = roll(cbuf[1, z // 4, part, :], (turn + 32) % LANES, 1)
+                    value = jnp.where(lane < 8 * HALO, value, outer)
                 if i == 0 or i == 1:
                     rf0[z, ne + b, part, :] = value
                 elif i == 2:
@@ -219,11 +303,11 @@
                     ra0[z, ne + b, pl.ds(8, 8), :] = value
                 else:
                     rtail[z, ne + b] = value
+        ra0[z, 0, pl.ds(0, 8), :] = roll(rtail[z, HALO - DEEP], 4, 0)
+        ra0[z, ne - 1, pl.ds(0, 8), :] = roll(rtail[z, ne - 1 - (HALO - DEEP)], 2, 0)
         return 0
 
-    lax.fori_loop(0, cz, halo_blocks, 0)
-    for copy in copies:
-        copy.wait()
+    lax.fori_loop(0, cz, halo_blocks, 0, unroll=2)
 
     def repeated(value):
         value = jnp.where(row < 2, value, 0.0)
@@ -231,8 +315,9 @@
         return value + roll(value, 4, 0)
 
     wide_row = iota((16, LANES), 0)
-
-    def start_rows(r, _):
+    own_code = ((wide_row % 8) // 2).astype(F32)
+
+    def start_row(r, _):
         for z in range(cz):
             t = rtail[z, r]
             rf0[z, r, pl.ds(16, 8), :] = repeated(t)
@@ -240,11 +325,12 @@
             code = jnp.broadcast_to(rtail[z, r, pl.ds(4, 1), :], (16, LANES))
             for m in range(4):
                 masks[z, r, pl.ds(16 * m, 16), :] = jnp.where(code == m, 1.0, 0.0).astype(BF16)
-            own = ((wide_row % 8) // 2).astype(F32)
-            masks[z, r, pl.ds(64, 16), :] = jnp.where(code == own, 1.0, 0.0).astype(BF16)
+            masks[z, r, pl.ds(64, 16), :] = jnp.where(code == own_code, 1.0, 0.0).astype(BF16)
         return 0
 
-    lax.fori_loop(0, ne + nb, start_rows, 0)
+    for b in range(nb):
+        start_row(ne + b, 0)
+    lax.fori_loop(0, ne // 4, lambda c, _: [start_row(4 * c + i, 0) for i in range(4)][0], 0)
 
     def operand(values, mask):
         v0, v1, v2 = values
@@ -333,7 +419,7 @@
             collect(xa, z, e, ra0[z, e, pl.ds(0, 8), :])
         return 0
 
-    lax.fori_loop(0, ne, gather_first, 0, unroll=2)
+    lax.fori_loop(0, ne // 4, lambda c, _: [gather_first(4 * c + i, 0) for i in range(4)][0], 0)
     flat = adjoint.reshape(adjoint.shape[0] * cz * nx, LANES)
 
     def in_pairs(before, after):
@@ -453,7 +539,7 @@
     total = ne + nb
     return pl.pallas_call(
         main_kernel,
-        in_specs=[SMEM, VMEM, VMEM, ANY, VMEM, VMEM, VMEM, VMEM],
+        in_specs=[SMEM, VMEM, VMEM, ANY, VMEM, VMEM, ANY, ANY],
         out_specs=[VMEM, VMEM],
         out_shape=[
             jax.ShapeDtypeStruct((ports, cz, nx, LANES), F32),
@@ -474,15 +560,15 @@
             pltpu.VMEM((cz, nb, SUB, LANES), F32),
             pltpu.VMEM((ne, SUB, LANES), F32),
             pltpu.VMEM((8 * ROWS, KDIM), F32),
-            pltpu.VMEM((SUB, LANES), F32),
-            pltpu.SemaphoreType.DMA((9,)),
+            pltpu.VMEM((2, DEEP, MSG, LANES), F32),
+            pltpu.SemaphoreType.DMA((3 + 8 * DEEP,)),
         ],
         compiler_params=pltpu.CompilerParams(vmem_limit_bytes=63 * MIB),
         name="adjoint_steps",
     )(flags, scatter, deriv, pk, fl, fr, hl, hr)
 
 
-def route_kernel(ids, owner_hot, rank_hot, id_slots):
+def route_kernel(ids, ranks, id_slots):
     nx = ids.shape[0]
     ndev, cap = id_slots.shape
     owned = nx * LANES
@@ -499,8 +585,7 @@
         ranked = (rank == place).astype(F32).astype(BF16)
         offset = offset + jnp.sum(hot, axis=1, keepdims=True)
         local = wanted % owned
-        owner_hot[:, pl.ds(x * LANES, LANES)] = hot.astype(BF16)
-        rank_hot[:, pl.ds(x * LANES, LANES)] = ranked
+        ranks[pl.ds(x, 1), :] = rank
         high = (hot * (local // 64).astype(F32)).astype(BF16)
         low = (hot * (local % 64).astype(F32)).astype(BF16)
         both = lax.dot_general(
@@ -510,14 +595,12 @@
 
 
 def route(ids, ndev, cap):
-    n = ids.shape[0] * ids.shape[1]
     return pl.pallas_call(
         route_kernel,
         in_specs=[VMEM],
-        out_specs=[VMEM] * 3,
+        out_specs=[VMEM] * 2,
         out_shape=[
-            jax.ShapeDtypeStruct((ndev, n), BF16),
-            jax.ShapeDtypeStruct((cap, n), BF16),
+            jax.ShapeDtypeStruct(ids.shape, jnp.int32),
             jax.ShapeDtypeStruct((ndev, cap), F32),
         ],
         compiler_params=pltpu.CompilerParams(vmem_limit_bytes=24 * MIB),
@@ -525,25 +608,27 @@
     )(ids)
 
 
-def send_kernel(column, owner_hot, rank_hot, id_slots, message):
+def send_kernel(column, ids, ranks, id_slots, message):
     nx = column.shape[0]
     ndev, cap = id_slots.shape
+    owned = nx * LANES
+    who = iota((ndev, LANES), 0)
+    place = iota((cap, LANES), 0)
     total = jnp.zeros((2 * ndev, cap), F32)
     for x in range(nx):
         value = jnp.broadcast_to(column[pl.ds(x, 1), :], (ndev, LANES))
-        high = value.astype(BF16)
-        low = (value - high.astype(F32)).astype(BF16)
-        part = pl.ds(x * LANES, LANES)
-        hot = owner_hot[:, part]
+        high = value.astype(BF16).astype(F32)
+        mine = ids[pl.ds(x, 1), :] // owned == who
+        left = jnp.concatenate([jnp.where(mine, high, 0.0), jnp.where(mine, value - high, 0.0)], axis=0)
+        ranked = (ranks[pl.ds(x, 1), :] == place).astype(F32).astype(BF16)
         total = total + lax.dot_general(
-            jnp.concatenate([high * hot, low * hot], axis=0), rank_hot[:, part],
-            (((1,), (1,)), ((), ())), preferred_element_type=F32,
+            left.astype(BF16), ranked, (((1,), (1,)), ((), ())), preferred_element_type=F32
         )
     message[:, pl.ds(0, cap)] = total[:ndev] + total[ndev:]
     message[:, pl.ds(cap, cap)] = id_slots[...]
 
 
-def send(column, owner_hot, rank_hot, id_slots):
+def send(column, ids, ranks, id_slots):
     ndev, cap = id_slots.shape
     return pl.pallas_call(
         send_kernel,
@@ -552,7 +637,7 @@
         out_shape=jax.ShapeDtypeStruct((ndev, 2 * cap), F32),
         compiler_params=pltpu.CompilerParams(vmem_limit_bytes=24 * MIB),
         name="send",
-    )(column, owner_hot, rank_hot, id_slots)
+    )(column, ids, ranks, id_slots)
 
 
 def gather_kernel(message, out):
@@ -597,21 +682,18 @@
     ndev = lax.axis_size("gx") * extent
     owned = param_ids.shape[0] * param_ids.shape[1]
     cap = 2 * owned // ndev
-    pk, es, xl, xr = pack(incident, cotangent, material_code, boundary_code[0:1], boundary_code[1:2])
-    fl = moved(es, "gy", 1, False)
-    fr = moved(es, "gy", -1, False)
-    owner_hot, rank_hot, id_slots = route(param_ids, ndev, cap)
-    near = (jnp.arange(LANES) % (2 * HALO) < HALO)[None, None, None]
-    low = jnp.where(near, fl[:, :1], fr[:, :1])
-    high = jnp.where(near, fl[:, -1:], fr[:, -1:])
-    place = 8 * HALO
-    low = jnp.roll(low, place, axis=3)
-    high = jnp.roll(high, place, axis=3)
-    hr = moved(jnp.concatenate([xl, low], axis=1), "gx", -1, True)
-    hl = moved(jnp.concatenate([xr, high], axis=1), "gx", 1, True)
+    pk, up, down, xl, xr = pack(
+        incident, cotangent, jnp.swapaxes(material_code, 1, 2), jnp.swapaxes(boundary_code, 1, 2)
+    )
+    fl = moved(up, "gy", 1, False)
+    fr = moved(down, "gy", -1, False)
+    ranks, id_slots = route(param_ids, ndev, cap)
+    xl, xr = corners(fl, fr, xl, xr)
+    hr = moved(xl, "gx", -1, True)
+    hl = moved(xr, "gx", 1, True)
     flags = jnp.stack([position == 0, position == extent - 1]).astype(jnp.int32)
     adjoint, column = main_call(flags, scatter_table, deriv_table, pk, fl, fr, hl, hr)
-    message = send(column, owner_hot, rank_hot, id_slots)
+    message = send(column, param_ids, ranks, id_slots)
     received = lax.all_to_all(message, ("gx", "gy"), 0, 0, tiled=True)
     sensitivity = gather(received, owned).reshape(-1)
     return adjoint, sensitivity

time: 111 us -> 97.8 us (0.88)
  waiting for transfers between devices: 30.2 us -> 16.9 us
  local copies, waits for them, and re-layouts: 11.5 us -> 2.07 us
  Pallas kernels: 49.8 us -> 55.4 us
  blocking collectives: 10.2 us -> 12.5 us
  starting transfers between devices: 7.05 us -> 8.92 us
    ppermute x4, waiting for transfers between devices: 30.2 us -> 16.9 us  [moved(): return lax.ppermute(block, axis, pairs)]
    unnamed x28 -> x15, local copies, waits for them, and re-layouts: 10.5 us -> 1.98 us
    pallas_call x2 -> x3, Pallas kernels: 8.19 us -> 14 us  [the longest x1 10.3 us: pack(): pl.pallas_call(pack_kernel, grid=(cz,), in_specs=[field, field, codes, bo...]
    all_to_all x1, blocking collectives: 10.2 us -> 12.5 us  [shards(): received = lax.all_to_all(message, ('gx', 'gy'), 0, 0, tiled=True)]
    ppermute x4, starting transfers between devices: 7.05 us -> 8.92 us  [moved(): return lax.ppermute(block, axis, pairs)]
  transfers between devices with their start and end apart: 4 -> 4, of which waited for: 4 -> 3; matrix products, arithmetic and copies ran while one was open for 2% -> 2% of each run, Pallas kernels for 3% -> 3%
where the time goes in v3:
time: 97.8 us; the launch traced here: 97.3 us
  Pallas kernels  55.4 us (57%)
  waiting for transfers between devices  16.9 us (17%)
  blocking collectives  12.5 us (13%)
  starting transfers between devices  8.92 us (9%)
  local copies, waits for them, and re-layouts  2.07 us (2%)
    pallas_call x1, Pallas kernels, main_call(): pl.pallas_call(main_kernel, in_specs=[SMEM, VMEM, VMEM, ANY, VMEM, VMEM,...  39.1 us
    ppermute x4, waiting for transfers between devices, moved(): return lax.ppermute(block, axis, pairs)  16.9 us
    all_to_all x1, blocking collectives, shards(): received = lax.all_to_all(message, ('gx', 'gy'), 0, 0, tiled=True)  12.5 us
    pallas_call x1, Pallas kernels, pack(): pl.pallas_call(pack_kernel, grid=(cz,), in_specs=[field, field, codes, bo...  10.3 us
    ppermute x4, starting transfers between devices, moved(): return lax.ppermute(block, axis, pairs)  8.92 us
    pallas_call x1, Pallas kernels, route(): pl.pallas_call(route_kernel, in_specs=[VMEM], out_specs=[VMEM] * 2, out_s...  2.63 us
    unnamed x15, local copies, waits for them, and re-layouts  1.98 us
  transfers between devices with their start and end apart: 4, of which 3 were waited for; matrix products, arithmetic and copies ran while one was open for 2% of the time, Pallas kernels for 3%

profile of v3, /device:TPU:0, one launch (start us, length us, event | category | flops | bytes accessed | tf_op | source)
XLA Modules:
  0.0 97.3 jit_solution(2326379733569943770)
XLA Ops:
  0.6 0.0 copy-start.4
  0.6 0.0 copy-start.5
  0.7 0.0 copy-start.2
  0.7 10.3 %pack.1 = (f32[10,32,40,128]{3,2,1,0:T(8,128)}, f32[10,40,128]{2,1,0:T(8,128)}, f32[10,40,128]{2,1,0:T(8,128)}, f32[11,120,128]{2,1,0:T(8,128)}, f32[11,120,128]{2,1,0:T(8,128)}) custom-call(f32[18,10,32,128]{3,2,1,0:T(8,128)} %inc.1, f32[18,10,32,128]{3,2,1,0:T(8,128)} %cot.1, s32[10,16,32]{2,1,0:T(8,128)} %bitcast.11, s32[2,16,32]{2,1,0:T(8,128)} %bitcast.12), custom_call_target="tpu_custom_call" | custom-call | tf_op jit(solution)/shard_map/pack/pallas_call | solution.py:137
  11.0 4.9 %collective-permute-start = (f32[10,40,128]{2,1,0:T(8,128)}, f32[10,40,128]{2,1,0:T(8,128)S(1)}, u32[]{:S(2)}, u32[]{:S(2)}) collective-permute-start(f32[10,40,128]{2,1,0:T(8,128)} %get-tuple-element.14), channel_id=1, source_target_pairs={{0,1},{1,2},{2,3},{4,5},{5,6},{6,7},{8,9},{9,10},{10,11},{12,13},{... | collective-permute-start | bytes 614408 | tf_op jit(solution)/shard_map/ppermute | solution.py:676
  16.0 1.3 %collective-permute-start.1 = (f32[10,40,128]{2,1,0:T(8,128)}, f32[10,40,128]{2,1,0:T(8,128)S(1)}, u32[]{:S(2)}, u32[]{:S(2)}) collective-permute-start(f32[10,40,128]{2,1,0:T(8,128)} %get-tuple-element.15), channel_id=1, source_target_pairs={{1,0},{2,1},{3,2},{5,4},{6,5},{7,6},{9,8},{10,9},{11,10},{13,12},{... | collective-permute-start | bytes 614408 | tf_op jit(solution)/shard_map/ppermute | solution.py:676
  17.3 3.3 %collective-permute-done.below.fl = f32[10,40,128]{2,1,0:T(8,128)S(1)} collective-permute-done((f32[10,40,128]{2,1,0:T(8,128)}, f32[10,40,128]{2,1,0:T(8,128)S(1)}, u32[]{:S(2)}, u32[]{:S(2)}) %collective-permute-start) | collective-permute-done | bytes 204832 | tf_op jit(solution)/shard_map/ppermute | solution.py:676
  20.6 0.0 copy-start
  20.6 4.0 %collective-permute-done.1.above.fr = f32[10,40,128]{2,1,0:T(8,128)S(1)} collective-permute-done((f32[10,40,128]{2,1,0:T(8,128)}, f32[10,40,128]{2,1,0:T(8,128)S(1)}, u32[]{:S(2)}, u32[]{:S(2)}) %collective-permute-start.1) | collective-permute-done | bytes 204832 | tf_op jit(solution)/shard_map/ppermute | solution.py:676
  24.6 0.0 copy-start.1
  24.6 1.0 %corners.1 = (f32[11,120,128]{2,1,0:T(8,128)}, f32[11,120,128]{2,1,0:T(8,128)}) custom-call(f32[10,40,128]{2,1,0:T(8,128)S(1)} %collective-permute-done.below.fl, f32[10,40,128]{2,1,0:T(8,128)S(1)} %collective-permute-done.1.above.fr, f32[11,120,128]{2,1,0:T(8,128)} %get-tuple-element.16.xl_in, ...), custom_call_target="tpu_custom_call", output_to_operand_aliasing={{0}: (2, {}), {1}: (3, {})} | custom-call | tf_op jit(solution)/shard_map/corners/pallas_call | solution.py:187
  25.7 0.1 collective-permute-start.2
  25.7 2.6 %collective-permute-start.3 = (f32[11,120,128]{2,1,0:T(8,128)}, f32[11,120,128]{2,1,0:T(8,128)}, u32[]{:S(2)}, u32[]{:S(2)}) collective-permute-start(f32[11,120,128]{2,1,0:T(8,128)} %get-tuple-element.19), channel_id=1, source_target_pairs={{0,28},{4,0},{8,4},{12,8},{16,12},{20,16},{24,20},{28,24},{1,29},{... | collective-permute-start | bytes 2027528 | tf_op jit(solution)/shard_map/ppermute | solution.py:676
  28.4 0.0 copy-done.4
  28.4 0.6 copy.13.scatter
  29.0 0.0 copy-done.5
  29.0 0.6 copy.14.deriv
  29.6 0.0 copy-done.2
  29.6 2.6 %route.1 = (s32[32,128]{1,0:T(8,128)S(1)}, f32[32,256]{1,0:T(8,128)S(1)}) custom-call(s32[32,128]{1,0:T(8,128)S(1)} %copy-done.2), custom_call_target="tpu_custom_call" | custom-call | tf_op jit(solution)/shard_map/route/pallas_call | solution.py:598
  32.2 0.7 add_convert_fusion.flags
  32.9 9.6 %collective-permute-done.2.hl = f32[11,120,128]{2,1,0:T(8,128)} collective-permute-done((f32[11,120,128]{2,1,0:T(8,128)}, f32[11,120,128]{2,1,0:T(8,128)}, u32[]{:S(2)}, u32[]{:S(2)}) %collective-permute-start.2) | collective-permute-done | bytes 675872 | tf_op jit(solution)/shard_map/ppermute | solution.py:676
  42.5 0.0 collective-permute-done.3.hr
  42.5 0.0 copy-done
  42.5 0.0 copy-done.1
  42.5 39.1 %adjoint_steps.1 = (f32[18,10,32,128]{3,2,1,0:T(8,128)}, f32[32,128]{1,0:T(8,128)}) custom-call(s32[2]{0:T(128)} %add_convert_fusion.flags, f32[4,18,18]{2,1,0:T(8,128)} %copy.13.scatter, f32[4,18,18]{2,1,0:T(8,128)} %copy.14.deriv, f32[10,32,40,128]{3,2,1,0:T(8,128)} %get-tuple-element.13.pk, f32[10,40,128]{2,1,0:T(8,128)} %copy-done, ...), custom_call_target="tpu_custom_call" | custom-call | tf_op jit(solution)/shard_map/adjoint_steps/pallas_call | solution.py:540
  81.6 0.0 copy-start.3
  81.6 0.7 copy-done.3
  82.4 0.8 send.1
  83.2 0.1 copy.15
  83.3 12.5 %all_to_all.11 = f32[32,1,512]{2,1,0:T(1,128)S(1)} all-to-all(f32[32,1,512]{2,1,0:T(1,128)S(1)} %copy.15), channel_id=1, replica_groups=mesh['gx'=8,'gy'=4] {'gx','gy'}, dimensions={0} | all-to-all | bytes 131072 | tf_op jit(solution)/shard_map/all_to_all | solution.py:697
  95.8 1.5 %gather.1 = f32[32,128]{1,0:T(8,128)} custom-call(f32[32,512]{1,0:T(8,128)S(1)} %bitcast.9), custom_call_target="tpu_custom_call" | custom-call | tf_op jit(solution)/shard_map/gather/pallas_call | solution.py:663
  (1 shorter events, 0.0 us)
Async XLA Ops:
  0.6 27.7 %copy-start.4 = (f32[4,18,18]{2,0,1:T(4,128)S(1)}, f32[4,18,18]{2,0,1:T(4,128)}, u32[]{:S(2)}) copy-start(f32[4,18,18]{2,0,1:T(4,128)} %param.9) | copy-start | bytes 15556
  0.6 28.3 %copy-start.5 = (f32[4,18,18]{2,0,1:T(4,128)S(1)}, f32[4,18,18]{2,0,1:T(4,128)}, u32[]{:S(2)}) copy-start(f32[4,18,18]{2,0,1:T(4,128)} %param.10) | copy-start | bytes 15556
  0.7 29.0 %copy-start.2 = (s32[32,128]{1,0:T(8,128)S(1)}, s32[32,128]{1,0:T(8,128)}, u32[]{:S(2)}) copy-start(s32[32,128]{1,0:T(8,128)} %ids.3) | copy-start | bytes 49156
  11.0 9.6 %collective-permute-start = (f32[10,40,128]{2,1,0:T(8,128)}, f32[10,40,128]{2,1,0:T(8,128)S(1)}, u32[]{:S(2)}, u32[]{:S(2)}) collective-permute-start(f32[10,40,128]{2,1,0:T(8,128)} %get-tuple-element.14), channel_id=1, source_target_pairs={{0,1},{1,2},{2,3},{4,5},{5,6},{6,7},{8,9},{9,10},{10,11},{12,13},{... | collective-permute-start | bytes 614408 | tf_op jit(solution)/shard_map/ppermute | solution.py:676
  16.0 8.6 %collective-permute-start.1 = (f32[10,40,128]{2,1,0:T(8,128)}, f32[10,40,128]{2,1,0:T(8,128)S(1)}, u32[]{:S(2)}, u32[]{:S(2)}) collective-permute-start(f32[10,40,128]{2,1,0:T(8,128)} %get-tuple-element.15), channel_id=1, source_target_pairs={{1,0},{2,1},{3,2},{5,4},{6,5},{7,6},{9,8},{10,9},{11,10},{13,12},{... | collective-permute-start | bytes 614408 | tf_op jit(solution)/shard_map/ppermute | solution.py:676
  20.6 21.9 %copy-start = (f32[10,40,128]{2,1,0:T(8,128)}, f32[10,40,128]{2,1,0:T(8,128)S(1)}, u32[]{:S(2)}) copy-start(f32[10,40,128]{2,1,0:T(8,128)S(1)} %collective-permute-done.below.fl) | copy-start | bytes 614404
  24.6 17.9 %copy-start.1 = (f32[10,40,128]{2,1,0:T(8,128)}, f32[10,40,128]{2,1,0:T(8,128)S(1)}, u32[]{:S(2)}) copy-start(f32[10,40,128]{2,1,0:T(8,128)S(1)} %collective-permute-done.1.above.fr) | copy-start | bytes 614404
  25.7 16.8 %collective-permute-start.2 = (f32[11,120,128]{2,1,0:T(8,128)}, f32[11,120,128]{2,1,0:T(8,128)}, u32[]{:S(2)}, u32[]{:S(2)}) collective-permute-start(f32[11,120,128]{2,1,0:T(8,128)} %get-tuple-element.18), channel_id=1, source_target_pairs={{0,4},{4,8},{8,12},{12,16},{16,20},{20,24},{24,28},{28,0},{1,5},{5... | collective-permute-start | bytes 2027528 | tf_op jit(solution)/shard_map/ppermute | solution.py:676
  25.7 16.8 %collective-permute-start.3 = (f32[11,120,128]{2,1,0:T(8,128)}, f32[11,120,128]{2,1,0:T(8,128)}, u32[]{:S(2)}, u32[]{:S(2)}) collective-permute-start(f32[11,120,128]{2,1,0:T(8,128)} %get-tuple-element.19), channel_id=1, source_target_pairs={{0,28},{4,0},{8,4},{12,8},{16,12},{20,16},{24,20},{28,24},{1,29},{... | collective-permute-start | bytes 2027528 | tf_op jit(solution)/shard_map/ppermute | solution.py:676
  81.6 0.7 copy-start.3

commit v4 on v3

--- a/solution.py
+++ b/solution.py
@@ -9,7 +9,7 @@
 
 BW = 8
 ITERS = 4
-CHUNK = 8
+CHUNK = 16
 PACK_VMEM = 60
 HALO = 4
 SUB = 8
@@ -245,10 +245,137 @@
         tables[pl.ds(ROWS * i, ROWS), :] = value.astype(F32)
 
 
+def repeated(value):
+    row = iota((SUB, LANES), 0)
+    value = jnp.where(row < 2, value, 0.0)
+    value = value + roll(value, 2, 0)
+    return value + roll(value, 4, 0)
+
+
+def masks_of(code):
+    code = jnp.broadcast_to(code, (16, LANES))
+    own = ((iota((16, LANES), 0) % 8) // 2).astype(F32)
+    return [jnp.where(code == m, 1.0, 0.0).astype(BF16) for m in (0, 1, 2, 3, own)]
+
+
+def collect(x, z, e, block):
+    lane = iota((SUB, LANES), 1)
+    g = e % GROUP
+    moved_block = roll(block, 8 * g + HALO, 1)
+    x[z, e // GROUP] = jnp.where(lane // 8 == g, moved_block, x[z, e // GROUP])
+
+
+def in_pairs(cz, before, after):
+    pending = None
+    for z in range(0, cz, 2):
+        made = before(z)
+        if pending is not None:
+            after(*pending)
+        pending = (z, made)
+    after(*pending)
+
+
+def operand(values, mask):
+    v0, v1, v2 = values
+    main = jnp.concatenate([v0, v1], axis=0)
+    high = main.astype(BF16)
+    low = (main - high.astype(F32)).astype(BF16)
+    high2 = v2.astype(BF16).astype(F32)
+    end = jnp.concatenate([high2, v2 - high2], axis=0).astype(BF16)
+    pieces = [high * mask[m] for m in range(4)] + [low * mask[m] for m in range(4)]
+    return jnp.concatenate(pieces + [end * mask[4]], axis=0)
+
+
+def apply(table, values, mask):
+    rhs = jnp.concatenate([operand(values[h], mask[h]) for h in range(2)], axis=1)
+    y = jnp.dot(table, rhs, preferred_element_type=F32)
+    outs = []
+    for h in range(2):
+        part = y[:, h * LANES : (h + 1) * LANES]
+        outs.append([
+            [part[at + 8 * i : at + 8 * i + 8] + part[at + ROWS + 8 * i : at + ROWS + 8 * i + 8] for i in range(3)]
+            for at in range(0, table.shape[0], 2 * ROWS)
+        ])
+    return outs
+
+
+def prep_kernel(scatter, deriv, pk, tables, masks, first, change, tails, xf, xa):
+    c = pl.program_id(0)
+    cz, rows = pk.shape[0], pk.shape[1]
+
+    @pl.when(c == 0)
+    def _():
+        build_tables(scatter, deriv, tables)
+        xf[...] = jnp.zeros_like(xf)
+        xa[...] = jnp.zeros_like(xa)
+
+    f_table = tables[pl.ds(0, 4 * ROWS), :].astype(BF16)
+    for x in range(rows):
+        e = c * rows + x + HALO
+
+        def before(z, x=x, e=e):
+            mask, values = [], []
+            for h in range(2):
+                t = pk[z + h, x, pl.ds(32, 8), :]
+                tails[z + h, x] = repeated(roll(t, 6, 0))
+                mask.append(masks_of(pk[z + h, x, pl.ds(36, 1), :]))
+                for m, value in enumerate(mask[h]):
+                    masks[z + h, x, pl.ds(16 * m, 16), :] = value
+                values.append([pk[z + h, x, pl.ds(0, 8), :], pk[z + h, x, pl.ds(8, 8), :], repeated(t)])
+                collect(xa, z + h, e, pk[z + h, x, pl.ds(16, 8), :])
+            return apply(f_table, values, mask)
+
+        def after(z, made, x=x, e=e):
+            for h in range(2):
+                part, other = made[h]
+                outer = shifted(part[0])
+                collect(xf, z + h, e, outer)
+                for i, value in enumerate((outer, part[1], part[2])):
+                    first[z + h, x, pl.ds(8 * i, 8), :] = value
+                for i, value in enumerate(other):
+                    change[z + h, x, pl.ds(8 * i, 8), :] = value
+
+        in_pairs(cz, before, after)
+
+
+def prep(scatter, deriv, pk):
+    cz, nx = pk.shape[0], pk.shape[1]
+    rows = 8
+    nb = (nx + 2 * HALO) // GROUP + 1
+
+    def by_rows(depth):
+        return pl.BlockSpec((cz, rows, depth, LANES), lambda c: (0, c, 0, 0))
+
+    table = pl.BlockSpec(scatter.shape, lambda c: (0, 0, 0))
+    edge = pl.BlockSpec((cz, nb, SUB, LANES), lambda c: (0, 0, 0, 0))
+    edges = jax.ShapeDtypeStruct((cz, nb, SUB, LANES), F32)
+    return pl.pallas_call(
+        prep_kernel,
+        grid=(nx // rows,),
+        in_specs=[table, table, by_rows(MSG)],
+        out_specs=[
+            pl.BlockSpec((8 * ROWS, KDIM), lambda c: (0, 0)),
+            by_rows(80), by_rows(ROWS), by_rows(ROWS), by_rows(SUB), edge, edge,
+        ],
+        out_shape=[
+            jax.ShapeDtypeStruct((8 * ROWS, KDIM), F32),
+            jax.ShapeDtypeStruct((cz, nx, 80, LANES), BF16),
+            jax.ShapeDtypeStruct((cz, nx, ROWS, LANES), F32),
+            jax.ShapeDtypeStruct((cz, nx, ROWS, LANES), F32),
+            jax.ShapeDtypeStruct((cz, nx, SUB, LANES), F32),
+            edges,
+            edges,
+        ],
+        compiler_params=pltpu.CompilerParams(vmem_limit_bytes=PACK_VMEM * MIB),
+        cost_estimate=pl.CostEstimate(flops=2 * 10**9, bytes_accessed=24 * 10**6, transcendentals=0),
+        name="prep",
+    )(scatter, deriv, pk)
+
+
 def main_kernel(
-    flags, scatter, deriv, pk, fl, fr, hl, hr,
+    flags, tables, xf_in, xa_in, pk, own_masks, first_in, change_in, tails_in, fl, fr, hl, hr,
     adjoint, column,
-    rf0, rf1, ra0, ra1, rtail, masks, saved_d, saved_r, xf, xa, tf, ta, acc, tables, cbuf, sems,
+    rf0, rf1, ra0, ra1, rtail, masks, saved_d, saved_r, xf, xa, tf, ta, acc, cbuf, sems,
 ):
     cz, nx = pk.shape[0], pk.shape[1]
     ne = nx + 2 * HALO
@@ -264,8 +391,10 @@
     def bring(source, target):
         copies.append(pltpu.make_async_copy(source, target, sems.at[len(copies)]))
 
-    for buffer, at in ((rf0, 0), (ra0, 16)):
-        bring(pk.at[:, :, pl.ds(at, 16)], buffer.at[:, pl.ds(HALO, nx), pl.ds(0, 16)])
+    own = pl.ds(HALO, nx)
+    bring(pk.at[:, :, pl.ds(16, 16)], ra0.at[:, own, pl.ds(0, 16)])
+    bring(tails_in, ra0.at[:, own, pl.ds(16, 8)])
+    bring(own_masks, masks.at[:, own])
     bring(pk.at[:, :, pl.ds(32, 8)], rtail.at[:, pl.ds(HALO, nx)])
     for source, first in ((hl, HALO - DEEP), (hr, HALO + nx)):
         for i in range(DEEP):
@@ -275,10 +404,15 @@
     for q in range(DEEP):
         for i, source in enumerate((hl, hr)):
             bring(source.at[cz, pl.ds(MSG * q, MSG)], cbuf.at[i, q])
-    for copy in copies:
+    halo_copies = len(copies)
+    bring(first_in, rf1.at[:, own])
+    bring(change_in, saved_d.at[0, :, own])
+    order = copies[4:halo_copies] + copies[:4] + copies[halo_copies:]
+    for copy in order:
         copy.start()
-    build_tables(scatter, deriv, tables)
-    for copy in copies:
+    xf[...] = xf_in[...]
+    xa[...] = xa_in[...]
+    for copy in copies[4:halo_copies]:
         copy.wait()
 
     places = [near_lanes(GROUP * b - HALO) for b in range(nb)]
@@ -309,53 +443,21 @@
 
     lax.fori_loop(0, cz, halo_blocks, 0, unroll=2)
 
-    def repeated(value):
-        value = jnp.where(row < 2, value, 0.0)
-        value = value + roll(value, 2, 0)
-        return value + roll(value, 4, 0)
-
-    wide_row = iota((16, LANES), 0)
-    own_code = ((wide_row % 8) // 2).astype(F32)
-
     def start_row(r, _):
         for z in range(cz):
             t = rtail[z, r]
             rf0[z, r, pl.ds(16, 8), :] = repeated(t)
             ra0[z, r, pl.ds(16, 8), :] = repeated(roll(t, 6, 0))
-            code = jnp.broadcast_to(rtail[z, r, pl.ds(4, 1), :], (16, LANES))
-            for m in range(4):
-                masks[z, r, pl.ds(16 * m, 16), :] = jnp.where(code == m, 1.0, 0.0).astype(BF16)
-            masks[z, r, pl.ds(64, 16), :] = jnp.where(code == own_code, 1.0, 0.0).astype(BF16)
+            for m, value in enumerate(masks_of(rtail[z, r, pl.ds(4, 1), :])):
+                masks[z, r, pl.ds(16 * m, 16), :] = value
         return 0
 
-    for b in range(nb):
-        start_row(ne + b, 0)
-    lax.fori_loop(0, ne // 4, lambda c, _: [start_row(4 * c + i, 0) for i in range(4)][0], 0)
-
-    def operand(values, mask):
-        v0, v1, v2 = values
-        main = jnp.concatenate([v0, v1], axis=0)
-        high = main.astype(BF16)
-        low = (main - high.astype(F32)).astype(BF16)
-        high2 = v2.astype(BF16).astype(F32)
-        end = jnp.concatenate([high2, v2 - high2], axis=0).astype(BF16)
-        pieces = [high * mask[m] for m in range(4)] + [low * mask[m] for m in range(4)]
-        return jnp.concatenate(pieces + [end * mask[4]], axis=0)
+    outer_rows = list(range(HALO)) + list(range(HALO + nx, ne))
+    for r in outer_rows + [ne + b for b in range(nb)]:
+        start_row(r, 0)
 
     def mask_of(z, r):
         return [masks[z, r, pl.ds(16 * m, 16), :] for m in range(5)]
-
-    def apply(table, values, mask):
-        rhs = jnp.concatenate([operand(values[h], mask[h]) for h in range(2)], axis=1)
-        y = jnp.dot(table, rhs, preferred_element_type=F32)
-        outs = []
-        for h in range(2):
-            part = y[:, h * LANES : (h + 1) * LANES]
-            outs.append([
-                [part[at + 8 * i : at + 8 * i + 8] + part[at + ROWS + 8 * i : at + ROWS + 8 * i + 8] for i in range(3)]
-                for at in range(0, table.shape[0], 2 * ROWS)
-            ])
-        return outs
 
     def load(ref, z, r, i):
         return ref[z, r, pl.ds(8 * i, 8), :]
@@ -399,11 +501,6 @@
         first = jnp.where(row < 2, after, jnp.where(row < 4, before, own))
         return [first, along_z(ref, z, ne + b), load(ref, z, ne + b, 2)]
 
-    def collect(x, z, e, block):
-        g = e % GROUP
-        moved = roll(block, 8 * g + HALO, 1)
-        x[z, e // GROUP] = jnp.where(lane // 8 == g, moved, x[z, e // GROUP])
-
     def write(ref, z, r, part):
         first = shifted(part[0])
         ref[z, r, pl.ds(0, 8), :] = first
@@ -411,25 +508,12 @@
         ref[z, r, pl.ds(16, 8), :] = part[2]
         return first
 
-    for x in (xf, xa):
-        x[...] = jnp.zeros_like(x)
-
-    def gather_first(e, _):
+    for e in outer_rows:
         for z in range(cz):
             collect(xa, z, e, ra0[z, e, pl.ds(0, 8), :])
-        return 0
-
-    lax.fori_loop(0, ne // 4, lambda c, _: [gather_first(4 * c + i, 0) for i in range(4)][0], 0)
+    for copy in copies[:4]:
+        copy.wait()
     flat = adjoint.reshape(adjoint.shape[0] * cz * nx, LANES)
-
-    def in_pairs(before, after):
-        pending = None
-        for z in range(0, cz, 2):
-            made = before(z)
-            if pending is not None:
-                after(*pending)
-            pending = (z, made)
-        after(*pending)
 
     for step in range(ITERS):
         fa, ta_, fb, tb = rf[step % 2], ra[step % 2], rf[(step + 1) % 2], ra[(step + 1) % 2]
@@ -460,9 +544,9 @@
                     write(tb, z + h, ne + b, made[0][h][0])
                     write(fb, z + h, ne + b, made[1][h][0])
 
-            in_pairs(before, after)
-
-        def rows(e, _):
+            in_pairs(cz, before, after)
+
+        def rows(e, outer=False):
             total = []
 
             def before(z):
@@ -479,9 +563,11 @@
                             total.append(av[h][i] * load(saved_d.at[ITERS - 1 - step], z + h, e, i))
                 if step > 0:
                     fv = [connect_row(fa, tf, z + h, e) for h in range(2)]
-                else:
+                    return a_out, apply(f_table, fv, mask)
+                if outer:
                     fv = [read(fa, z + h, e) for h in range(2)]
-                return a_out, apply(f_table, fv, mask)
+                    return a_out, apply(s_table, fv, mask)
+                return a_out, None
 
             def after(z, made):
                 a_out, f_out = made
@@ -496,7 +582,11 @@
                         change = f_out[h][0]
                     else:
                         collect(xa, z + h, e, write(tb, z + h, e, part))
+                        if f_out is None:
+                            continue
                         collect(xf, z + h, e, write(fb, z + h, e, f_out[h][0]))
+                        if step == 0:
+                            continue
                         change = f_out[h][1]
                     for i in range(3):
                         if step < 2:
@@ -508,38 +598,45 @@
                     del total[:]
                     total.append(value)
 
-            in_pairs(before, after)
+            in_pairs(cz, before, after)
             if step == 2:
                 acc[e] = total[0]
             elif step > 2:
                 acc[e] = acc[e] + total[0]
             return 0
 
-        first, end = 1 + step, ne - 1 - step
-        spare = (end - first) % CHUNK
-        for e in range(first, first + spare):
-            rows(e, 0)
-
-        def chunk(c, _):
+        begin, end = 1 + step, ne - 1 - step
+        if step == 0:
+            begin, spare = HALO, [r for r in outer_rows if begin <= r < end]
+        else:
+            spare = list(range(begin, begin + (end - begin) % CHUNK))
+            begin += len(spare)
+        for e in spare:
+            rows(e, step == 0)
+
+        def chunk(c, _, begin=begin):
             for i in range(CHUNK):
-                rows(first + spare + c * CHUNK + i, 0)
+                rows(begin + c * CHUNK + i)
             return 0
 
-        lax.fori_loop(0, (end - first) // CHUNK, chunk, 0)
+        lax.fori_loop(0, nx // CHUNK, chunk, 0)
+        if step == 0:
+            copies[halo_copies].wait()
+        if step == 2:
+            copies[halo_copies + 1].wait()
 
     for x in range(nx):
         column[pl.ds(x, 1), :] = jnp.sum(acc[HALO + x], axis=0, keepdims=True) * sens_scale
 
 
-def main_call(flags, scatter, deriv, pk, fl, fr, hl, hr):
+def main_call(flags, ports, tables, xf, xa, pk, masks, first, change, tails, fl, fr, hl, hr):
     cz, nx = pk.shape[0], pk.shape[1]
-    ports = scatter.shape[1]
     ne = nx + 2 * HALO
     nb = ne // GROUP + 1
     total = ne + nb
     return pl.pallas_call(
         main_kernel,
-        in_specs=[SMEM, VMEM, VMEM, ANY, VMEM, VMEM, ANY, ANY],
+        in_specs=[SMEM, VMEM, VMEM, VMEM, ANY, ANY, ANY, ANY, ANY, VMEM, VMEM, ANY, ANY],
         out_specs=[VMEM, VMEM],
         out_shape=[
             jax.ShapeDtypeStruct((ports, cz, nx, LANES), F32),
@@ -559,13 +656,12 @@
             pltpu.VMEM((cz, nb, SUB, LANES), F32),
             pltpu.VMEM((cz, nb, SUB, LANES), F32),
             pltpu.VMEM((ne, SUB, LANES), F32),
-            pltpu.VMEM((8 * ROWS, KDIM), F32),
             pltpu.VMEM((2, DEEP, MSG, LANES), F32),
-            pltpu.SemaphoreType.DMA((3 + 8 * DEEP,)),
+            pltpu.SemaphoreType.DMA((6 + 8 * DEEP,)),
         ],
         compiler_params=pltpu.CompilerParams(vmem_limit_bytes=63 * MIB),
         name="adjoint_steps",
-    )(flags, scatter, deriv, pk, fl, fr, hl, hr)
+    )(flags, tables, xf, xa, pk, masks, first, change, tails, fl, fr, hl, hr)
 
 
 def route_kernel(ids, ranks, id_slots):
@@ -688,11 +784,15 @@
     fl = moved(up, "gy", 1, False)
     fr = moved(down, "gy", -1, False)
     ranks, id_slots = route(param_ids, ndev, cap)
+    fl, fr, ranks, id_slots = lax.optimization_barrier((fl, fr, ranks, id_slots))
+    tables, masks, first, change, tails, xf, xa = prep(scatter_table, deriv_table, pk)
     xl, xr = corners(fl, fr, xl, xr)
     hr = moved(xl, "gx", -1, True)
     hl = moved(xr, "gx", 1, True)
     flags = jnp.stack([position == 0, position == extent - 1]).astype(jnp.int32)
-    adjoint, column = main_call(flags, scatter_table, deriv_table, pk, fl, fr, hl, hr)
+    adjoint, column = main_call(
+        flags, scatter_table.shape[1], tables, xf, xa, pk, masks, first, change, tails, fl, fr, hl, hr
+    )
     message = send(column, param_ids, ranks, id_slots)
     received = lax.all_to_all(message, ("gx", "gy"), 0, 0, tiled=True)
     sensitivity = gather(received, owned).reshape(-1)

time: 97.8 us -> 93 us (0.951)
  waiting for transfers between devices: 16.9 us -> 5.41 us
  Pallas kernels: 55.4 us -> 60.7 us
  local copies, waits for them, and re-layouts: 2.07 us -> 3.76 us
    ppermute x4, waiting for transfers between devices: 16.9 us -> 5.41 us  [moved(): return lax.ppermute(block, axis, pairs)]
    pallas_call x1 -> x2, Pallas kernels: 39.1 us -> 44.3 us  [the longest x1 32.9 us: main_call(): pl.pallas_call(main_kernel, in_specs=[SMEM, VMEM, VMEM, VMEM, ANY, ANY, A...]
    unnamed x15 -> x19, local copies, waits for them, and re-layouts: 1.98 us -> 3.67 us
  transfers between devices with their start and end apart: 4 -> 4, of which waited for: 3 -> 3; matrix products, arithmetic and copies ran while one was open for 2% -> 2% of each run, Pallas kernels for 3% -> 15%
where the time goes in v4:
time: 93 us; the launch traced here: 92.4 us
  Pallas kernels  60.7 us (65%)
  blocking collectives  12.3 us (13%)
  starting transfers between devices  8.92 us (10%)
  waiting for transfers between devices  5.41 us (6%)
  local copies, waits for them, and re-layouts  3.76 us (4%)
    pallas_call x1, Pallas kernels, main_call(): pl.pallas_call(main_kernel, in_specs=[SMEM, VMEM, VMEM, VMEM, ANY, ANY, A...  32.9 us
    all_to_all x1, blocking collectives, shards(): received = lax.all_to_all(message, ('gx', 'gy'), 0, 0, tiled=True)  12.3 us
    pallas_call x1, Pallas kernels, prep(): pl.pallas_call(prep_kernel, grid=(nx // rows,), in_specs=[table, table, b...  11.4 us
    pallas_call x1, Pallas kernels, pack(): pl.pallas_call(pack_kernel, grid=(cz,), in_specs=[field, field, codes, bo...  10.3 us
    ppermute x4, starting transfers between devices, moved(): return lax.ppermute(block, axis, pairs)  8.92 us
    ppermute x4, waiting for transfers between devices, moved(): return lax.ppermute(block, axis, pairs)  5.41 us
    unnamed x19, local copies, waits for them, and re-layouts  3.67 us
    pallas_call x1, Pallas kernels, route(): pl.pallas_call(route_kernel, in_specs=[VMEM], out_specs=[VMEM] * 2, out_s...  2.63 us
  transfers between devices with their start and end apart: 4, of which 3 were waited for; matrix products, arithmetic and copies ran while one was open for 2% of the time, Pallas kernels for 15%

profile of v4, /device:TPU:0, one launch (start us, length us, event | category | flops | bytes accessed | tf_op | source)
XLA Modules:
  0.0 92.4 jit_solution(16934593647775364554)
XLA Ops:
  0.6 0.0 copy-start.2
  0.6 0.0 copy-start.6
  0.7 0.0 copy-start.7
  0.7 10.3 %pack.1 = (f32[10,32,40,128]{3,2,1,0:T(8,128)}, f32[10,40,128]{2,1,0:T(8,128)}, f32[10,40,128]{2,1,0:T(8,128)}, f32[11,120,128]{2,1,0:T(8,128)}, f32[11,120,128]{2,1,0:T(8,128)}) custom-call(f32[18,10,32,128]{3,2,1,0:T(8,128)} %inc.1, f32[18,10,32,128]{3,2,1,0:T(8,128)} %cot.1, s32[10,16,32]{2,1,0:T(8,128)} %bitcast.11, s32[2,16,32]{2,1,0:T(8,128)} %bitcast.12), custom_call_target="tpu_custom_call" | custom-call | tf_op jit(solution)/shard_map/pack/pallas_call | solution.py:137
  11.0 4.9 %collective-permute-start = (f32[10,40,128]{2,1,0:T(8,128)}, f32[10,40,128]{2,1,0:T(8,128)S(1)}, u32[]{:S(2)}, u32[]{:S(2)}) collective-permute-start(f32[10,40,128]{2,1,0:T(8,128)} %get-tuple-element.32), channel_id=1, source_target_pairs={{0,1},{1,2},{2,3},{4,5},{5,6},{6,7},{8,9},{9,10},{10,11},{12,13},{... | collective-permute-start | bytes 614408 | tf_op jit(solution)/shard_map/ppermute | solution.py:772
  16.0 1.3 %collective-permute-start.1 = (f32[10,40,128]{2,1,0:T(8,128)}, f32[10,40,128]{2,1,0:T(8,128)S(1)}, u32[]{:S(2)}, u32[]{:S(2)}) collective-permute-start(f32[10,40,128]{2,1,0:T(8,128)} %get-tuple-element.33), channel_id=1, source_target_pairs={{1,0},{2,1},{3,2},{5,4},{6,5},{7,6},{9,8},{10,9},{11,10},{13,12},{... | collective-permute-start | bytes 614408 | tf_op jit(solution)/shard_map/ppermute | solution.py:772
  17.3 0.0 copy-done.2
  17.3 2.6 %route.1 = (s32[32,128]{1,0:T(8,128)S(1)}, f32[32,256]{1,0:T(8,128)S(1)}) custom-call(s32[32,128]{1,0:T(8,128)S(1)} %copy-done.2), custom_call_target="tpu_custom_call" | custom-call | tf_op jit(solution)/shard_map/route/pallas_call | solution.py:694
  19.9 0.7 collective-permute-done.below.fl
  20.6 0.0 copy-start
  20.6 4.0 %collective-permute-done.1.above.fr = f32[10,40,128]{2,1,0:T(8,128)S(1)} collective-permute-done((f32[10,40,128]{2,1,0:T(8,128)}, f32[10,40,128]{2,1,0:T(8,128)S(1)}, u32[]{:S(2)}, u32[]{:S(2)}) %collective-permute-start.1) | collective-permute-done | bytes 204832 | tf_op jit(solution)/shard_map/ppermute | solution.py:772
  24.6 0.0 copy-start.1
  24.6 1.0 %corners.1 = (f32[11,120,128]{2,1,0:T(8,128)}, f32[11,120,128]{2,1,0:T(8,128)}) custom-call(f32[10,40,128]{2,1,0:T(8,128)S(1)} %collective-permute-done.below.fl, f32[10,40,128]{2,1,0:T(8,128)S(1)} %collective-permute-done.1.above.fr, f32[11,120,128]{2,1,0:T(8,128)} %get-tuple-element.38.xl_in, ...), custom_call_target="tpu_custom_call", output_to_operand_aliasing={{0}: (2, {}), {1}: (3, {})} | custom-call | tf_op jit(solution)/shard_map/corners/pallas_call | solution.py:187
  25.6 0.1 collective-permute-start.2
  25.7 2.6 %collective-permute-start.3 = (f32[11,120,128]{2,1,0:T(8,128)}, f32[11,120,128]{2,1,0:T(8,128)S(1)}, u32[]{:S(2)}, u32[]{:S(2)}) collective-permute-start(f32[11,120,128]{2,1,0:T(8,128)} %get-tuple-element.41), channel_id=1, source_target_pairs={{0,28},{4,0},{8,4},{12,8},{16,12},{20,16},{24,20},{28,24},{1,29},{... | collective-permute-start | bytes 2027528 | tf_op jit(solution)/shard_map/ppermute | solution.py:772
  28.3 0.0 copy-done.6
  28.4 0.6 copy.13.scatter
  29.0 0.0 copy-done.7
  29.0 0.6 copy.14.deriv
  29.6 0.6 add_convert_fusion.flags
  30.2 11.4 %prep.1 = (f32[192,144]{1,0:T(8,128)}, bf16[10,32,80,128]{3,2,1,0:T(8,128)(2,1)}, f32[10,32,24,128]{3,2,1,0:T(8,128)}, f32[10,32,24,128]{3,2,1,0:T(8,128)}, f32[...) custom-call(f32[4,18,18]{2,1,0:T(8,128)} %copy.13.scatter, f32[4,18,18]{2,1,0:T(8,128)} %copy.14.deriv, ...), custom_call_target="tpu_custom_call" | custom-call | flops 2000000000 | bytes 24000000 | tf_op jit(solution)/shard_map/prep/pallas_call | solution.py:352
  41.6 0.0 copy-done
  41.6 0.0 copy-done.1
  41.6 0.7 collective-permute-done.2.hl
  42.4 0.0 copy-start.4
  42.4 0.8 copy-done.4
  43.2 0.0 collective-permute-done.3.hr
  43.2 0.0 copy-start.5
  43.2 0.8 copy-done.5
  44.1 32.9 %adjoint_steps.1 = (f32[18,10,32,128]{3,2,1,0:T(8,128)}, f32[32,128]{1,0:T(8,128)}) custom-call(s32[2]{0:T(128)} %add_convert_fusion.flags, f32[192,144]{1,0:T(8,128)} %get-tuple-element.25.tables, f32[10,3,8,128]{3,2,1,0:T(8,128)} %get-tuple-element.26.xf_in, f32[10,3,8,128]{3,2,1,0:T(8,128)} %get-tuple-element.27.xa_in, ...), custom_call_target="tpu_custom_call" | custom-call | tf_op jit(solution)/shard_map/adjoint_steps/pallas_call | solution.py:637
  77.0 0.0 copy-start.3
  77.0 0.7 copy-done.3
  77.7 0.8 send.1
  78.5 0.1 copy.15
  78.6 12.3 %all_to_all.11 = f32[32,1,512]{2,1,0:T(1,128)S(1)} all-to-all(f32[32,1,512]{2,1,0:T(1,128)S(1)} %copy.15), channel_id=1, replica_groups=mesh['gx'=8,'gy'=4] {'gx','gy'}, dimensions={0} | all-to-all | bytes 131072 | tf_op jit(solution)/shard_map/all_to_all | solution.py:797
  91.0 1.5 %gather.1 = f32[32,128]{1,0:T(8,128)} custom-call(f32[32,512]{1,0:T(8,128)S(1)} %bitcast.9), custom_call_target="tpu_custom_call" | custom-call | tf_op jit(solution)/shard_map/gather/pallas_call | solution.py:759
  (1 shorter events, 0.0 us)
Async XLA Ops:
  0.6 16.6 %copy-start.2 = (s32[32,128]{1,0:T(8,128)S(1)}, s32[32,128]{1,0:T(8,128)}, u32[]{:S(2)}) copy-start(s32[32,128]{1,0:T(8,128)} %ids.3) | copy-start | bytes 49156
  0.6 27.7 %copy-start.6 = (f32[4,18,18]{2,0,1:T(4,128)S(1)}, f32[4,18,18]{2,0,1:T(4,128)}, u32[]{:S(2)}) copy-start(f32[4,18,18]{2,0,1:T(4,128)} %param.9) | copy-start | bytes 15556
  0.7 28.3 %copy-start.7 = (f32[4,18,18]{2,0,1:T(4,128)S(1)}, f32[4,18,18]{2,0,1:T(4,128)}, u32[]{:S(2)}) copy-start(f32[4,18,18]{2,0,1:T(4,128)} %param.10) | copy-start | bytes 15556
  11.0 9.6 %collective-permute-start = (f32[10,40,128]{2,1,0:T(8,128)}, f32[10,40,128]{2,1,0:T(8,128)S(1)}, u32[]{:S(2)}, u32[]{:S(2)}) collective-permute-start(f32[10,40,128]{2,1,0:T(8,128)} %get-tuple-element.32), channel_id=1, source_target_pairs={{0,1},{1,2},{2,3},{4,5},{5,6},{6,7},{8,9},{9,10},{10,11},{12,13},{... | collective-permute-start | bytes 614408 | tf_op jit(solution)/shard_map/ppermute | solution.py:772
  16.0 8.6 %collective-permute-start.1 = (f32[10,40,128]{2,1,0:T(8,128)}, f32[10,40,128]{2,1,0:T(8,128)S(1)}, u32[]{:S(2)}, u32[]{:S(2)}) collective-permute-start(f32[10,40,128]{2,1,0:T(8,128)} %get-tuple-element.33), channel_id=1, source_target_pairs={{1,0},{2,1},{3,2},{5,4},{6,5},{7,6},{9,8},{10,9},{11,10},{13,12},{... | collective-permute-start | bytes 614408 | tf_op jit(solution)/shard_map/ppermute | solution.py:772
  20.6 21.0 %copy-start = (f32[10,40,128]{2,1,0:T(8,128)}, f32[10,40,128]{2,1,0:T(8,128)S(1)}, u32[]{:S(2)}) copy-start(f32[10,40,128]{2,1,0:T(8,128)S(1)} %collective-permute-done.below.fl) | copy-start | bytes 614404
  24.6 17.0 %copy-start.1 = (f32[10,40,128]{2,1,0:T(8,128)}, f32[10,40,128]{2,1,0:T(8,128)S(1)}, u32[]{:S(2)}) copy-start(f32[10,40,128]{2,1,0:T(8,128)S(1)} %collective-permute-done.1.above.fr) | copy-start | bytes 614404
  25.6 16.7 %collective-permute-start.2 = (f32[11,120,128]{2,1,0:T(8,128)}, f32[11,120,128]{2,1,0:T(8,128)S(1)}, u32[]{:S(2)}, u32[]{:S(2)}) collective-permute-start(f32[11,120,128]{2,1,0:T(8,128)} %get-tuple-element.40), channel_id=1, source_target_pairs={{0,4},{4,8},{8,12},{12,16},{16,20},{20,24},{24,28},{28,0},{1,5},{5... | collective-permute-start | bytes 2027528 | tf_op jit(solution)/shard_map/ppermute | solution.py:772
  25.7 17.5 %collective-permute-start.3 = (f32[11,120,128]{2,1,0:T(8,128)}, f32[11,120,128]{2,1,0:T(8,128)S(1)}, u32[]{:S(2)}, u32[]{:S(2)}) collective-permute-start(f32[11,120,128]{2,1,0:T(8,128)} %get-tuple-element.41), channel_id=1, source_target_pairs={{0,28},{4,0},{8,4},{12,8},{16,12},{20,16},{24,20},{28,24},{1,29},{... | collective-permute-start | bytes 2027528 | tf_op jit(solution)/shard_map/ppermute | solution.py:772
  42.4 0.9 copy-start.4
  43.2 0.8 copy-start.5
  77.0 0.7 copy-start.3
